TPU v7x, 32 devices: a whole 2x2x4 slice. The times are simulated.
32 devices in a mesh: section: 2 (over y), fsdp: 16 (over z, x, core).
Axes of the slice: x: 2, y: 2, z: 4, core: 2. Of those that a mesh axis runs over, the one named last changes fastest.
Arguments:
- token_ids: int32 [2, 8192], P('section', 'fsdp'), may hold values from 0 to 49151
- scored: int32 [2, 32, 32], P('section', 'fsdp'), may hold values from 0 to 127
- targets: int32 [2, 32, 32], P('section'), may hold values from 0 to 49151
- pairs: int32 [64], replicated, may hold values from 0 to 63, each once
- table: float32 [49152, 960], P('fsdp')
- w_qkv: float32 [2, 960, 1600], P('section', 'fsdp'), may hold values from -0.1875 to 0.1875
- w_out: float32 [2, 960, 960], P('section', 'fsdp'), may hold values from -0.75 to 0.75
- w_gu: float32 [2, 960, 5120], P('section', 'fsdp'), may hold values from -0.1875 to 0.1875
- w_down: float32 [2, 2560, 960], P('section', 'fsdp'), may hold values from -0.125 to 0.125
- gains: float32 [2, 2, 960], P('section', None, 'fsdp'), may hold values from 0.5 to 1.5
- final_gain: float32 [960], P('fsdp'), may hold values from 0.5 to 1.5
- first_table: float32 [49152, 960], P('fsdp'), may hold values from -3.8146973e-05 to 3.8146973e-05
- first_qkv: float32 [2, 960, 1600], P('section', 'fsdp'), may hold values from -7.6293945e-05 to 7.6293945e-05
- first_out: float32 [2, 960, 960], P('section', 'fsdp'), may hold values from -7.6293945e-05 to 7.6293945e-05
- first_gu: float32 [2, 960, 5120], P('section', 'fsdp'), may hold values from -7.6293945e-05 to 7.6293945e-05
- first_down: float32 [2, 2560, 960], P('section', 'fsdp'), may hold values from -7.6293945e-05 to 7.6293945e-05
- first_gains: float32 [2, 2, 960], P('section', None, 'fsdp'), may hold values from -0.0008544922 to 0.0008544922
- first_final: float32 [960], P('fsdp'), may hold values from -0.0008544922 to 0.0008544922
- second_table: float32 [49152, 960], P('fsdp'), may hold values from 3.739631e-11 to 1.5108108e-10
- second_qkv: float32 [2, 960, 1600], P('section', 'fsdp'), may hold values from 1.5108108e-10 to 6.043243e-10
- second_out: float32 [2, 960, 960], P('section', 'fsdp'), may hold values from 1.5108108e-10 to 6.043243e-10
- second_gu: float32 [2, 960, 5120], P('section', 'fsdp'), may hold values from 1.5108108e-10 to 6.043243e-10
- second_down: float32 [2, 2560, 960], P('section', 'fsdp'), may hold values from 1.5108108e-10 to 6.043243e-10
- second_gains: float32 [2, 2, 960], P('section', None, 'fsdp'), may hold values from 1.5108109e-08 to 6.0432434e-08
- second_final: float32 [960], P('fsdp'), may hold values from 1.5108109e-08 to 6.0432434e-08
Outputs:
- loss: float32 [], replicated
- grad_norm: float32 [], replicated
- matrix_norms: float32 [2, 14], replicated
- new_table: float32 [49152, 960], P('fsdp')
- new_first_table: float32 [49152, 960], P('fsdp')
- new_second_table: float32 [49152, 960], P('fsdp')
- new_qkv: float32 [2, 960, 1600], P('section', 'fsdp')
- new_first_qkv: float32 [2, 960, 1600], P('section', 'fsdp')
- new_second_qkv: float32 [2, 960, 1600], P('section', 'fsdp')
- new_out: float32 [2, 960, 960], P('section', 'fsdp')
- new_first_out: float32 [2, 960, 960], P('section', 'fsdp')
- new_second_out: float32 [2, 960, 960], P('section', 'fsdp')
- new_gu: float32 [2, 960, 5120], P('section', 'fsdp')
- new_first_gu: float32 [2, 960, 5120], P('section', 'fsdp')
- new_second_gu: float32 [2, 960, 5120], P('section', 'fsdp')
- new_down: float32 [2, 2560, 960], P('section', 'fsdp')
- new_first_down: float32 [2, 2560, 960], P('section', 'fsdp')
- new_second_down: float32 [2, 2560, 960], P('section', 'fsdp')
- new_gains: float32 [2, 2, 960], P('section', None, 'fsdp')
- new_first_gains: float32 [2, 2, 960], P('section', None, 'fsdp')
- new_second_gains: float32 [2, 2, 960], P('section', None, 'fsdp')
- new_final: float32 [960], P('fsdp')
- new_first_final: float32 [960], P('fsdp')
- new_second_final: float32 [960], P('fsdp')
- table_half: bfloat16 [49152, 960], P('fsdp')
- qkv_half: bfloat16 [2, 960, 1600], P('section', 'fsdp')
- out_half: bfloat16 [2, 960, 960], P('section', 'fsdp')
- gu_half: bfloat16 [2, 960, 5120], P('section', 'fsdp')
- down_half: bfloat16 [2, 2560, 960], P('section', 'fsdp')
Inputs may be any that keep to these rules, and one draw needn't show every extreme that they name: `pairs`: each continuation appears once.
All inputs are finite; a program needn't handle non-finite values.
Results may differ from a plain program's by a relative error of at most 0.022.
Values may be sent and summed in bfloat16 or wider, within the bound.
A program may use at most 896 MiB of HBM per device.

v0:
```python
import jax
import jax.numpy as jnp
from jax import lax
from jax.sharding import PartitionSpec as P

HEADS = 15
KV = 5
HD = 64
FF = 2560
PROMPT = 256
NCONT = 2
CONT = 128
SCORED = 32
STEP = 10
TOK_MB = 512


EPS = 1e-05
SCALE = 0.125
THETA = 100000.0
BETA = 0.1
CLIP = 1.0
RATE = 0.3
BETA_ONE = 0.9
BETA_TWO = 0.99
ADAM_EPS = 1e-08
DECAY = 0.01


def swapped(array, axis, stride):
    return lax.ppermute(array, axis, [(i, i ^ 1 << stride) for i in range(lax.axis_size(axis))])


def joined(array, axis, combine):
    everything = jax.tree.map(lambda part: lax.all_gather(part, axis), array)
    initial = jax.tree.map(lambda part: part[0], everything)

    def turn(k, so_far):
        return combine(so_far, jax.tree.map(lambda part: part[k], everything))

    return lax.fori_loop(1, lax.axis_size(axis), turn, initial)


def dense(left, right):
    return jnp.dot(left, right, preferred_element_type=jnp.float32)


def dense_t(left, right):
    return lax.dot_general(
        left, right, (((0,), (0,)), ((), ())), preferred_element_type=jnp.float32
    )


def dense_nt(left, right):
    return lax.dot_general(
        left, right, (((1,), (1,)), ((), ())), preferred_element_type=jnp.float32
    )


def row_scale(x):
    return lax.rsqrt(jnp.mean(x * x, axis=-1, keepdims=True) + EPS)


def norm_back(x, scale, gain, upstream):
    inner = upstream * gain
    grad_gain = jnp.sum(upstream * x * scale, axis=0)
    grad_x = scale * inner - x * scale**3 * jnp.mean(inner * x, axis=-1, keepdims=True)
    return (grad_x, grad_gain)


def rotate(x, cosine, sine):
    half = x.shape[-1] // 2
    first, second = (x[..., :half], x[..., half:])
    return jnp.concatenate(
        [first * cosine - second * sine, second * cosine + first * sine], axis=-1
    )


def rotate_back(grad, cosine, sine):
    half = grad.shape[-1] // 2
    first, second = (grad[..., :half], grad[..., half:])
    return jnp.concatenate(
        [first * cosine + second * sine, second * cosine - first * sine], axis=-1
    )


def layer_tables():
    place = jnp.arange(TOK_MB)
    segment = jnp.where(place >= PROMPT, 1 + (place - PROMPT) // CONT, 0)
    rotary = jnp.where(place >= PROMPT, PROMPT + (place - PROMPT) % CONT, place).astype(jnp.float32)
    freq = THETA ** (-2.0 * jnp.arange(HD // 2).astype(jnp.float32) / HD)
    angle = rotary[:, None] * freq[None, :]
    allowed = (place[None, :] <= place[:, None]) & (
        (segment[None, :] == 0) | (segment[None, :] == segment[:, None])
    )
    return (jnp.cos(angle)[:, None, :], jnp.sin(angle)[:, None, :], allowed)


def layer_forward(x, weights, tables):
    w_qkv, w_out, w_gu, w_down, gains = weights
    cosine, sine, allowed = tables
    width = HEADS * HD
    kv_width = KV * HD
    first_scale = row_scale(x)
    normed_in = (x * first_scale * gains[0]).astype(jnp.bfloat16)
    qkv = dense(normed_in, w_qkv)
    query = (
        rotate(qkv[:, :width].reshape(-1, HEADS, HD), cosine, sine)
        .astype(jnp.bfloat16)
        .reshape(-1, KV, HEADS // KV, HD)
    )
    key = rotate(qkv[:, width : width + kv_width].reshape(-1, KV, HD), cosine, sine).astype(
        jnp.bfloat16
    )
    value = qkv[:, width + kv_width :].reshape(-1, KV, HD).astype(jnp.bfloat16)
    scores = jnp.einsum("qhgd,khd->hgqk", query, key, preferred_element_type=jnp.float32) * SCALE
    scores = jnp.where(allowed, scores, -1e30)
    expo = jnp.exp(scores - jnp.max(scores, axis=-1, keepdims=True))
    probs = expo / jnp.sum(expo, axis=-1, keepdims=True)
    probs_low = probs.astype(jnp.bfloat16)
    attended = jnp.einsum("hgqk,khd->qhgd", probs_low, value, preferred_element_type=jnp.float32)
    attended = attended.reshape(-1, width).astype(jnp.bfloat16)
    mixed = x + dense(attended, w_out)
    second_scale = row_scale(mixed)
    normed_mid = (mixed * second_scale * gains[1]).astype(jnp.bfloat16)
    gate_up = dense(normed_mid, w_gu)
    gate, upper = (gate_up[:, :FF], gate_up[:, FF:])
    hidden = (jax.nn.silu(gate) * upper).astype(jnp.bfloat16)
    output = mixed + dense(hidden, w_down)
    kept = (
        first_scale,
        normed_in,
        query,
        key,
        value,
        probs,
        probs_low,
        attended,
        mixed,
        second_scale,
        normed_mid,
        gate,
        upper,
        hidden,
    )
    return (output, kept)


def layer_backward(x, upstream, weights, tables):
    w_qkv, w_out, w_gu, w_down, gains = weights
    cosine, sine, allowed = tables
    width = HEADS * HD
    kv_width = KV * HD
    unused, kept = layer_forward(x, weights, tables)
    (
        first_scale,
        normed_in,
        query,
        key,
        value,
        probs,
        probs_low,
        attended,
        mixed,
        second_scale,
        normed_mid,
        gate,
        upper,
        hidden,
    ) = kept
    branch = upstream.astype(jnp.bfloat16)
    grad_down = dense_t(hidden, branch)
    grad_hidden = dense_nt(branch, w_down)
    sig = jax.nn.sigmoid(gate)
    grad_gate = grad_hidden * upper * sig * (1.0 + gate * (1.0 - sig))
    grad_upper = grad_hidden * gate * sig
    grad_gate_up = jnp.concatenate([grad_gate, grad_upper], axis=1).astype(jnp.bfloat16)
    grad_gu = dense_t(normed_mid, grad_gate_up)
    grad_mid, gain_two = norm_back(mixed, second_scale, gains[1], dense_nt(grad_gate_up, w_gu))
    grad_mixed = grad_mid + upstream
    branch_attn = grad_mixed.astype(jnp.bfloat16)
    grad_out = dense_t(attended, branch_attn)
    grad_att = dense_nt(branch_attn, w_out).astype(jnp.bfloat16).reshape(-1, KV, HEADS // KV, HD)
    grad_probs = jnp.einsum("qhgd,khd->hgqk", grad_att, value, preferred_element_type=jnp.float32)
    grad_scores = probs * (grad_probs - jnp.sum(grad_probs * probs, axis=-1, keepdims=True))
    grad_scores = grad_scores.astype(jnp.bfloat16)
    grad_query = (
        jnp.einsum("hgqk,khd->qhgd", grad_scores, key, preferred_element_type=jnp.float32) * SCALE
    )
    grad_key = (
        jnp.einsum("hgqk,qhgd->khd", grad_scores, query, preferred_element_type=jnp.float32) * SCALE
    )
    grad_value = jnp.einsum(
        "hgqk,qhgd->khd", probs_low, grad_att, preferred_element_type=jnp.float32
    )
    grad_qkv = jnp.concatenate(
        [
            rotate_back(grad_query.reshape(-1, HEADS, HD), cosine, sine).reshape(-1, width),
            rotate_back(grad_key, cosine, sine).reshape(-1, kv_width),
            grad_value.reshape(-1, kv_width),
        ],
        axis=1,
    ).astype(jnp.bfloat16)
    grad_qkv_w = dense_t(normed_in, grad_qkv)
    grad_in, gain_one = norm_back(x, first_scale, gains[0], dense_nt(grad_qkv, w_qkv))
    return (
        grad_in + grad_mixed,
        (grad_qkv_w, grad_out, grad_gu, grad_down, jnp.stack([gain_one, gain_two])),
    )


def zero_grads(x, weights):
    return (jnp.zeros_like(x), tuple((jnp.zeros(w.shape, jnp.float32) for w in weights)))


def combine_stats(left, right):
    top = jnp.maximum(left[0], right[0])
    total = left[1] * jnp.exp(left[0] - top) + right[1] * jnp.exp(right[0] - top)
    return (top, total, left[2] + right[2])


def lamb_parts(weight, grad, first, second, decay):
    first_new = BETA_ONE * first + (1.0 - BETA_ONE) * grad
    second_new = BETA_TWO * second + (1.0 - BETA_TWO) * grad * grad
    update = (
        first_new
        / (1.0 - BETA_ONE**STEP)
        / (jnp.sqrt(second_new / (1.0 - BETA_TWO**STEP)) + ADAM_EPS)
        + decay * weight
    )
    return (first_new, second_new, update)


def shards(
    token_ids,
    scored,
    targets,
    pairs,
    table,
    w_qkv,
    w_out,
    w_gu,
    w_down,
    gains,
    final_gain,
    first_table,
    first_qkv,
    first_out,
    first_gu,
    first_down,
    first_gains,
    first_final,
    second_table,
    second_qkv,
    second_out,
    second_gu,
    second_down,
    second_gains,
    second_final,
):
    section_index = lax.axis_index("section")
    leader = section_index == 0
    vshard = table.shape[0]
    vstart = lax.axis_index("fsdp") * vshard
    ids = token_ids[0]
    tables_here = layer_tables()
    table_low = table.astype(jnp.bfloat16)
    qkv_low = w_qkv[0].astype(jnp.bfloat16)
    out_low = w_out[0].astype(jnp.bfloat16)
    gu_low = w_gu[0].astype(jnp.bfloat16)
    down_low = w_down[0].astype(jnp.bfloat16)
    gains_low = gains[0].astype(jnp.bfloat16)
    final_low_shard = final_gain.astype(jnp.bfloat16)
    gathered = (
        lax.all_gather(qkv_low, "fsdp", axis=0, tiled=True),
        lax.all_gather(out_low, "fsdp", axis=0, tiled=True),
        lax.all_gather(gu_low, "fsdp", axis=0, tiled=True),
        lax.all_gather(down_low, "fsdp", axis=0, tiled=True),
        lax.all_gather(gains_low, "fsdp", axis=1, tiled=True),
        lax.all_gather(final_low_shard, "fsdp", axis=0, tiled=True),
    )
    fwd_weights = gathered[:5]
    final_low = gathered[5]
    piece = lax.all_gather(table_low, "fsdp", axis=0, tiled=True)
    local = ids
    inside = (local >= 0) & (local < piece.shape[0])
    rows = jnp.take(piece, jnp.clip(local, 0, piece.shape[0] - 1), axis=0)
    embedded = jnp.where(inside[:, None], rows.astype(jnp.float32), 0.0)
    saved = []
    incoming = embedded
    outputs = embedded
    for tick in range(3):
        inputs = embedded if tick == 0 else incoming
        saved.append(inputs)
        if tick == 1:
            outputs = layer_forward(inputs, fwd_weights, tables_here)[0]
        else:
            outputs = lax.cond(
                leader if tick == 0 else jnp.logical_not(leader),
                lambda v: layer_forward(v, fwd_weights, tables_here)[0],
                jnp.zeros_like,
                inputs,
            )
        if tick < 2:
            payload = jnp.where(leader, outputs, embedded) if tick == 0 else outputs
            incoming = swapped(payload, "section", 0)
    final_in = jnp.where(leader, saved[2], outputs)
    final_scale = row_scale(final_in)
    place = (PROMPT + CONT * jnp.arange(NCONT)[:, None] + scored[0]).reshape(-1)
    picked = jnp.take(final_in, place, axis=0)
    picked_scale = jnp.take(final_scale, place, axis=0)
    head_in = (picked * picked_scale * final_low).astype(jnp.bfloat16)
    rows_all = lax.all_gather(head_in, "fsdp", axis=0, tiled=True)
    logits = dense_nt(rows_all, table_low)
    wanted = targets[0].reshape(-1) - vstart
    hit = jnp.arange(vshard)[None, :] == wanted[:, None]
    top = jnp.max(logits, axis=1)
    total = jnp.sum(jnp.exp(logits - top[:, None]), axis=1)
    target_logit = jnp.sum(jnp.where(hit, logits, 0.0), axis=1)
    top, total, target_logit = joined((top, total, target_logit), "fsdp", combine_stats)
    row_logp = target_logit - top - jnp.log(total)
    seq_logp = jnp.sum(row_logp.reshape(-1, SCORED), axis=1)
    every = lax.all_gather(seq_logp, "section", axis=0, tiled=True)
    pair = pairs.reshape(-1, 2)
    delta = every[pair[:, 0]] - every[pair[:, 1]]
    loss = jnp.sum(jax.nn.softplus(-BETA * delta))
    push = BETA * jax.nn.sigmoid(-BETA * delta)
    grad_every = jnp.zeros_like(every).at[pair[:, 0]].add(-push).at[pair[:, 1]].add(push)
    grad_seq = lax.dynamic_slice_in_dim(
        grad_every, section_index * seq_logp.shape[0], seq_logp.shape[0]
    )
    grad_row = jnp.repeat(grad_seq, SCORED)
    prob = jnp.exp(logits - top[:, None]) / total[:, None]
    grad_logits = (grad_row[:, None] * (hit.astype(jnp.float32) - prob)).astype(jnp.bfloat16)
    grad_table = dense_t(grad_logits, rows_all)
    grad_head = lax.psum_scatter(
        dense(grad_logits, table_low), "fsdp", scatter_dimension=0, tiled=True
    )
    grad_picked, grad_final_gain = norm_back(picked, picked_scale, final_low, grad_head)
    grad_final_in = jnp.zeros_like(final_in).at[place].add(grad_picked)
    back_weights = (
        lax.all_gather(qkv_low, "fsdp", axis=0, tiled=True),
        lax.all_gather(out_low, "fsdp", axis=0, tiled=True),
        lax.all_gather(gu_low, "fsdp", axis=0, tiled=True),
        lax.all_gather(down_low, "fsdp", axis=0, tiled=True),
        lax.all_gather(gains_low, "fsdp", axis=1, tiled=True),
    )
    grad_sums = None
    incoming = grad_final_in
    grad_in = grad_final_in
    for tick in range(3):
        inputs = saved[2 - tick]
        upstream = grad_final_in if tick == 0 else incoming
        if tick == 1:
            grad_in, grads = layer_backward(inputs, upstream, back_weights, tables_here)
        else:
            grad_in, grads = lax.cond(
                jnp.logical_not(leader) if tick == 0 else leader,
                lambda pack: layer_backward(pack[0], pack[1], back_weights, tables_here),
                lambda pack: zero_grads(pack[0], back_weights),
                (inputs, upstream),
            )
        grad_sums = (
            grads
            if grad_sums is None
            else tuple((left + right for left, right in zip(grad_sums, grads)))
        )
        if tick < 2:
            payload = jnp.where(leader, grad_final_in, grad_in) if tick == 0 else grad_in
            incoming = swapped(payload, "section", 0)
    grad_embedded = jnp.where(leader, grad_in, incoming)
    count = lax.axis_size("fsdp") * vshard
    local = ids
    slot = jnp.where((local >= 0) & (local < count), local, count)
    grad_lookup = lax.psum_scatter(
        jax.ops.segment_sum(grad_embedded, slot, num_segments=count + 1)[:count],
        "fsdp",
        scatter_dimension=0,
        tiled=True,
    )
    g_qkv, g_out, g_gu, g_down, g_gains = grad_sums
    shard_grads = (
        lax.psum_scatter(g_qkv, "fsdp", scatter_dimension=0, tiled=True),
        lax.psum_scatter(g_out, "fsdp", scatter_dimension=0, tiled=True),
        lax.psum_scatter(g_gu, "fsdp", scatter_dimension=0, tiled=True),
        lax.psum_scatter(g_down, "fsdp", scatter_dimension=0, tiled=True),
        lax.psum_scatter(g_gains, "fsdp", scatter_dimension=1, tiled=True),
        lax.psum_scatter(grad_final_gain, "fsdp", scatter_dimension=0, tiled=True),
    )
    table_grad, final_grad = (
        lax.psum((grad_table + grad_lookup).astype(jnp.bfloat16), "section").astype(jnp.float32),
        lax.psum(shard_grads[5].astype(jnp.bfloat16), "section").astype(jnp.float32),
    )
    grads_all = (
        table_grad,
        shard_grads[0][None],
        shard_grads[1][None],
        shard_grads[2][None],
        shard_grads[3][None],
        shard_grads[4][None],
        final_grad,
    )
    weights_all = (table, w_qkv, w_out, w_gu, w_down, gains, final_gain)
    firsts = (first_table, first_qkv, first_out, first_gu, first_down, first_gains, first_final)
    seconds = (
        second_table,
        second_qkv,
        second_out,
        second_gu,
        second_down,
        second_gains,
        second_final,
    )
    slot_total = 6 * lax.axis_size("section") + 2
    shared_share = jnp.where(leader, 1.0, 0.0)

    def slot_squares(arrays):
        rows_each_section = jnp.stack(
            [
                jnp.sum(arrays[1] ** 2),
                jnp.sum(arrays[2] ** 2),
                jnp.sum(arrays[3] ** 2),
                jnp.sum(arrays[4] ** 2),
                jnp.sum(arrays[5][0, 0] ** 2),
                jnp.sum(arrays[5][0, 1] ** 2),
            ]
        )
        slot_entries = 6 * section_index + jnp.arange(6)
        positioned_rows = jnp.sum(
            jnp.where(
                slot_entries[:, None] == jnp.arange(slot_total)[None, :],
                rows_each_section[:, None],
                0.0,
            ),
            axis=0,
        )
        common_prompt = shared_share * jnp.stack([jnp.sum(arrays[0] ** 2), jnp.sum(arrays[6] ** 2)])
        return positioned_rows + jnp.concatenate(
            [jnp.zeros((slot_total - 2,), jnp.float32), common_prompt]
        )

    grad_sq, weight_sq = lax.psum(
        (slot_squares(grads_all), slot_squares(weights_all)), ("section", "fsdp")
    )
    grad_norm = jnp.sqrt(jnp.sum(grad_sq))
    clip = jnp.minimum(1.0, CLIP / grad_norm)
    decays = (DECAY, DECAY, DECAY, DECAY, DECAY, 0.0, 0.0)
    parts = [
        lamb_parts(w, clip * g, m, v, d)
        for w, g, m, v, d in zip(weights_all, grads_all, firsts, seconds, decays)
    ]
    update_sq = lax.psum(slot_squares(tuple((p[2] for p in parts))), ("section", "fsdp"))
    weight_norms = jnp.sqrt(weight_sq)
    update_norms = jnp.sqrt(update_sq)
    trust_ratio = weight_norms / update_norms
    own = lax.dynamic_slice_in_dim(trust_ratio, 6 * section_index, 6)
    scales = (
        trust_ratio[slot_total - 2],
        own[0],
        own[1],
        own[2],
        own[3],
        own[4:6][None, :, None],
        trust_ratio[slot_total - 1],
    )
    new = [w - RATE * s * p[2] for w, s, p in zip(weights_all, scales, parts)]
    matrix_norms = jnp.stack([weight_norms, update_norms])
    return (
        loss,
        grad_norm,
        matrix_norms,
        new[0],
        parts[0][0],
        parts[0][1],
        new[1],
        parts[1][0],
        parts[1][1],
        new[2],
        parts[2][0],
        parts[2][1],
        new[3],
        parts[3][0],
        parts[3][1],
        new[4],
        parts[4][0],
        parts[4][1],
        new[5],
        parts[5][0],
        parts[5][1],
        new[6],
        parts[6][0],
        parts[6][1],
        new[0].astype(jnp.bfloat16),
        new[1].astype(jnp.bfloat16),
        new[2].astype(jnp.bfloat16),
        new[3].astype(jnp.bfloat16),
        new[4].astype(jnp.bfloat16),
    )


def solution(mesh):
    placed = (
        P("section", "fsdp"),
        P("section", "fsdp", None),
        P("section", None, None),
        P(),
        P("fsdp", None),
        P("section", "fsdp", None),
        P("section", "fsdp", None),
        P("section", "fsdp", None),
        P("section", "fsdp", None),
        P("section", None, "fsdp"),
        P("fsdp"),
        P("fsdp", None),
        P("section", "fsdp", None),
        P("section", "fsdp", None),
        P("section", "fsdp", None),
        P("section", "fsdp", None),
        P("section", None, "fsdp"),
        P("fsdp"),
        P("fsdp", None),
        P("section", "fsdp", None),
        P("section", "fsdp", None),
        P("section", "fsdp", None),
        P("section", "fsdp", None),
        P("section", None, "fsdp"),
        P("fsdp"),
    )
    return jax.shard_map(
        shards,
        mesh=mesh,
        in_specs=placed,
        out_specs=(
            P(),
            P(),
            P(),
            P("fsdp", None),
            P("fsdp", None),
            P("fsdp", None),
            P("section", "fsdp", None),
            P("section", "fsdp", None),
            P("section", "fsdp", None),
            P("section", "fsdp", None),
            P("section", "fsdp", None),
            P("section", "fsdp", None),
            P("section", "fsdp", None),
            P("section", "fsdp", None),
            P("section", "fsdp", None),
            P("section", "fsdp", None),
            P("section", "fsdp", None),
            P("section", "fsdp", None),
            P("section", None, "fsdp"),
            P("section", None, "fsdp"),
            P("section", None, "fsdp"),
            P("fsdp"),
            P("fsdp"),
            P("fsdp"),
            P("fsdp", None),
            P("section", "fsdp", None),
            P("section", "fsdp", None),
            P("section", "fsdp", None),
            P("section", "fsdp", None),
        ),
        check_vma=False,
    )
```

profile of v0, /device:TPU:0, one launch (start us, length us, event | category | flops | bytes accessed | tf_op | source)
XLA Modules:
  0.0 4425.8 jit_solution(6535603779867955325)
XLA Ops:
  19.3 9.9 copy.301
  31.3 25.3 all-gather
  69.0 60.0 %all-gather.19.cloned.1.call-done = bf16[1,960,1600]{2,0,1:T(2,128)(2,1)} async-done(((bf16[1,60,1600]{2,0,1:T(2,128)(2,1)}), bf16[1,960,1600]{2,0,1:T(2,128)(2,1)}) %all-gather.19.cloned.1.call-update) | async-done | bytes 3072016 | tf_op jit(solution)/shard_map/all_gather | solution.py:275
  134.0 98.5 %all-gather.23.cloned.1.call-done = bf16[1,960,5120]{2,0,1:T(2,128)(2,1)} async-done(((bf16[1,60,5120]{2,0,1:T(2,128)(2,1)}), bf16[1,960,5120]{2,0,1:T(2,128)(2,1)}) %all-gather.23.cloned.1.call-update) | async-done | bytes 9830416 | tf_op jit(solution)/shard_map/all_gather | solution.py:277
  232.5 15.7 copy.464
  248.2 470.5 %all-gather.15.cloned.1.call-done = bf16[49152,960]{1,0:T(8,128)(2,1)} async-done(((bf16[3072,960]{1,0:T(8,128)(2,1)}), bf16[49152,960]{1,0:T(8,128)(2,1)}) %all-gather.15.cloned.1.call-update) | async-done | bytes 94371856 | tf_op jit(solution)/shard_map/all_gather | solution.py:284
  727.7 49.7 %all-gather.25.cloned.1.call-done = bf16[1,2560,960]{2,1,0:T(8,128)(2,1)} async-done(((bf16[1,160,960]{2,1,0:T(8,128)(2,1)}), bf16[1,2560,960]{2,1,0:T(8,128)(2,1)}) %all-gather.25.cloned.1.call-update) | async-done | bytes 4915216 | tf_op jit(solution)/shard_map/all_gather | solution.py:278
  777.4 44.8 %conditional.4 = (f32[512,960]{0,1:T(8,128)}) conditional(s32[]{:T(128)} %convert_element_type.571, () %tuple.58, (f32[512,960]{0,1:T(8,128)}, bf16[2,960]{1,0:T(2,128)(2,1)S(1)}, bf16[960,1600]{1,0:T(8,128)(2,1)}, pred[512,512]{0,1:T(8,128)(4,1)S(1)}, f32[512,1,32]{0,2,1:T(8,128)S(1)}, /*index=5*/f32[512,1,32]{0,2,1:T(8,128)S(1)}, ...), branch_computations={%region_0.1_spmd, %region_1.6_spmd} | conditional | flops 11116056576 | bytes 140311392 | solution.py:298
  786.4 12.1 fusion.285
  830.6 38.7 collective-permute-done
  873.9 9.6 fusion.292
  913.2 30.5 all-reduce.3
  943.8 11.1 collective-permute-done.1
  972.8 71.7 %all-gather.17.cloned.1.call-done = bf16[1024,960]{1,0:T(8,128)(2,1)} async-done(((bf16[64,960]{1,0:T(8,128)(2,1)}), bf16[1024,960]{1,0:T(8,128)(2,1)}) %all-gather.17.cloned.1.call-update) | async-done | bytes 1966096 | tf_op jit(solution)/shard_map/all_gather | solution.py:313
  1044.5 12.3 fusion.293
  1056.8 19.3 all-gather.5
  1083.3 17.6 all-gather.6
  1100.9 18.9 all-gather.7
  1141.5 10.0 fusion.294
  1151.7 69.6 %reduce-scatter.11.cloned.1.call-done = f32[64,960]{1,0:T(8,128)} async-done(((f32[1024,960]{1,0:T(8,128)}), f32[64,960]{1,0:T(8,128)}) %reduce-scatter.11.cloned.1.call-update) | async-done | bytes 245776 | tf_op jit(solution)/shard_map/reduce_scatter | solution.py:336
  1229.0 23.2 conditional.6
  1230.1 9.1 broadcast.815
  1258.3 100.0 %collective-permute-start.2 = (f32[512,960]{0,1:T(8,128)S(1)}, f32[512,960]{0,1:T(8,128)S(1)}, u32[]{:S(2)}, u32[]{:S(2)}) collective-permute-start(f32[512,960]{0,1:T(8,128)S(1)} %broadcast_select_fusion.1), channel_id=1, source_target_pairs={{0,16},{16,0},{1,17},{17,1},{2,18},{18,2},{3,19},{19,3},{4,20},{20... | collective-permute-start | bytes 5898248 | tf_op jit(solution)/shard_map/ppermute | solution.py:31
  1358.2 41.1 collective-permute-done.2
  1399.3 11.2 multiply_convert_fusion.30
  1410.6 9.4 multiply_reduce_fusion.18
  1454.3 40.6 collective-permute-done.3
  1494.9 118.2 %conditional.7 = (f32[512,960]{0,1:T(8,128)}, f32[960,1600]{1,0:T(8,128)}, f32[960,960]{1,0:T(8,128)}, f32[960,5120]{1,0:T(8,128)}, f32[2,960]{1,0:T(2,128)}, /*index=5*/f32[2560,960]{1,0:T(8,128)}) conditional(s32[]{:T(128)} %convert_element_type.571, () %tuple.65, (f32[512,960]{0,1:T(8,128)}, bf16[2,960]{1,0:T(2,128)(2,1)S(1)}, ...), branch_computations={%region_43.44_spmd, %region_44.54_spmd} | conditional | flops 30854017024 | bytes 574429760 | solution.py:357
  1527.9 12.3 multiply_convert_fusion.20
  1595.3 9.5 fusion.125
  1618.4 61.2 %broadcast_in_dim.158 = f32[49153,960]{1,0:T(8,128)} broadcast(f32[]{:T(128)} %constant.216.clone.1), dimensions={} | broadcast | bytes 188747520 | tf_op jit(solution)/shard_map/broadcast_in_dim | solution.py:376
  1679.5 69.8 %scatter_fusion.1 = f32[49153,960]{1,0:T(8,128)} fusion(f32[49153,960]{1,0:T(8,128)} %broadcast_in_dim.158, s32[512]{0:T(512)S(1)} %bitcast.696, f32[512,960]{1,0:T(8,128)S(1)} %copy.315), kind=kCustom, calls=%fused_computation.8 | custom fusion | flops 491520 | bytes 5900288 | tf_op jit(solution)/shard_map/scatter-add | solution.py:376
  1749.3 130.4 %slice.395 = f32[49152,960]{1,0:T(8,128)} slice(f32[49153,960]{1,0:T(8,128)} %scatter_fusion.1), slice={[0:49152], [0:960]} | slice | bytes 377487360 | tf_op jit(solution)/shard_map/slice | solution.py:376
  1879.7 188.5 %copy.377 = f32[49152,960]{0,1:T(8,128)} copy(f32[49152,960]{1,0:T(8,128)} %slice.395) | data formatting | bytes 377487360
  2074.5 17.5 add_add_fusion.1
  2102.5 18.3 fusion.181
  2120.8 9.1 add_add_fusion.3
  2130.0 30.3 add_add_fusion
  2160.3 1571.1 %reduce-scatter.15.cloned.1.call-done = f32[3072,960]{0,1:T(8,128)} async-done(((f32[49152,960]{0,1:T(8,128)}), f32[3072,960]{0,1:T(8,128)}) %reduce-scatter.15.cloned.1.call-update) | async-done | bytes 11796496 | tf_op jit(solution)/shard_map/reduce_scatter | solution.py:375
  3731.4 13.2 add_convert_fusion.12
  3744.6 12.6 add_add_fusion.2
  3757.2 345.3 %fusion.270 = (f32[64,1600]{1,0:T(8,128)S(1)}, f32[64,960]{1,0:T(8,128)S(1)}, f32[64,5120]{1,0:T(8,128)S(1)}) fusion(f32[960,1600]{1,0:T(8,128)} %add_add_fusion.2, f32[960,960]{1,0:T(8,128)} %add_add_fusion.3, f32[960,5120]{1,0:T(8,128)} %add_add_fusion), kind=kCustom, calls=%all-reduce-scatter.3 | all-reduce-scatter fusion | flops 7864321 | bytes 31457792
  4103.8 27.7 collective-permute-start.6
  4140.1 64.8 %all-reduce.14 = (f32[2,960]{1,0:T(2,128)S(1)}, bf16[960]{0:T(1024)(128)(2,1)S(1)}) all-reduce(f32[2,960]{1,0:T(2,128)S(1)} %fusion.233, f32[960]{0:T(1024)S(1)} %copy-done.102), channel_id=15, replica_groups=mesh['section'=2,'fsdp'=16] {'fsdp'}, use_global_device_ids=true, to_apply=%region_64.65.clone | all-reduce | flops 2880 | bytes 21120
  4239.1 36.8 psum.37
  4301.7 26.4 multiply_reduce_fusion.17
  4330.9 42.6 all-reduce.13
  4398.5 17.5 fusion.275
  (605 shorter events, 426.9 us)
Async XLA Ops:
  7.2 57.7 %all-gather.21.cloned.1.call-start = ((), (), s32[]{:S(2)}) async-start(), calls=%async_computation.10 | async-start | bytes 4177920 | tf_op jit(solution)/shard_map/all_gather | solution.py:276
  10.0 119.0 %all-gather.19.cloned.1.call-start = ((), (), s32[]{:S(2)}) async-start(), calls=%async_computation.9 | async-start | bytes 6789120 | tf_op jit(solution)/shard_map/all_gather | solution.py:275
  13.4 219.1 %all-gather.23.cloned.1.call-start = ((), (), s32[]{:S(2)}) async-start(), calls=%async_computation.11 | async-start | bytes 20889600 | tf_op jit(solution)/shard_map/all_gather | solution.py:277
  19.3 699.4 %all-gather.15.cloned.1.call-start = ((), (), s32[]{:S(2)}) async-start(), calls=%async_computation.3 | async-start | bytes 106954752 | tf_op jit(solution)/shard_map/all_gather | solution.py:284
  29.2 28.1 copy-start.101
  29.2 748.2 %all-gather.25.cloned.1.call-start = ((), (), s32[]{:S(2)}) async-start(), calls=%async_computation.12 | async-start | bytes 5570560 | tf_op jit(solution)/shard_map/all_gather | solution.py:278
  31.1 1013.4 %all-gather.17.cloned.1.call-start = ((), (), s32[]{:S(2)}) async-start(), calls=%async_computation.4 | async-start | bytes 2228224 | tf_op jit(solution)/shard_map/all_gather | solution.py:313
  58.5 718.9 %copy-start.89 = (pred[512,512]{0,1:T(8,128)(4,1)}, pred[512,512]{0,1:T(8,128)(4,1)S(1)}, u32[]{:S(2)}) copy-start(pred[512,512]{0,1:T(8,128)(4,1)S(1)} %fusion.200) | copy-start | bytes 786436
  822.2 48.2 %copy-start.28 = (bf16[1,960,1600]{2,1,0:T(8,128)(2,1)S(1)}, bf16[1,960,1600]{2,1,0:T(8,128)(2,1)}, u32[]{:S(2)}) copy-start(bf16[1,960,1600]{2,1,0:T(8,128)(2,1)} %copy.465) | copy-start | bytes 9216004
  824.3 45.0 %collective-permute-start = (f32[512,960]{0,1:T(8,128)S(1)}, f32[512,960]{0,1:T(8,128)S(1)}, u32[]{:S(2)}, u32[]{:S(2)}) collective-permute-start(f32[512,960]{0,1:T(8,128)S(1)} %broadcast_select_fusion.3), channel_id=1, source_target_pairs={{0,16},{16,0},{1,17},{17,1},{2,18},{18,2},{3,19},{19,3},{4,20},{20... | collective-permute-start | bytes 5898248 | tf_op jit(solution)/shard_map/ppermute | solution.py:31
  824.6 49.1 %copy-start.61 = (f32[512,32]{0,1:T(8,128)}, f32[512,32]{0,1:T(8,128)S(1)}, u32[]{:S(2)}) copy-start(f32[512,32]{0,1:T(8,128)S(1)} %get-tuple-element.968) | copy-start | bytes 196612
  824.7 49.1 %copy-start.63 = (f32[512,32]{0,1:T(8,128)}, f32[512,32]{0,1:T(8,128)S(1)}, u32[]{:S(2)}) copy-start(f32[512,32]{0,1:T(8,128)S(1)} %get-tuple-element.969) | copy-start | bytes 196612
  830.5 41.9 copy-start.86
  830.6 62.3 %copy-start.76 = (f32[960]{0:T(1024)}, f32[960]{0:T(1024)S(1)}, u32[]{:S(2)}) copy-start(f32[960]{0:T(1024)S(1)} %get-tuple-element.804) | copy-start | bytes 11524
  910.4 44.4 %collective-permute-start.1 = (f32[512,960]{0,1:T(8,128)}, f32[512,960]{0,1:T(8,128)S(1)}, u32[]{:S(2)}, u32[]{:S(2)}) collective-permute-start(f32[512,960]{0,1:T(8,128)} %convolution_add_fusion.4), channel_id=1, source_target_pairs={{0,16},{16,0},{1,17},{17,1},{2,18},{18,2},{3,19},{19,3},{4,20},{20... | collective-permute-start | bytes 5898248 | tf_op jit(solution)/shard_map/ppermute | solution.py:31
  971.1 250.2 %reduce-scatter.11.cloned.1.call-start = ((), (), s32[]{:S(2)}) async-start(), calls=%async_computation.5 | async-start | bytes 4456448 | tf_op jit(solution)/shard_map/reduce_scatter | solution.py:336
  1151.6 2579.8 %reduce-scatter.15.cloned.1.call-start = ((), (), s32[]{:S(2)}) async-start(), calls=%async_computation.7 | async-start | bytes 200540160 | tf_op jit(solution)/shard_map/reduce_scatter | solution.py:375
  1254.8 155.8 %copy-start.7 = (f32[960,960]{1,0:T(8,128)}, f32[960,960]{1,0:T(8,128)S(1)}, u32[]{:S(2)}) copy-start(f32[960,960]{1,0:T(8,128)S(1)} %get-tuple-element.425) | copy-start | bytes 11059204
  1254.8 155.8 %copy-start.99 = (f32[2,960]{1,0:T(2,128)}, f32[2,960]{1,0:T(2,128)S(1)}, u32[]{:S(2)}) copy-start(f32[2,960]{1,0:T(2,128)S(1)} %get-tuple-element.431) | copy-start | bytes 23044
  1254.8 155.8 %slice-start.3 = ((s8[9830400]{0:T(1024)(128)(4,1)}), s8[4194304]{0:T(1024)(128)(4,1)S(1)}, s32[]{:S(2)}) async-start(s8[9830400]{0:T(1024)(128)(4,1)} %bitcast.531), calls=%async_computation.16 | async-start | bytes 8388608
  1258.2 152.3 %slice-start.4 = ((s8[9830400]{0:T(1024)(128)(4,1)}), s8[4194304]{0:T(1024)(128)(4,1)S(1)}, s32[]{:S(2)}) async-start(s8[9830400]{0:T(1024)(128)(4,1)} %bitcast.531), calls=%async_computation.17 | async-start | bytes 8388608
  1258.2 152.3 %slice-start.5 = ((s8[9830400]{0:T(1024)(128)(4,1)}), s8[1441792]{0:T(1024)(128)(4,1)S(1)}, s32[]{:S(2)}) async-start(s8[9830400]{0:T(1024)(128)(4,1)} %bitcast.531), calls=%async_computation.18 | async-start | bytes 2883584
  1258.3 152.3 %copy-start.77 = (f32[960]{0:T(1024)S(1)}, f32[960]{0:T(1024)}, u32[]{:S(2)}) copy-start(f32[960]{0:T(1024)} %copy-done.76) | copy-start | bytes 11524
  1258.3 152.3 %copy-start.92 = (f32[512]{0:T(512)S(1)}, f32[512]{0:T(512)}, u32[]{:S(2)}) copy-start(f32[512]{0:T(512)} %copy-done.91) | copy-start | bytes 6148
  1258.3 141.0 %collective-permute-start.2 = (f32[512,960]{0,1:T(8,128)S(1)}, f32[512,960]{0,1:T(8,128)S(1)}, u32[]{:S(2)}, u32[]{:S(2)}) collective-permute-start(f32[512,960]{0,1:T(8,128)S(1)} %broadcast_select_fusion.1), channel_id=1, source_target_pairs={{0,16},{16,0},{1,17},{17,1},{2,18},{18,2},{3,19},{19,3},{4,20},{20... | collective-permute-start | bytes 5898248 | tf_op jit(solution)/shard_map/ppermute | solution.py:31
  1423.4 28.6 copy-start.6
  1452.0 42.9 copy-start.90
  1452.6 42.4 collective-permute-start.3
  1618.4 61.2 %copy-start.106 = (s32[512,1]{0,1:T(1,128)S(1)}, s32[512,1]{0,1:T(1,128)}, u32[]{:S(2)}) copy-start(s32[512,1]{0,1:T(1,128)} %get-tuple-element.972) | copy-start | bytes 6148
  2068.3 2156.9 %reduce-scatter.13.cloned.1.call-start = ((), (), s32[]{:S(2)}) async-start(), calls=%async_computation.6 | async-start | bytes 11141120 | tf_op jit(solution)/shard_map/reduce_scatter | solution.py:386
  2092.1 2139.1 %all-reduce.18.cloned.1.call-start = ((), (), s32[]{:S(2)}) async-start(), calls=%async_computation.8 | async-start | bytes 11796480 | tf_op jit(solution)/shard_map/psum | solution.py:391
  2102.5 27.4 slice-start.18
  2102.5 27.4 slice-start.19
  2102.5 27.4 slice-start.20
  2130.0 1601.4 %copy-start.120 = (bf16[1024,960]{1,0:T(8,128)(2,1)S(1)}, bf16[1024,960]{1,0:T(8,128)(2,1)}, u32[]{:S(2)}) copy-start(bf16[1024,960]{1,0:T(8,128)(2,1)} %all-gather.17.cloned.1.call-done) | copy-start | bytes 5898244
  3757.2 375.5 %copy-start.105 = (f32[1,2,60]{2,1,0:T(2,128)S(1)}, f32[1,2,60]{2,1,0:T(2,128)}, u32[]{:S(2)}) copy-start(f32[1,2,60]{2,1,0:T(2,128)} %param.44) | copy-start | bytes 1444
  4102.5 36.9 copy-start.100
  4102.6 36.8 copy-start.110
  4102.6 36.8 copy-start.111
  4102.6 37.5 copy-start.102
  4103.8 110.5 %collective-permute-start.6 = (f32[60,5120]{1,0:T(8,128)}, f32[60,5120]{1,0:T(8,128)}, u32[]{:S(2)}, u32[]{:S(2)}) collective-permute-start(f32[60,5120]{1,0:T(8,128)} %slice.398), channel_id=1, source_target_pairs={{0,1},{1,2},{2,3},{3,4},{4,5},{5,6},{6,7},{7,8},{8,9},{9,10},{10,1... | collective-permute-start | bytes 3686408
  4133.4 79.7 %collective-permute-start.4 = (f32[60,1600]{1,0:T(8,128)S(1)}, f32[60,1600]{1,0:T(8,128)S(1)}, u32[]{:S(2)}, u32[]{:S(2)}) collective-permute-start(f32[60,1600]{1,0:T(8,128)S(1)} %slice.396), channel_id=1, source_target_pairs={{0,1},{1,2},{2,3},{3,4},{4,5},{5,6},{6,7},{7,8},{8,9},{9,10},{10,1... | collective-permute-start | bytes 1152008
  4136.8 74.4 %collective-permute-start.5 = (f32[60,960]{1,0:T(8,128)S(1)}, f32[60,960]{1,0:T(8,128)}, u32[]{:S(2)}, u32[]{:S(2)}) collective-permute-start(f32[60,960]{1,0:T(8,128)S(1)} %slice.397), channel_id=1, source_target_pairs={{0,1},{1,2},{2,3},{3,4},{4,5},{5,6},{6,7},{7,8},{8,9},{9,10},{10,1... | collective-permute-start | bytes 691208
  4225.2 52.1 %copy-start.114 = (f32[1,2,60]{2,1,0:T(2,128)S(1)}, f32[1,2,60]{2,1,0:T(2,128)}, u32[]{:S(2)}) copy-start(f32[1,2,60]{2,1,0:T(2,128)} %param.51) | copy-start | bytes 1444
  4225.2 52.1 %copy-start.115 = (f32[1,2,60]{2,1,0:T(2,128)S(1)}, f32[1,2,60]{2,1,0:T(2,128)}, u32[]{:S(2)}) copy-start(f32[1,2,60]{2,1,0:T(2,128)} %param.58) | copy-start | bytes 1444
  4225.2 54.2 %copy-start.26 = (f32[1,60,1600]{2,0,1:T(1,128)S(1)}, f32[1,60,1600]{2,0,1:T(1,128)}, u32[]{:S(2)}) copy-start(f32[1,60,1600]{2,0,1:T(1,128)} %param.40) | copy-start | bytes 1152004
  4231.2 51.2 %copy-start.38 = (f32[1,60,960]{2,0,1:T(1,128)S(1)}, f32[1,60,960]{2,0,1:T(1,128)}, u32[]{:S(2)}) copy-start(f32[1,60,960]{2,0,1:T(1,128)} %param.41) | copy-start | bytes 691204
  4237.5 47.5 %copy-start.8 = (f32[1,60,5120]{2,0,1:T(1,128)S(1)}, f32[1,60,5120]{2,0,1:T(1,128)}, u32[]{:S(2)}) copy-start(f32[1,60,5120]{2,0,1:T(1,128)} %param.42) | copy-start | bytes 3686404
  (108 other events, 823.7 us)
Sparse Core Ops, SparseCore 0:
  10.9 53.9 all-gather.20
  67.6 61.3 all-gather.18
  131.2 101.2 all-gather.22
  234.5 484.1 all-gather.14
  721.4 55.9 all-gather.24
  971.2 73.2 all-gather.16
  1151.7 69.5 reduce-scatter.10
  2068.4 1662.9 reduce-scatter.14
  3736.6 200.5 reduce-scatter.12
  3940.2 144.0 all-reduce.17
where the time goes:
time: 4440 us; the launch traced here: 4430 us
  waiting for transfers between devices  2530 us (57%)
  blocking collectives  611 us (14%)
  local copies, waits for them, and re-layouts  512 us (12%)
  other arithmetic  322 us (7%)
  matrix products  275 us (6%)
  starting transfers between devices  136 us (3%)
    reduce_scatter x1, waiting for transfers between devices, shards(): lax.psum_scatter(jax.ops.segment_sum(grad_embedded, slot, num_segments=co...  1570 us
    all_gather x1, waiting for transfers between devices, shards(): piece = lax.all_gather(table_low, 'fsdp', axis=0, tiled=True)  470 us
    unnamed x4, blocking collectives  446 us
    unnamed x245, local copies, waits for them, and re-layouts  264 us
    ppermute x4, waiting for transfers between devices, swapped(): lax.ppermute(array, axis, [(i, i ^ 1 << stride) for i in range(lax.axis_s...  131 us
    slice x1, local copies, waits for them, and re-layouts, shards(): jax.ops.segment_sum(grad_embedded, slot, num_segments=count + 1)[:count]  130 us
    ppermute x4, starting transfers between devices, swapped(): lax.ppermute(array, axis, [(i, i ^ 1 << stride) for i in range(lax.axis_s...  102 us
    all_gather x1, waiting for transfers between devices, shards(): lax.all_gather(gu_low, 'fsdp', axis=0, tiled=True)  98.5 us
  transfers between devices with their start and end apart: 17, of which 12 were waited for; matrix products, arithmetic and copies ran while one was open for 12% of the time, Pallas kernels for 0%

commit v1 on v0

v1 whole, which is shorter than its diff:
```python
import jax
import jax.numpy as jnp
from jax import lax
from jax.sharding import PartitionSpec as P

HEADS = 15
KV = 5
HD = 64
FF = 2560
PROMPT = 256
NCONT = 2
CONT = 128
SCORED = 32
STEP = 10
TOK_MB = 512

EPS = 1e-05
SCALE = 0.125
THETA = 100000.0
BETA = 0.1
CLIP = 1.0
RATE = 0.3
BETA_ONE = 0.9
BETA_TWO = 0.99
ADAM_EPS = 1e-08
DECAY = 0.01

WIDTH = HEADS * HD
KVW = KV * HD
BOTH = ("section", "fsdp")
HI = lax.Precision.HIGHEST
LOW = jnp.bfloat16


def up16(count):
    return -(-count // 16) * 16


def dense(left, right):
    return jnp.dot(left, right, preferred_element_type=jnp.float32)


def dense_t(left, right):
    return lax.dot_general(
        left, right, (((0,), (0,)), ((), ())), preferred_element_type=jnp.float32
    )


def dense_nt(left, right):
    return lax.dot_general(
        left, right, (((1,), (1,)), ((), ())), preferred_element_type=jnp.float32
    )


def spread_matrix(parts, real, padded):
    feature = jnp.arange(parts * real)
    place = feature // real * padded + feature % real
    return (place[:, None] == jnp.arange(parts * padded)[None, :]).astype(LOW)


def inverse_rms(x, width):
    return lax.rsqrt(jnp.sum(x * x, axis=-1, keepdims=True) / width + EPS)


def norm_back(x, scale, gain, upstream, width):
    inner = upstream * gain
    grad_gain = jnp.sum(upstream * x * scale, axis=0)
    mean = jnp.sum(inner * x, axis=-1, keepdims=True) / width
    return (scale * inner - x * scale**3 * mean, grad_gain)


def rotate(x, cosine, sine):
    half = x.shape[-1] // 2
    first, second = (x[..., :half], x[..., half:])
    return jnp.concatenate(
        [first * cosine - second * sine, second * cosine + first * sine], axis=-1
    )


def rotate_back(grad, cosine, sine):
    return rotate(grad, cosine, -sine)


def rotary_angles(place):
    rotary = jnp.where(place >= PROMPT, PROMPT + (place - PROMPT) % CONT, place).astype(jnp.float32)
    freq = THETA ** (-2.0 * jnp.arange(HD // 2).astype(jnp.float32) / HD)
    angle = rotary[:, None] * freq[None, :]
    return (jnp.cos(angle)[:, None, :], jnp.sin(angle)[:, None, :])


def may_attend(place):
    keys = jnp.arange(TOK_MB)

    def segment(p):
        return jnp.where(p >= PROMPT, 1 + (p - PROMPT) // CONT, 0)

    return (keys[None, :] <= place[:, None]) & (
        (segment(keys)[None, :] == 0) | (segment(keys)[None, :] == segment(place)[:, None])
    )


def attend(query, key, value, allowed):
    scores = jnp.einsum("qhgd,khd->hgqk", query, key, preferred_element_type=jnp.float32) * SCALE
    scores = jnp.where(allowed, scores, -1e30)
    expo = jnp.exp(scores - jnp.max(scores, axis=-1, keepdims=True))
    probs = expo / jnp.sum(expo, axis=-1, keepdims=True)
    out = jnp.einsum("hgqk,khd->qhgd", probs.astype(LOW), value, preferred_element_type=jnp.float32)
    return (out.reshape(-1, WIDTH).astype(LOW), probs)


def attend_back(query, key, value, probs, grad):
    grad = grad.reshape(-1, KV, HEADS // KV, HD)
    grad_probs = jnp.einsum("qhgd,khd->hgqk", grad, value, preferred_element_type=jnp.float32)
    grad_scores = probs * (grad_probs - jnp.sum(grad_probs * probs, axis=-1, keepdims=True))
    grad_scores = grad_scores.astype(LOW)
    grad_query = (
        jnp.einsum("hgqk,khd->qhgd", grad_scores, key, preferred_element_type=jnp.float32) * SCALE
    )
    grad_key = (
        jnp.einsum("hgqk,qhgd->khd", grad_scores, query, preferred_element_type=jnp.float32) * SCALE
    )
    grad_value = jnp.einsum(
        "hgqk,qhgd->khd", probs.astype(LOW), grad, preferred_element_type=jnp.float32
    )
    return (grad_query.reshape(-1, HEADS, HD), grad_key, grad_value)


def heads_of(q, cosine, sine):
    return (
        rotate(q.reshape(-1, HEADS, HD), cosine, sine).astype(LOW).reshape(-1, KV, HEADS // KV, HD)
    )


def keys_values(kv, cosine, sine):
    key = rotate(kv[:, :KVW].reshape(-1, KV, HD), cosine, sine).astype(LOW)
    return (key, kv[:, KVW:].reshape(-1, KV, HD).astype(LOW))


def mlp(b, w_gu, w_down):
    gate_up = dense(b, w_gu)
    half = gate_up.shape[1] // 2
    gate, upper = (gate_up[:, :half], gate_up[:, half:])
    hidden = (jax.nn.silu(gate) * upper).astype(LOW)
    return (dense(hidden, w_down), gate, upper, hidden)


def mlp_back(branch, b, gate, upper, hidden, w_gu, w_down):
    grad_down = dense_t(hidden, branch)
    grad_hidden = dense_nt(branch, w_down)
    sig = jax.nn.sigmoid(gate)
    grad_gate = grad_hidden * upper * sig * (1.0 + gate * (1.0 - sig))
    grad_upper = grad_hidden * gate * sig
    grad_gate_up = jnp.concatenate([grad_gate, grad_upper], axis=1).astype(LOW)
    return (grad_down, dense_t(b, grad_gate_up), dense_nt(grad_gate_up, w_gu))


def lamb_parts(weight, grad, first, second, decay):
    first_new = BETA_ONE * first + (1.0 - BETA_ONE) * grad
    second_new = BETA_TWO * second + (1.0 - BETA_TWO) * grad * grad
    update = (
        first_new
        / (1.0 - BETA_ONE**STEP)
        / (jnp.sqrt(second_new / (1.0 - BETA_TWO**STEP)) + ADAM_EPS)
        + decay * weight
    )
    return (first_new, second_new, update)


def lookup_ranks(ids, vshard):
    place = jnp.arange(ids.shape[0])
    same = ids[:, None] == ids[None, :]
    first = jnp.min(jnp.where(same, place[None, :], ids.shape[0]), axis=1)
    owner = ids // vshard
    before = (
        (owner[:, None] == owner[None, :])
        & (first == place)[None, :]
        & (place[None, :] < first[:, None])
    )
    return (owner, jnp.sum(before.astype(jnp.int32), axis=1))


def lookup_round(ids, owner, rank, turn, slots, parts, vshard):
    slot = jnp.where(rank // slots == turn, owner * slots + rank - turn * slots, -1)
    onehot = slot[:, None] == jnp.arange(parts * slots)[None, :]
    wanted = jnp.max(jnp.where(onehot, (ids - owner * vshard)[:, None], -1), axis=0)
    return (onehot.astype(LOW), wanted)


def shards(
    token_ids,
    scored,
    targets,
    pairs,
    table,
    w_qkv,
    w_out,
    w_gu,
    w_down,
    gains,
    final_gain,
    first_table,
    first_qkv,
    first_out,
    first_gu,
    first_down,
    first_gains,
    first_final,
    second_table,
    second_qkv,
    second_out,
    second_gu,
    second_down,
    second_gains,
    second_final,
):
    n = lax.axis_size("fsdp")
    sections = lax.axis_size("section")
    section_index = lax.axis_index("section")
    fsdp_index = lax.axis_index("fsdp")
    leader = section_index == 0
    vshard, width = table.shape
    vstart = fsdp_index * vshard
    r = w_qkv.shape[1]
    rp = up16(r)
    rd = w_down.shape[1]
    rdp = up16(rd)
    wide = n * rp
    ffp = n * rdp
    slots = up16(768 // n)
    sel = spread_matrix(n, r, rp)

    qkv_block = jnp.pad(w_qkv[0].astype(LOW), ((0, rp - r), (0, 0)))
    out_block = jnp.pad(dense(w_out[0].astype(LOW), sel).astype(LOW), ((0, rp - r), (0, 0)))
    gu_block = w_gu[0].astype(LOW)
    if rdp != rd:
        gu_block = jnp.pad(gu_block.reshape(r, 2, n, rd), ((0, 0), (0, 0), (0, 0), (0, rdp - rd)))
    gu_block = jnp.pad(gu_block.reshape(r, 2 * ffp), ((0, rp - r), (0, 0)))
    down_block = jnp.pad(dense(w_down[0].astype(LOW), sel).astype(LOW), ((0, rdp - rd), (0, 0)))
    gain_block = jnp.pad(
        jnp.concatenate([gains[0], final_gain[None]], axis=0).astype(LOW), ((0, 0), (0, rp - r))
    )

    ids = token_ids[0]
    owner, rank = lookup_ranks(ids, vshard)
    onehot, wanted = lookup_round(ids, owner, rank, 0, slots, n, vshard)
    note = jnp.concatenate([wanted, jnp.full((128,), jnp.max(rank) // slots + 1, jnp.int32)])
    notes = lax.all_gather(note, BOTH, axis=0)
    turns = jnp.max(notes[:, n * slots])

    def asked(all_wanted):
        mine = lax.dynamic_slice_in_dim(all_wanted.reshape(sections, n, n, slots), fsdp_index, 1, 2)
        return mine[:, :, 0]

    def fetch(all_asked, choose):
        here = lax.dynamic_index_in_dim(all_asked, section_index, 0, keepdims=False).reshape(-1)
        rows = jnp.take(table, jnp.maximum(here, 0), axis=0).astype(LOW)
        got = lax.all_to_all(rows.reshape(n, slots, width), "fsdp", 0, 0).reshape(n * slots, width)
        return dense(dense(choose, got).astype(LOW), sel)

    asked_first = asked(notes[:, : n * slots])
    x0 = fetch(asked_first, onehot)

    def fetch_more(state):
        turn, total = state
        choose, more = lookup_round(ids, owner, rank, turn, slots, n, vshard)
        return (turn + 1, total + fetch(asked(lax.all_gather(more, BOTH, axis=0)), choose))

    x0 = lax.while_loop(lambda state: state[0] < turns, fetch_more, (jnp.int32(1), x0))[1]

    def everywhere(block):
        return lax.all_gather(block, BOTH, axis=0, tiled=True).reshape(
            sections, n * block.shape[0], block.shape[1]
        )

    qkv_all = everywhere(qkv_block)
    out_all = everywhere(out_block)
    gu_all = everywhere(gu_block)
    down_all = everywhere(down_block)
    gain_all = lax.all_gather(gain_block, BOTH, axis=0).reshape(sections, n, 3, rp)
    gain_all = jnp.moveaxis(gain_all, 2, 1).reshape(sections, 3, wide).astype(jnp.float32)
    final_all = gain_all[0, 2]
    wanted_rows = lax.all_gather(targets[0].reshape(-1), "section", axis=0, tiled=True)

    everyone = jnp.arange(TOK_MB)
    cosine, sine = rotary_angles(everyone)
    allowed = may_attend(everyone)
    x = x0
    kept = []
    for layer in range(sections - 1):
        scale_a = inverse_rms(x, width)
        a = (x * scale_a * gain_all[layer, 0]).astype(LOW)
        qkv = dense(a, qkv_all[layer])
        query = heads_of(qkv[:, :WIDTH], cosine, sine)
        key, value = keys_values(qkv[:, WIDTH:], cosine, sine)
        attended, probs = attend(query, key, value, allowed)
        attended = dense(attended, sel).astype(LOW)
        mixed = x + dense(attended, out_all[layer])
        scale_b = inverse_rms(mixed, width)
        b = (mixed * scale_b * gain_all[layer, 1]).astype(LOW)
        branch, gate, upper, hidden = mlp(b, gu_all[layer], down_all[layer])
        kept.append(
            (x, scale_a, a, query, key, value, probs, attended, mixed, scale_b, b, gate, upper, hidden)
        )
        x = mixed + branch

    last = sections - 1
    place = (PROMPT + CONT * jnp.arange(NCONT)[:, None] + scored[0]).reshape(-1)
    pick = (place[:, None] == everyone[None, :]).astype(LOW)
    pick32 = pick.astype(jnp.float32)
    cosine_s, sine_s = rotary_angles(place)
    allowed_s = may_attend(place)
    scale_last = inverse_rms(x, width)
    a_last = (x * scale_last * gain_all[last, 0]).astype(LOW)
    key_last, value_last = keys_values(dense(a_last, qkv_all[last][:, WIDTH:]), cosine, sine)
    a_s = dense(pick, a_last).astype(LOW)
    x_s = jnp.dot(pick32, x, precision=HI)
    query_s = heads_of(dense(a_s, qkv_all[last][:, :WIDTH]), cosine_s, sine_s)
    attended_s, probs_s = attend(query_s, key_last, value_last, allowed_s)
    attended_s = dense(attended_s, sel).astype(LOW)
    mixed_s = x_s + dense(attended_s, out_all[last])
    scale_s = inverse_rms(mixed_s, width)
    b_s = (mixed_s * scale_s * gain_all[last, 1]).astype(LOW)
    branch_s, gate_s, upper_s, hidden_s = mlp(b_s, gu_all[last], down_all[last])
    y_s = mixed_s + branch_s
    scale_y = inverse_rms(y_s, width)
    head_in = dense_nt((y_s * scale_y * final_all).astype(LOW), sel).astype(LOW)

    rows_all = lax.all_gather(head_in, BOTH, axis=0, tiled=True)
    own_rows = rows_all.shape[0] // sections
    table_low = table.astype(LOW)
    logits = dense_nt(rows_all, table_low)
    hit = jnp.arange(vshard)[None, :] == (wanted_rows - vstart)[:, None]
    top_here = jnp.max(logits, axis=1)
    total_here = jnp.sum(jnp.exp(logits - top_here[:, None]), axis=1)
    target_here = jnp.sum(jnp.where(hit, logits, 0.0), axis=1)
    stats = lax.all_gather(jnp.stack([top_here, total_here, target_here]), "fsdp", axis=0)
    top = jnp.max(stats[:, 0], axis=0)
    total = jnp.sum(stats[:, 1] * jnp.exp(stats[:, 0] - top), axis=0)
    row_logp = jnp.sum(stats[:, 2], axis=0) - top - jnp.log(total)
    seq = jnp.sum(row_logp.reshape(-1, SCORED), axis=1)
    pair = pairs.reshape(-1, 2)
    conts = jnp.arange(seq.shape[0])
    chosen = (pair[:, 0][:, None] == conts[None, :]).astype(jnp.float32)
    passed = (pair[:, 1][:, None] == conts[None, :]).astype(jnp.float32)
    delta = jnp.sum((chosen - passed) * seq[None, :], axis=1)
    loss = jnp.sum(jax.nn.softplus(-BETA * delta))
    push = BETA * jax.nn.sigmoid(-BETA * delta)
    grad_seq = jnp.sum((passed - chosen) * push[:, None], axis=0)
    grad_row = jnp.repeat(grad_seq, SCORED)
    prob = jnp.exp(logits - top[:, None]) * (1.0 / total)[:, None]
    grad_logits = (grad_row[:, None] * (hit.astype(jnp.float32) - prob)).astype(LOW)
    grad_table = dense_t(grad_logits, rows_all)
    own_grads = lax.dynamic_slice_in_dim(grad_logits, section_index * own_rows, own_rows)
    grad_head = lax.psum_scatter(
        dense(own_grads, table_low).astype(LOW), "fsdp", scatter_dimension=0, tiled=True
    )
    grad_y, grad_final = norm_back(y_s, scale_y, final_all, dense(grad_head, sel), width)

    grads = [None] * sections
    g_down, g_gu, grad_b = mlp_back(
        grad_y.astype(LOW), b_s, gate_s, upper_s, hidden_s, gu_all[last], down_all[last]
    )
    grad_mid, gain_two = norm_back(mixed_s, scale_s, gain_all[last, 1], grad_b, width)
    grad_mixed = grad_mid + grad_y
    branch = grad_mixed.astype(LOW)
    g_out = dense_t(attended_s, branch)
    grad_att = dense_nt(dense_nt(branch, out_all[last]).astype(LOW), sel).astype(LOW)
    grad_query, grad_key, grad_value = attend_back(query_s, key_last, value_last, probs_s, grad_att)
    grad_q = rotate_back(grad_query, cosine_s, sine_s).reshape(-1, WIDTH).astype(LOW)
    grad_kv = jnp.concatenate(
        [rotate_back(grad_key, cosine, sine).reshape(-1, KVW), grad_value.reshape(-1, KVW)], axis=1
    ).astype(LOW)
    g_qkv = jnp.concatenate([dense_t(a_s, grad_q), dense_t(a_last, grad_kv)], axis=1)
    grad_a_s = dense_nt(grad_q, qkv_all[last][:, :WIDTH])
    spread_back = lax.dot_general(
        pick32,
        jnp.concatenate([grad_a_s, grad_mixed], axis=1),
        (((0,), (0,)), ((), ())),
        precision=HI,
    )
    grad_a = dense_nt(grad_kv, qkv_all[last][:, WIDTH:]) + spread_back[:, :wide]
    grad_in, gain_one = norm_back(x, scale_last, gain_all[last, 0], grad_a, width)
    upstream = grad_in + spread_back[:, wide:]
    grads[last] = (g_qkv, g_out, g_gu, g_down, jnp.stack([gain_one, gain_two]))

    for layer in range(sections - 2, -1, -1):
        (x, scale_a, a, query, key, value, probs, attended, mixed, scale_b, b, gate, upper, hidden) = kept[
            layer
        ]
        g_down, g_gu, grad_b = mlp_back(
            upstream.astype(LOW), b, gate, upper, hidden, gu_all[layer], down_all[layer]
        )
        grad_mid, gain_two = norm_back(mixed, scale_b, gain_all[layer, 1], grad_b, width)
        grad_mixed = grad_mid + upstream
        branch = grad_mixed.astype(LOW)
        g_out = dense_t(attended, branch)
        grad_att = dense_nt(dense_nt(branch, out_all[layer]).astype(LOW), sel).astype(LOW)
        grad_query, grad_key, grad_value = attend_back(query, key, value, probs, grad_att)
        grad_qkv = jnp.concatenate(
            [
                rotate_back(grad_query, cosine, sine).reshape(-1, WIDTH),
                rotate_back(grad_key, cosine, sine).reshape(-1, KVW),
                grad_value.reshape(-1, KVW),
            ],
            axis=1,
        ).astype(LOW)
        g_qkv = dense_t(a, grad_qkv)
        grad_in, gain_one = norm_back(
            x, scale_a, gain_all[layer, 0], dense_nt(grad_qkv, qkv_all[layer]), width
        )
        upstream = grad_in + grad_mixed
        grads[layer] = (g_qkv, g_out, g_gu, g_down, jnp.stack([gain_one, gain_two]))

    grad_x0 = dense_nt(upstream.astype(LOW), sel).astype(LOW)

    def give(grad_rows, all_asked, choose):
        rows = dense_t(choose, grad_x0).astype(LOW)
        got = lax.all_to_all(rows.reshape(n, slots, width), "fsdp", 0, 0)
        every = lax.all_gather(got, "section", axis=0).reshape(-1, width)
        place_of = (jnp.arange(vshard)[:, None] == all_asked.reshape(-1)[None, :]).astype(LOW)
        return grad_rows + dense(place_of, every)

    grad_table = give(grad_table, asked_first, onehot)

    def give_more(state):
        turn, grad_rows = state
        choose, more = lookup_round(ids, owner, rank, turn, slots, n, vshard)
        return (turn + 1, give(grad_rows, asked(lax.all_gather(more, BOTH, axis=0)), choose))

    grad_table = lax.while_loop(lambda state: state[0] < turns, give_more, (jnp.int32(1), grad_table))[1]

    def to_owner(which, rows_each):
        stacked = jnp.concatenate([grads[layer][which].astype(LOW) for layer in range(sections)], axis=0)
        return lax.psum_scatter(stacked, BOTH, scatter_dimension=0, tiled=True).astype(jnp.float32)

    s_qkv = to_owner(0, rp)[:r]
    s_out = to_owner(1, rp)[:r].reshape(r, n, rp)[:, :, :r].reshape(r, width)
    s_gu = to_owner(2, rp)[:r].reshape(r, 2, n, rdp)[:, :, :, :rd].reshape(r, 2 * n * rd)
    s_down = to_owner(3, rdp)[:rd].reshape(rd, n, rp)[:, :, :r].reshape(rd, width)
    small = lax.psum(
        jnp.concatenate([grads[layer][4] for layer in range(sections)] + [grad_final[None]], axis=0), BOTH
    )
    small = lax.dynamic_index_in_dim(
        small.reshape(2 * sections + 1, n, rp), fsdp_index, 1, keepdims=False
    )[:, :r]
    s_gains = lax.dynamic_slice_in_dim(small, 2 * section_index, 2)
    s_final = small[2 * sections]

    grads_all = (
        grad_table,
        s_qkv[None],
        s_out[None],
        s_gu[None],
        s_down[None],
        s_gains[None],
        s_final,
    )
    weights_all = (table, w_qkv, w_out, w_gu, w_down, gains, final_gain)
    firsts = (first_table, first_qkv, first_out, first_gu, first_down, first_gains, first_final)
    seconds = (
        second_table,
        second_qkv,
        second_out,
        second_gu,
        second_down,
        second_gains,
        second_final,
    )
    slot_total = 6 * sections + 2
    shared_share = jnp.where(leader, 1.0, 0.0)

    def slot_squares(arrays):
        rows_each_section = jnp.stack(
            [
                jnp.sum(arrays[1] ** 2),
                jnp.sum(arrays[2] ** 2),
                jnp.sum(arrays[3] ** 2),
                jnp.sum(arrays[4] ** 2),
                jnp.sum(arrays[5][0, 0] ** 2),
                jnp.sum(arrays[5][0, 1] ** 2),
            ]
        )
        slot_entries = 6 * section_index + jnp.arange(6)
        positioned_rows = jnp.sum(
            jnp.where(
                slot_entries[:, None] == jnp.arange(slot_total)[None, :],
                rows_each_section[:, None],
                0.0,
            ),
            axis=0,
        )
        common_prompt = shared_share * jnp.stack([jnp.sum(arrays[0] ** 2), jnp.sum(arrays[6] ** 2)])
        return positioned_rows + jnp.concatenate(
            [jnp.zeros((slot_total - 2,), jnp.float32), common_prompt]
        )

    grad_sq = lax.psum(slot_squares(grads_all), BOTH)
    grad_norm = jnp.sqrt(jnp.sum(grad_sq))
    clip = jnp.minimum(1.0, CLIP / grad_norm)
    decays = (DECAY, DECAY, DECAY, DECAY, DECAY, 0.0, 0.0)
    parts = [
        lamb_parts(w, clip * g, m, v, d)
        for w, g, m, v, d in zip(weights_all, grads_all, firsts, seconds, decays)
    ]
    squares = lax.psum(
        jnp.stack([slot_squares(weights_all), slot_squares(tuple((p[2] for p in parts)))]), BOTH
    )
    weight_norms, update_norms = (jnp.sqrt(squares[0]), jnp.sqrt(squares[1]))
    trust_ratio = weight_norms / update_norms
    own = lax.dynamic_slice_in_dim(trust_ratio, 6 * section_index, 6)
    scales = (
        trust_ratio[slot_total - 2],
        own[0],
        own[1],
        own[2],
        own[3],
        own[4:6][None, :, None],
        trust_ratio[slot_total - 1],
    )
    new = [w - RATE * s * p[2] for w, s, p in zip(weights_all, scales, parts)]
    matrix_norms = jnp.stack([weight_norms, update_norms])
    outs = [loss, grad_norm, matrix_norms]
    for k in range(7):
        outs += [new[k], parts[k][0], parts[k][1]]
    return tuple(outs + [new[k].astype(LOW) for k in range(5)])


def solution(mesh):
    tall, layered, gainy, flat = (
        P("fsdp", None),
        P("section", "fsdp", None),
        P("section", None, "fsdp"),
        P("fsdp"),
    )
    weights = (tall, layered, layered, layered, layered, gainy, flat)
    placed = (
        P("section", "fsdp"),
        P("section", "fsdp", None),
        P("section", None, None),
        P(),
    ) + weights * 3
    results = (P(), P(), P())
    for spec in weights:
        results += (spec, spec, spec)
    return jax.shard_map(
        shards, mesh=mesh, in_specs=placed, out_specs=results + weights[:5], check_vma=False
    )
```

time: 4440 us -> 1750 us (0.39)
  waiting for transfers between devices: 2530 us -> 842 us
  local copies, waits for them, and re-layouts: 512 us -> 99.6 us
  blocking collectives: 611 us -> 303 us
  starting transfers between devices: 136 us -> 4.58 us
  other arithmetic: 322 us -> 211 us
    reduce_scatter x3 -> x4, waiting for transfers between devices: 1640 us -> 431 us  [the longest x3 373 us: to_owner(): lax.psum_scatter(stacked, BOTH, scatter_dimension=0, tiled=True)]
    all_gather x6, waiting for transfers between devices: 757 us -> 266 us  [the longest x4 173 us: everywhere(): lax.all_gather(block, BOTH, axis=0, tiled=True)]
    unnamed x4 -> x0, blocking collectives: 446 us -> none
    unnamed x245 -> x339, local copies, waits for them, and re-layouts: 264 us -> 58.6 us
    unnamed x13 -> x12, waiting for transfers between devices: 0.17 us -> 145 us
    ppermute x4 -> x0, waiting for transfers between devices: 131 us -> none  [swapped(): lax.ppermute(array, axis, [(i, i ^ 1 << stride) for i in range(lax.axis_s...]
    slice x13 -> x11, local copies, waits for them, and re-layouts: 132 us -> 5.65 us  [the longest x3 2.86 us: keys_values(): return (key, kv[:, KVW:].reshape(-1, KV, HD).astype(LOW))]
    ppermute x4 -> x0, starting transfers between devices: 102 us -> none  [swapped(): lax.ppermute(array, axis, [(i, i ^ 1 << stride) for i in range(lax.axis_s...]
  transfers between devices with their start and end apart: 17 -> 12, of which waited for: 12 -> 9; matrix products, arithmetic and copies ran while one was open for 12% -> 11% of each run, Pallas kernels for 0% -> 0%
where the time goes in v1:
time: 1750 us; the launch traced here: 1740 us
  waiting for transfers between devices  842 us (48%)
  blocking collectives  303 us (17%)
  matrix products  250 us (14%)
  other arithmetic  211 us (12%)
  local copies, waits for them, and re-layouts  99.6 us (6%)
  between operations  24.2 us (1%)
    reduce_scatter x3, waiting for transfers between devices, to_owner(): lax.psum_scatter(stacked, BOTH, scatter_dimension=0, tiled=True)  373 us
    all_gather x4, waiting for transfers between devices, everywhere(): lax.all_gather(block, BOTH, axis=0, tiled=True)  173 us
    unnamed x12, waiting for transfers between devices  145 us
    dot_general x12, matrix products, dense_nt(): lax.dot_general(left, right, (((1,), (1,)), ((), ())), preferred_element_...  76 us
    dot_general x18, matrix products, dense(): return jnp.dot(left, right, preferred_element_type=jnp.float32)  75.8 us
    all_gather x1, blocking collectives, shards(): lax.all_gather(gain_block, BOTH, axis=0).reshape(sections, n, 3, rp)  68.6 us
    unnamed x339, local copies, waits for them, and re-layouts  58.6 us
    reduce_scatter x1, waiting for transfers between devices, shards(): lax.psum_scatter(dense(own_grads, table_low).astype(LOW), 'fsdp', scatter...  58.2 us
  transfers between devices with their start and end apart: 12, of which 9 were waited for; matrix products, arithmetic and copies ran while one was open for 11% of the time, Pallas kernels for 0%

profile of v1, /device:TPU:0, one launch (start us, length us, event | category | flops | bytes accessed | tf_op | source)
XLA Modules:
  0.0 1736.0 jit_solution(11294611305406440844)
XLA Ops:
  22.9 9.8 copy.197
  33.0 44.0 %all-gather.9 = s32[32,1,896]{2,1,0:T(1,128)S(1)} all-gather(s32[1,1,896]{2,1,0:T(1,128)S(1)} %reshape.1053), channel_id=5, replica_groups=mesh['section'=2,'fsdp'=16] {'section','fsdp'}, dimensions={0}, use_global_device_ids=true | all-gather | bytes 118272 | tf_op jit(solution)/shard_map/all_gather | solution.py:247
  77.9 7.4 gather_fusion.1
  91.3 68.6 %all-gather.10 = bf16[32,3,64]{2,1,0:T(4,128)(2,1)S(1)} all-gather(bf16[1,3,64]{2,1,0:T(4,128)(2,1)S(1)} %fusion.251), channel_id=6, replica_groups=mesh['section'=2,'fsdp'=16] {'section','fsdp'}, dimensions={0}, use_global_device_ids=true | all-gather | bytes 12672 | tf_op jit(solution)/shard_map/all_gather | solution.py:279
  170.7 4.6 fusion.67
  176.1 8.4 fusion.301
  184.6 7.0 fusion.117
  194.0 4.5 multiply_reduce_fusion.10
  199.1 101.5 %all-gather.31.cloned.1.call-done = bf16[2048,5120]{1,0:T(8,128)(2,1)} async-done(((bf16[64,5120]{1,0:T(8,128)(2,1)}), bf16[2048,5120]{1,0:T(8,128)(2,1)}) %all-gather.31.cloned.1.call-update) | async-done | bytes 20971536 | tf_op jit(solution)/shard_map/all_gather | solution.py:271
  300.6 9.1 fusion.36
  316.8 71.9 %all-gather.33.cloned.1.call-done = bf16[5120,1024]{1,0:T(8,128)(2,1)} async-done(((bf16[160,1024]{1,0:T(8,128)(2,1)}), bf16[5120,1024]{1,0:T(8,128)(2,1)}) %all-gather.33.cloned.1.call-update) | async-done | bytes 10485776 | tf_op jit(solution)/shard_map/all_gather | solution.py:271
  388.7 6.9 multiply_reduce_fusion.9
  417.3 6.1 fusion.32
  432.3 55.4 %all-gather.35.cloned.1.call-done = bf16[2048,960]{1,0:T(8,128)(2,1)} async-done(((bf16[64,960]{1,0:T(8,128)(2,1)}), bf16[2048,960]{1,0:T(8,128)(2,1)}) %all-gather.35.cloned.1.call-update) | async-done | bytes 3932176 | tf_op jit(solution)/shard_map/all_gather | solution.py:328
  487.7 22.3 %fusion.303 = (f32[2048]{0:T(1024)S(1)}, f32[2048,3072]{1,0:T(8,128)}) fusion(bf16[2048,960]{1,0:T(8,128)(2,1)} %all-gather.35.cloned.1.call-done, f32[3072,960]{0,1:T(8,128)} %param.33), kind=kOutput, calls=%fused_computation.549 | convolution fusion | flops 12088834048 | bytes 40902656 | tf_op jit(solution)/shard_map/dot_general | solution.py:50
  510.0 11.6 exponential_reduce_fusion
  521.7 21.1 %all-gather.11 = f32[16,3,2048]{2,1,0:T(4,128)S(1)} all-gather(f32[1,3,2048]{2,1,0:T(4,128)S(1)} %maximum_bitcast_fusion.13), channel_id=7, replica_groups=mesh['section'=2,'fsdp'=16] {'fsdp'}, dimensions={0}, use_global_device_ids=true | all-gather | bytes 417792 | tf_op jit(solution)/shard_map/all_gather | solution.py:336
  545.9 14.4 multiply_convert_fusion
  560.3 4.5 copy-done
  564.9 10.7 fusion.85
  575.7 58.2 %reduce-scatter.8.cloned.1.call-done = bf16[64,960]{1,0:T(8,128)(2,1)} async-done(((bf16[1024,960]{1,0:T(8,128)(2,1)}), bf16[64,960]{1,0:T(8,128)(2,1)}) %reduce-scatter.8.cloned.1.call-update) | async-done | bytes 122896 | tf_op jit(solution)/shard_map/reduce_scatter | solution.py:354
  641.0 7.0 multiply_reduce_fusion.19
  674.2 8.9 multiply_convert_fusion.2
  683.2 12.0 multiply_reduce_fusion.5
  697.1 5.6 fusion.122
  702.7 9.1 fusion.136
  712.5 6.7 fusion.24
  719.2 7.6 fusion.26
  740.7 40.3 %all_to_all.30 = bf16[16,48,960]{2,1,0:T(8,128)(2,1)} all-to-all(bf16[16,48,960]{2,1,0:T(8,128)(2,1)S(1)} %bitcast.354), channel_id=1, replica_groups=mesh['section'=2,'fsdp'=16] {'fsdp'}, dimensions={0} | all-to-all | bytes 2949120 | tf_op jit(solution)/shard_map/all_to_all | solution.py:418
  789.2 37.2 %all-gather.37.cloned.1.call-done = bf16[32,48,960]{2,1,0:T(8,128)(2,1)} async-done(((bf16[16,48,960]{2,1,0:T(8,128)(2,1)}), bf16[32,48,960]{2,1,0:T(8,128)(2,1)}) %all-gather.37.cloned.1.call-update) | async-done | bytes 2949136 | tf_op jit(solution)/shard_map/all_gather | solution.py:419
  826.4 14.2 fusion.23
  840.6 21.2 %convolution_add_fusion = f32[3072,960]{0,1:T(8,128)} fusion(f32[3072,960]{0,1:T(8,128)} %fusion.23, bf16[2048,3072]{1,0:T(8,128)(2,1)} %copy-done, bf16[2048,960]{1,0:T(8,128)(2,1)} %all-gather.35.cloned.1.call-done), kind=kOutput, calls=%fused_computation.84 | convolution fusion | flops 12082544640 | bytes 40108032 | tf_op jit(solution)/shard_map/dot_general | solution.py:44
  871.5 18.7 %maximum_maximum_fusion = bf16[2048,1600]{0,1:T(8,128)(2,1)} fusion(bf16[1024,640]{0,1:T(8,128)(2,1)S(1)} %copy-done.42, bf16[1024,960]{0,1:T(8,128)(2,1)S(1)} %convolution_convert_fusion.8, bf16[1024,1600]{0,1:T(8,128)(2,1)} %convolution_convert_fusion.5), kind=kLoop, calls=%fused_computation.83 | loop fusion | flops 19660800 | bytes 13107200 | tf_op jit(solution)/shard_map/concatenate | solution.py:433
  890.2 9.6 copy.246
  906.0 15.7 pad_maximum_fusion.1
  926.2 8.7 convolution_convert_fusion.2
  934.9 12.7 pad_maximum_fusion
  952.9 40.1 %psum.21 = f32[5,16,64]{2,1,0:T(8,128)S(1)} all-reduce(f32[5,16,64]{2,1,0:T(8,128)S(1)} %reshape.1013), channel_id=1, replica_groups=mesh['section'=2,'fsdp'=16] {'section','fsdp'}, use_global_device_ids=true, to_apply=%region_47.48 | all-reduce | flops 5120 | bytes 40960 | tf_op jit(solution)/shard_map/psum | solution.py:440
  994.3 8.0 multiply_reduce_fusion.2
  1009.9 143.7 %reduce-scatter.16.cloned.1.call-done = bf16[64,1600]{1,0:T(8,128)(2,1)} async-done(((bf16[2048,1600]{1,0:T(8,128)(2,1)}), bf16[64,1600]{1,0:T(8,128)(2,1)}) %reduce-scatter.16.cloned.1.call-update) | async-done | bytes 204816
  1155.6 149.6 %reduce-scatter.14.cloned.1.call-done = bf16[160,1024]{1,0:T(8,128)(2,1)} async-done(((bf16[5120,1024]{1,0:T(8,128)(2,1)}), bf16[160,1024]{1,0:T(8,128)(2,1)}) %reduce-scatter.14.cloned.1.call-update) | async-done | bytes 327696 | tf_op jit(solution)/shard_map/reduce_scatter | solution.py:434
  1307.6 218.9 %reduce-scatter.12.cloned.1.call-done = bf16[64,5120]{1,0:T(8,128)(2,1)} async-done(((bf16[2048,5120]{1,0:T(8,128)(2,1)}), bf16[64,5120]{1,0:T(8,128)(2,1)}) %reduce-scatter.12.cloned.1.call-update) | async-done | bytes 655376 | tf_op jit(solution)/shard_map/reduce_scatter | solution.py:434
  1532.6 45.3 %psum.22 = f32[14]{0:T(128)S(1)} all-reduce(f32[14]{0:T(128)S(1)} %pad_add_fusion), channel_id=1, replica_groups=mesh['section'=2,'fsdp'=16] {'section','fsdp'}, use_global_device_ids=true, to_apply=%region_57.58 | all-reduce | flops 14 | bytes 112 | tf_op jit(solution)/shard_map/psum | solution.py:497
  1584.9 4.5 multiply_reduce_fusion.24
  1599.3 5.1 multiply_reduce_fusion.12
  1609.6 27.4 %multiply_reduce_fusion.1 = (f32[]{:T(128)}, f32[]{:T(128)}, f32[3072,960]{0,1:T(8,128)}, f32[3072,960]{0,1:T(8,128)}) fusion(f32[3072,960]{0,1:T(8,128)} %param.33, f32[3072,960]{0,1:T(8,128)} %get-tuple-element.1059, f32[]{:T(128)S(6)} %min.3, f32[3072,960]{0,1:T(8,128)} %param.40, f32[3072,960]{0,1:T(8,128)} %param.47), kind=kLoop, calls=%fused_computation.65 | loop fusion | flops 53084160 | bytes 70778896 | tf_op jit(solution)/shard_map/reduce_sum | solution.py:492
  1639.8 39.6 %psum.23 = f32[2,14]{1,0:T(2,128)S(1)} all-reduce(f32[2,14]{1,0:T(2,128)S(1)} %pad_maximum_fusion.28), channel_id=1, replica_groups=mesh['section'=2,'fsdp'=16] {'section','fsdp'}, use_global_device_ids=true, to_apply=%region_77.78 | all-reduce | flops 28 | bytes 224 | tf_op jit(solution)/shard_map/psum | solution.py:505
  1706.0 20.8 %fusion.285 = (bf16[3072,960]{0,1:T(8,128)(2,1)}, f32[3072,960]{0,1:T(8,128)}) fusion(f32[3072,960]{0,1:T(8,128)} %param.33, f32[3072,960]{0,1:T(8,128)} %get-tuple-element.695, f32[3072,960]{0,1:T(8,128)} %get-tuple-element.694, f32[]{:T(128)} %bitcast.122), kind=kLoop, calls=%fused_computation.541 | loop fusion | flops 26542080 | bytes 53084164 | tf_op jit(solution)/shard_map/convert_element_type | solution.py:525
  (562 shorter events, 225.4 us)
Async XLA Ops:
  7.2 163.5 %all-gather.27.cloned.1.call-start = ((), (), s32[]{:S(2)}) async-start(), calls=%async_computation.9 | async-start | bytes 7028736 | tf_op jit(solution)/shard_map/all_gather | solution.py:271
  10.7 183.4 %all-gather.29.cloned.1.call-start = ((), (), s32[]{:S(2)}) async-start(), calls=%async_computation.10 | async-start | bytes 4325376 | tf_op jit(solution)/shard_map/all_gather | solution.py:271
  13.4 287.2 %all-gather.31.cloned.1.call-start = ((), (), s32[]{:S(2)}) async-start(), calls=%async_computation.11 | async-start | bytes 21626880 | tf_op jit(solution)/shard_map/all_gather | solution.py:271
  17.7 371.0 %all-gather.33.cloned.1.call-start = ((), (), s32[]{:S(2)}) async-start(), calls=%async_computation.12 | async-start | bytes 10813440 | tf_op jit(solution)/shard_map/all_gather | solution.py:271
  20.9 142.8 %copy-start.105 = (s32[512]{0:T(512)}, s32[512]{0:T(512)S(1)}, u32[]{:S(2)}) copy-start(s32[512]{0:T(512)S(1)} %get-tuple-element.769) | copy-start | bytes 6148
  85.3 74.8 %copy-start.141 = (s32[1,2,32]{2,1,0:T(2,128)S(1)}, s32[1,2,32]{2,1,0:T(2,128)}, u32[]{:S(2)}) copy-start(s32[1,2,32]{2,1,0:T(2,128)} %param.30) | copy-start | bytes 772
  86.8 76.9 %all-to-all-start.2 = ((bf16[16,48,960]{2,1,0:T(8,128)(2,1)}), bf16[16,48,960]{2,1,0:T(8,128)(2,1)S(1)}, u32[]{:S(2)}, u32[]{:S(2)}) async-start(bf16[16,48,960]{2,1,0:T(8,128)(2,1)} %select_convert_fusion.1), calls=%async_computation.2 | async-start | bytes 3145728 | tf_op jit(solution)/shard_map/all_to_all | solution.py:257
  90.6 397.1 %all-gather.35.cloned.1.call-start = ((), (), s32[]{:S(2)}) async-start(), calls=%async_computation.13 | async-start | bytes 4325376 | tf_op jit(solution)/shard_map/all_gather | solution.py:328
  161.0 9.7 copy-start.115
  161.0 487.0 %copy-start.92 = (f32[1,1,1024]{2,0,1:T(1,128)}, f32[1,1,1024]{2,0,1:T(1,128)S(1)}, u32[]{:S(2)}) copy-start(f32[1,1,1024]{2,0,1:T(1,128)S(1)} %get-tuple-element.752) | copy-start | bytes 12292
  161.0 534.2 %copy-start.98 = (f32[1,1,1024]{2,0,1:T(1,128)}, f32[1,1,1024]{2,0,1:T(1,128)S(1)}, u32[]{:S(2)}) copy-start(f32[1,1,1024]{2,0,1:T(1,128)S(1)} %get-tuple-element.754) | copy-start | bytes 12292
  168.3 257.1 %copy-start.118 = (s32[960]{0:T(1024)}, s32[960]{0:T(1024)S(1)}, u32[]{:S(2)}) copy-start(s32[960]{0:T(1024)S(1)} %get-tuple-element.1087) | copy-start | bytes 11524
  175.4 9.2 copy-start.80
  199.1 110.6 %copy-start.107 = (f32[512]{0:T(512)}, f32[512]{0:T(512)S(1)}, u32[]{:S(2)}) copy-start(f32[512]{0:T(512)S(1)} %get-tuple-element.764) | copy-start | bytes 6148
  412.8 10.8 slice-start.9
  416.7 231.3 %copy-start.14 = (f32[64,1024]{1,0:T(8,128)}, f32[64,1024]{1,0:T(8,128)S(1)}, u32[]{:S(2)}) copy-start(f32[64,1024]{1,0:T(8,128)S(1)} %get-tuple-element.800) | copy-start | bytes 786436
  427.0 206.9 %reduce-scatter.8.cloned.1.call-start = ((), (), s32[]{:S(2)}) async-start(), calls=%async_computation.14 | async-start | bytes 2228224 | tf_op jit(solution)/shard_map/reduce_scatter | solution.py:354
  564.9 69.0 %copy-start.119 = (s32[960]{0:T(1024)S(1)}, s32[960]{0:T(1024)}, u32[]{:S(2)}) copy-start(s32[960]{0:T(1024)} %copy-done.118) | copy-start | bytes 11524
  564.9 69.0 %copy-start.140 = (f32[64]{0:T(128)S(1)}, f32[64]{0:T(128)}, u32[]{:S(2)}) copy-start(f32[64]{0:T(128)} %copy-done.139) | copy-start | bytes 772
  575.6 60.8 %copy-start.138 = (f32[64]{0:T(128)S(1)}, f32[64]{0:T(128)}, u32[]{:S(2)}) copy-start(f32[64]{0:T(128)} %get-tuple-element.787) | copy-start | bytes 772
  575.6 250.8 %all-gather.37.cloned.1.call-start = ((), (), s32[]{:S(2)}) async-start(), calls=%async_computation.18 | async-start | bytes 4718592 | tf_op jit(solution)/shard_map/all_gather | solution.py:419
  636.6 11.4 copy-start.25
  674.2 21.0 %copy-start.4 = (f32[512,1024]{1,0:T(8,128)}, f32[512,1024]{1,0:T(8,128)S(1)}, u32[]{:S(2)}) copy-start(f32[512,1024]{1,0:T(8,128)S(1)} %slice_add_fusion) | copy-start | bytes 6291460
  683.2 12.0 copy-start.110
  697.1 14.7 slice-start
  702.7 9.5 slice-start.3
  702.7 9.5 copy-start.81
  702.7 9.5 copy-start.96
  702.7 9.8 copy-start.142
  740.7 41.5 %copy-start.54 = (bf16[512,960]{0,1:T(8,128)(2,1)S(1)}, bf16[512,960]{0,1:T(8,128)(2,1)}, u32[]{:S(2)}) copy-start(bf16[512,960]{0,1:T(8,128)(2,1)} %copy-done.53) | copy-start | bytes 2949124
  740.7 42.8 %copy-start.70 = (bf16[64,1024]{1,0:T(8,128)(2,1)S(1)}, bf16[64,1024]{1,0:T(8,128)(2,1)}, u32[]{:S(2)}) copy-start(bf16[64,1024]{1,0:T(8,128)(2,1)} %copy-done.69) | copy-start | bytes 393220
  840.6 21.2 %copy-start.49 = (bf16[512,960]{1,0:T(8,128)(2,1)S(1)}, bf16[512,960]{1,0:T(8,128)(2,1)}, u32[]{:S(2)}) copy-start(bf16[512,960]{1,0:T(8,128)(2,1)} %copy.215) | copy-start | bytes 2949124
  840.6 21.2 %copy-start.72 = (s32[1,512]{1,0:T(1,128)S(1)}, s32[1,512]{1,0:T(1,128)}, u32[]{:S(2)}) copy-start(s32[1,512]{1,0:T(1,128)} %param.29) | copy-start | bytes 6148
  840.6 21.2 %copy-start.87 = (s32[512]{0:T(512)S(1)}, s32[512]{0:T(512)}, u32[]{:S(2)}) copy-start(s32[512]{0:T(512)} %copy-done.86) | copy-start | bytes 6148
  840.6 21.2 %copy-start.89 = (s32[512]{0:T(512)S(1)}, s32[512]{0:T(512)}, u32[]{:S(2)}) copy-start(s32[512]{0:T(512)} %copy-done.88) | copy-start | bytes 6148
  840.6 21.2 %copy-start.91 = (s32[512,1]{0,1:T(1,128)S(1)}, s32[512,1]{0,1:T(1,128)}, u32[]{:S(2)}) copy-start(s32[512,1]{0,1:T(1,128)} %copy-done.90) | copy-start | bytes 6148
  862.7 145.4 %reduce-scatter.10.cloned.1.call-start = ((), (), s32[]{:S(2)}) async-start(), calls=%async_computation.15 | async-start | bytes 4325376 | tf_op jit(solution)/shard_map/reduce_scatter | solution.py:434
  863.5 290.1 %reduce-scatter.16.cloned.1.call-start = ((), (), s32[]{:S(2)}) async-start(), calls=%async_computation.19 | async-start | bytes 7028736
  899.9 405.3 %reduce-scatter.14.cloned.1.call-start = ((), (), s32[]{:S(2)}) async-start(), calls=%async_computation.17 | async-start | bytes 10813440 | tf_op jit(solution)/shard_map/reduce_scatter | solution.py:434
  921.8 604.7 %reduce-scatter.12.cloned.1.call-start = ((), (), s32[]{:S(2)}) async-start(), calls=%async_computation.16 | async-start | bytes 21626880 | tf_op jit(solution)/shard_map/reduce_scatter | solution.py:434
  1580.3 9.2 copy-start.19
  1599.2 9.2 copy-start.131
  1599.2 9.2 copy-start.136
  1599.3 9.2 copy-start.137
  1704.2 22.6 %copy-start.56 = (f32[1,60,960]{2,0,1:T(1,128)}, f32[1,60,960]{2,0,1:T(1,128)S(1)}, u32[]{:S(2)}) copy-start(f32[1,60,960]{2,0,1:T(1,128)S(1)} %multiply_subtract_fusion.7) | copy-start | bytes 691204
  1706.0 20.8 %copy-start.20 = (f32[1,160,960]{2,1,0:T(8,128)S(1)}, f32[1,160,960]{2,1,0:T(8,128)}, u32[]{:S(2)}) copy-start(f32[1,160,960]{2,1,0:T(8,128)} %param.37) | copy-start | bytes 1843204
  1706.0 20.8 %copy-start.21 = (f32[1,160,960]{2,1,0:T(8,128)S(1)}, f32[1,160,960]{2,1,0:T(8,128)}, u32[]{:S(2)}) copy-start(f32[1,160,960]{2,1,0:T(8,128)} %get-tuple-element.714) | copy-start | bytes 1843204
  1706.0 20.8 %copy-start.22 = (f32[1,160,960]{2,1,0:T(8,128)S(1)}, f32[1,160,960]{2,1,0:T(8,128)}, u32[]{:S(2)}) copy-start(f32[1,160,960]{2,1,0:T(8,128)} %get-tuple-element.715) | copy-start | bytes 1843204
  (123 other events, 511.2 us)
Sparse Core Ops, SparseCore 0:
  11.5 74.5 all-gather.26
  89.5 74.5 all-gather.28
  167.5 133.0 all-gather.30
  303.9 84.6 all-gather.32
  427.1 60.5 all-gather.34
  575.7 58.0 reduce-scatter.7
  781.1 45.2 all-gather.36
  866.5 141.5 reduce-scatter.9
  1010.5 143.0 reduce-scatter.15
  1156.3 148.8 reduce-scatter.13
  1307.5 218.9 reduce-scatter.11

commit v2 on v1

--- a/solution.py
+++ b/solution.py
@@ -1,6 +1,10 @@
+import functools
+
 import jax
 import jax.numpy as jnp
 from jax import lax
+from jax.experimental import pallas as pl
+from jax.experimental.pallas import tpu as pltpu
 from jax.sharding import PartitionSpec as P
 
 HEADS = 15
@@ -30,6 +34,329 @@
 BOTH = ("section", "fsdp")
 HI = lax.Precision.HIGHEST
 LOW = jnp.bfloat16
+
+WEIGHT_PIECES = [
+    (0, 0, 64, 0),
+    (1, 0, 64, 1),
+    (2, 0, 16, 0),
+    (2, 16, 16, 1),
+    (2, 32, 16, 0),
+    (2, 48, 16, 1),
+    (3, 0, 80, 0),
+    (3, 80, 80, 1),
+    (4, 0, 16, 1),
+]
+
+MESH = pl.DeviceIdType.MESH
+ANYWHERE = pl.BlockSpec(memory_space=pl.ANY)
+IN_VMEM = pl.BlockSpec(memory_space=pltpu.VMEM)
+TILE_R, TILE_C = 32, 1024
+
+
+def coords():
+    f = lax.axis_index("fsdp")
+    return (lax.axis_index("section"), f // 4, f // 2 % 2, f % 2)
+
+
+def device(y, z, x, c):
+    return (y, z * 4 + x * 2 + c)
+
+
+def greet(peers):
+    barrier = pltpu.get_barrier_semaphore()
+    for peer in peers:
+        pl.semaphore_signal(barrier, inc=1, device_id=peer, device_id_type=MESH)
+    pl.semaphore_wait(barrier, len(peers))
+
+
+def send(src, dst, send_sem, recv_sem, peer):
+    pltpu.make_async_remote_copy(
+        src_ref=src,
+        dst_ref=dst,
+        send_sem=send_sem,
+        recv_sem=recv_sem,
+        device_id=peer,
+        device_id_type=MESH,
+    ).start()
+
+
+def settle(ref, sem):
+    pltpu.make_async_copy(ref, ref, sem).wait()
+
+
+def gather_kernel(pieces, count, *refs):
+    blocks, outs = (refs[:count], refs[count : 2 * count])
+    send_sem, recv_sem, sib_sem, own_sem = refs[2 * count :]
+    y, z, x, c = coords()
+    to_x, to_y, to_sib = (device(y, z, 1 - x, c), device(1 - y, z, x, c), device(y, z, x, 1 - c))
+    zs = [(z + k) % 4 for k in range(4)]
+    greet([to_x, to_y, to_sib] + [device(y, zz, x, c) for zz in zs[1:]])
+
+    def part(ref, p):
+        return ref.at[pl.ds(pieces[p][1], pieces[p][2])]
+
+    def there(p, o):
+        return part(outs[pieces[p][0]].at[o[0] * 16 + o[1] * 4 + o[2] * 2 + c], p)
+
+    def mark(p, o):
+        return recv_sem.at[p, o[0] * 8 + o[1] * 2 + o[2]]
+
+    def push(p, o, peer, own=False, sib=False):
+        src = part(blocks[pieces[p][0]], p) if own else there(p, o)
+        send(src, there(p, o), send_sem.at[p], sib_sem.at[p] if sib else mark(p, o), peer)
+
+    every = range(len(pieces))
+    for p in every:
+        me = (y, z, x)
+        push(p, me, to_x, own=True)
+        push(p, me, to_y, own=True)
+        for zz in zs[1:]:
+            push(p, me, device(y, zz, x, c), own=True)
+        push(p, me, to_sib, own=True, sib=True)
+        pltpu.make_async_copy(part(blocks[pieces[p][0]], p), there(p, me), own_sem).start()
+
+    def from_x(p, zz):
+        o = (y, zz, 1 - x)
+        settle(there(p, o), mark(p, o))
+        if pieces[p][3] == 0:
+            push(p, o, to_y)
+        push(p, o, to_sib, sib=True)
+
+    def from_y(p, zz):
+        o = (1 - y, zz, x)
+        settle(there(p, o), mark(p, o))
+        if pieces[p][3] == 1:
+            push(p, o, to_x)
+        push(p, o, to_sib, sib=True)
+
+    for p in every:
+        for zz in zs[1:]:
+            o = (y, zz, x)
+            settle(there(p, o), mark(p, o))
+            push(p, o, to_x)
+            push(p, o, to_y)
+            push(p, o, to_sib, sib=True)
+        from_x(p, z)
+        from_y(p, z)
+    for p in every:
+        for zz in zs[1:]:
+            from_x(p, zz)
+            from_y(p, zz)
+    for p in every:
+        for zz in zs:
+            o = (1 - y, zz, 1 - x)
+            settle(there(p, o), mark(p, o))
+            push(p, o, to_sib, sib=True)
+    for p in every:
+        a, start, rows, unused = pieces[p]
+        own = part(blocks[a], p)
+        settle(own, own_sem)
+        settle(outs[a].at[pl.ds(0, 31), pl.ds(start, rows)], send_sem.at[p])
+        settle(outs[a].at[pl.ds(0, 16), pl.ds(start, rows)], sib_sem.at[p])
+
+
+def gather_all(blocks, pieces, name):
+    many = len(pieces)
+    return pl.pallas_call(
+        functools.partial(gather_kernel, pieces, len(blocks)),
+        out_shape=[jax.ShapeDtypeStruct((32,) + b.shape, b.dtype) for b in blocks],
+        in_specs=[ANYWHERE] * len(blocks),
+        out_specs=[ANYWHERE] * len(blocks),
+        scratch_shapes=[
+            pltpu.SemaphoreType.DMA((many,)),
+            pltpu.SemaphoreType.DMA((many, 16)),
+            pltpu.SemaphoreType.DMA((many,)),
+            pltpu.SemaphoreType.DMA,
+        ],
+        compiler_params=pltpu.CompilerParams(collective_id=name, has_side_effects=True),
+    )(*blocks)
+
+
+def reduce_pieces(shapes):
+    out = []
+    for a, (rows, cols) in enumerate(shapes):
+        for row in range(0, rows, TILE_R):
+            for col in range(0, cols, TILE_C):
+                out.append((a, row, col, min(TILE_C, cols - col)))
+    return out
+
+
+def reduce_kernel(pieces, count, lag, *refs):
+    grads = (refs[:count], refs[count : 2 * count])
+    outs = refs[2 * count : 3 * count]
+    held, from_one, from_two, from_z, mine = refs[3 * count : 3 * count + 5]
+    sib_recv, sib_send, recv_one, send_one, recv_two, send_two, recv_z, send_z, own_sem = refs[
+        3 * count + 5 :
+    ]
+    y, z, x, c = coords()
+    to_x, to_y, to_sib = (device(y, z, 1 - x, c), device(1 - y, z, x, c), device(y, z, x, 1 - c))
+    zs = [(z + k) % 4 for k in range(4)]
+    greet([to_x, to_y, to_sib] + [device(y, zz, x, c) for zz in zs[1:]])
+    many = len(pieces)
+
+    def source(p, yo, xo, core):
+        a, row, col, cols = pieces[p]
+        return grads[yo][a].at[:, xo, core, pl.ds(row, TILE_R), pl.ds(col, cols)]
+
+    def cut(ref, p):
+        cols = pieces[p][3]
+        return ref if cols == TILE_C else ref.at[..., pl.ds(0, cols)]
+
+    def fetch(p):
+        for yo in range(2):
+            for xo in range(2):
+                pltpu.make_async_copy(
+                    source(p, yo, xo, c), cut(mine.at[p % 2, yo, xo], p), own_sem.at[p % 2]
+                ).start()
+
+    for p in range(many):
+        for yo in range(2):
+            for xo in range(2):
+                send(
+                    source(p, yo, xo, 1 - c),
+                    cut(held.at[p, yo, xo], p),
+                    sib_send.at[p],
+                    sib_recv.at[p],
+                    to_sib,
+                )
+        if p == 0:
+            fetch(0)
+
+    def add(dst, src, p):
+        cols = pl.ds(0, pieces[p][3])
+        dst[:, cols] = (dst[:, cols].astype(jnp.float32) + src[:, cols].astype(jnp.float32)).astype(LOW)
+
+    def two_cores(p):
+        if p + 1 < many:
+            fetch(p + 1)
+        settle(cut(mine.at[p % 2], p), own_sem.at[p % 2])
+        settle(cut(held.at[p], p), sib_recv.at[p])
+
+        def each(i, carry):
+            yo, xo, zo = (i // 8, i // 4 % 2, i % 4)
+            add(held.at[p, yo, xo, zo], mine.at[p % 2, yo, xo, zo], p)
+            return carry
+
+        lax.fori_loop(0, 16, each, 0)
+        if p % 2 == 0:
+            send(cut(held.at[p, 1 - y], p), cut(from_one.at[p], p), send_one.at[p], recv_one.at[p], to_y)
+        else:
+            for yo in range(2):
+                send(
+                    cut(held.at[p, yo, 1 - x], p),
+                    cut(from_one.at[p, yo], p),
+                    send_one.at[p],
+                    recv_one.at[p],
+                    to_x,
+                )
+
+    def first_axis(p):
+        settle(cut(from_one.at[p], p), recv_one.at[p])
+
+        def each(i, carry):
+            if p % 2 == 0:
+                add(held.at[p, y, i // 4, i % 4], from_one.at[p, i // 4, i % 4], p)
+            else:
+                add(held.at[p, i // 4, x, i % 4], from_one.at[p, i // 4, i % 4], p)
+            return carry
+
+        lax.fori_loop(0, 8, each, 0)
+        if p % 2 == 0:
+            src, peer = (held.at[p, y, 1 - x], to_x)
+        else:
+            src, peer = (held.at[p, 1 - y, x], to_y)
+        send(cut(src, p), cut(from_two.at[p], p), send_two.at[p], recv_two.at[p], peer)
+
+    def second_axis(p):
+        settle(cut(from_two.at[p], p), recv_two.at[p])
+
+        def each(i, carry):
+            add(held.at[p, y, x, i], from_two.at[p, i], p)
+            return carry
+
+        lax.fori_loop(0, 4, each, 0)
+        for k in range(1, 4):
+            send(
+                cut(held.at[p, y, x, zs[k]], p),
+                cut(from_z.at[p, 3 - k], p),
+                send_z.at[p],
+                recv_z.at[p],
+                device(y, zs[k], x, c),
+            )
+
+    def along_z(p):
+        settle(cut(from_z.at[p], p), recv_z.at[p])
+        a, row, col, cols = pieces[p]
+        part = pl.ds(0, cols)
+        total = held[p, y, x, z, :, part].astype(jnp.float32)
+        for k in range(3):
+            total = total + from_z[p, k, :, part].astype(jnp.float32)
+        outs[a][pl.ds(row, TILE_R), pl.ds(col, cols)] = total
+
+    for step in range(many + 3 * lag):
+        for k, stage in enumerate((two_cores, first_axis, second_axis, along_z)):
+            if 0 <= step - k * lag < many:
+                stage(step - k * lag)
+    for p in range(many):
+        settle(cut(held.at[p], p), sib_send.at[p])
+        settle(cut(from_one.at[p], p), send_one.at[p])
+        settle(cut(from_two.at[p], p), send_two.at[p])
+        settle(cut(from_z.at[p], p), send_z.at[p])
+
+
+def reduce_all(grads, name, lag):
+    count = len(grads[0])
+    shapes = [(g.shape[0] // 16, g.shape[1]) for g in grads[0]]
+    pieces = reduce_pieces(shapes)
+    many = len(pieces)
+    views = [g.reshape(4, 2, 2, g.shape[0] // 16, g.shape[1]) for layer in grads for g in layer]
+    return pl.pallas_call(
+        functools.partial(reduce_kernel, pieces, count, lag),
+        out_shape=[jax.ShapeDtypeStruct(s, jnp.float32) for s in shapes],
+        in_specs=[ANYWHERE] * len(views),
+        out_specs=[IN_VMEM] * count,
+        scratch_shapes=[
+            pltpu.VMEM((many, 2, 2, 4, TILE_R, TILE_C), LOW),
+            pltpu.VMEM((many, 2, 4, TILE_R, TILE_C), LOW),
+            pltpu.VMEM((many, 4, TILE_R, TILE_C), LOW),
+            pltpu.VMEM((many, 3, TILE_R, TILE_C), LOW),
+            pltpu.VMEM((2, 2, 2, 4, TILE_R, TILE_C), LOW),
+        ]
+        + [pltpu.SemaphoreType.DMA((many,)) for unused in range(8)]
+        + [pltpu.SemaphoreType.DMA((2,))],
+        compiler_params=pltpu.CompilerParams(
+            collective_id=name,
+            has_side_effects=True,
+            vmem_limit_bytes=(12 + 3 * many) * 2**20 if many < 16 else 58 * 2**20,
+        ),
+    )(*views)
+
+
+def exchange_kernel(whole, src, out, send_sem, recv_sem, own_sem):
+    y, f = (lax.axis_index("section"), lax.axis_index("fsdp"))
+    count = 32 if whole else 16
+    me = y * 16 + f if whole else f
+    peers = [(me + k) % count for k in range(1, count)]
+    where = [(p // 16, p % 16) if whole else (y, p) for p in peers]
+    greet(where)
+    for peer in where:
+        send(src, out.at[me], send_sem, recv_sem, peer)
+    own = pltpu.make_async_copy(src, out.at[me], own_sem)
+    own.start()
+    own.wait()
+    settle(out.at[pl.ds(0, count - 1)], send_sem)
+    settle(out.at[pl.ds(0, count - 1)], recv_sem)
+
+
+def exchange(small, name, whole=True):
+    return pl.pallas_call(
+        functools.partial(exchange_kernel, whole),
+        out_shape=jax.ShapeDtypeStruct((32 if whole else 16,) + small.shape, small.dtype),
+        in_specs=[IN_VMEM],
+        out_specs=IN_VMEM,
+        scratch_shapes=[pltpu.SemaphoreType.DMA] * 3,
+        compiler_params=pltpu.CompilerParams(collective_id=name, has_side_effects=True),
+    )(small)
 
 
 def up16(count):
@@ -228,8 +555,12 @@
     ffp = n * rdp
     slots = up16(768 // n)
     sel = spread_matrix(n, r, rp)
-
-    qkv_block = jnp.pad(w_qkv[0].astype(LOW), ((0, rp - r), (0, 0)))
+    fast = (sections, n) == (2, 16)
+    qkv_wide = -(-w_qkv.shape[2] // 128) * 128
+
+    qkv_block = jnp.pad(
+        w_qkv[0].astype(LOW), ((0, rp - r), (0, qkv_wide - w_qkv.shape[2]))
+    )
     out_block = jnp.pad(dense(w_out[0].astype(LOW), sel).astype(LOW), ((0, rp - r), (0, 0)))
     gu_block = w_gu[0].astype(LOW)
     if rdp != rd:
@@ -237,15 +568,24 @@
     gu_block = jnp.pad(gu_block.reshape(r, 2 * ffp), ((0, rp - r), (0, 0)))
     down_block = jnp.pad(dense(w_down[0].astype(LOW), sel).astype(LOW), ((0, rdp - rd), (0, 0)))
     gain_block = jnp.pad(
-        jnp.concatenate([gains[0], final_gain[None]], axis=0).astype(LOW), ((0, 0), (0, rp - r))
+        jnp.concatenate([gains[0], final_gain[None]], axis=0).astype(LOW),
+        ((0, 13), (0, 128 - r)),
     )
 
     ids = token_ids[0]
     owner, rank = lookup_ranks(ids, vshard)
     onehot, wanted = lookup_round(ids, owner, rank, 0, slots, n, vshard)
-    note = jnp.concatenate([wanted, jnp.full((128,), jnp.max(rank) // slots + 1, jnp.int32)])
-    notes = lax.all_gather(note, BOTH, axis=0)
-    turns = jnp.max(notes[:, n * slots])
+    turns_here = jnp.max(rank) // slots + 1
+    own_targets = lax.dynamic_slice_in_dim(targets[0], fsdp_index * NCONT, NCONT).reshape(-1)
+    note = jnp.concatenate(
+        [wanted, jnp.pad(own_targets, (0, 128 - NCONT * SCORED)), jnp.full((128,), turns_here, jnp.int32)]
+    )
+    if fast:
+        notes = exchange(note.reshape(-1, 128), 0).reshape(sections * n, -1)
+    else:
+        notes = lax.all_gather(note, BOTH, axis=0)
+    turns = jnp.max(notes[:, -1])
+    wanted_rows = notes[:, n * slots : n * slots + NCONT * SCORED].reshape(-1)
 
     def asked(all_wanted):
         mine = lax.dynamic_slice_in_dim(all_wanted.reshape(sections, n, n, slots), fsdp_index, 1, 2)
@@ -267,19 +607,17 @@
 
     x0 = lax.while_loop(lambda state: state[0] < turns, fetch_more, (jnp.int32(1), x0))[1]
 
-    def everywhere(block):
-        return lax.all_gather(block, BOTH, axis=0, tiled=True).reshape(
-            sections, n * block.shape[0], block.shape[1]
-        )
-
-    qkv_all = everywhere(qkv_block)
-    out_all = everywhere(out_block)
-    gu_all = everywhere(gu_block)
-    down_all = everywhere(down_block)
-    gain_all = lax.all_gather(gain_block, BOTH, axis=0).reshape(sections, n, 3, rp)
+    blocks = (qkv_block, out_block, gu_block, down_block, gain_block)
+    if fast:
+        gathered = gather_all(blocks, WEIGHT_PIECES, 1)
+    else:
+        gathered = [lax.all_gather(block, BOTH, axis=0) for block in blocks]
+    qkv_all, out_all, gu_all, down_all = [
+        g.reshape(sections, n * g.shape[1], g.shape[2]) for g in gathered[:4]
+    ]
+    gain_all = gathered[4].reshape(sections, n, 16, 128)[:, :, :3, :rp]
     gain_all = jnp.moveaxis(gain_all, 2, 1).reshape(sections, 3, wide).astype(jnp.float32)
     final_all = gain_all[0, 2]
-    wanted_rows = lax.all_gather(targets[0].reshape(-1), "section", axis=0, tiled=True)
 
     everyone = jnp.arange(TOK_MB)
     cosine, sine = rotary_angles(everyone)
@@ -291,7 +629,7 @@
         a = (x * scale_a * gain_all[layer, 0]).astype(LOW)
         qkv = dense(a, qkv_all[layer])
         query = heads_of(qkv[:, :WIDTH], cosine, sine)
-        key, value = keys_values(qkv[:, WIDTH:], cosine, sine)
+        key, value = keys_values(qkv[:, WIDTH : WIDTH + 2 * KVW], cosine, sine)
         attended, probs = attend(query, key, value, allowed)
         attended = dense(attended, sel).astype(LOW)
         mixed = x + dense(attended, out_all[layer])
@@ -311,7 +649,8 @@
     allowed_s = may_attend(place)
     scale_last = inverse_rms(x, width)
     a_last = (x * scale_last * gain_all[last, 0]).astype(LOW)
-    key_last, value_last = keys_values(dense(a_last, qkv_all[last][:, WIDTH:]), cosine, sine)
+    qkv_last = qkv_all[last][:, WIDTH : WIDTH + 2 * KVW]
+    key_last, value_last = keys_values(dense(a_last, qkv_last), cosine, sine)
     a_s = dense(pick, a_last).astype(LOW)
     x_s = jnp.dot(pick32, x, precision=HI)
     query_s = heads_of(dense(a_s, qkv_all[last][:, :WIDTH]), cosine_s, sine_s)
@@ -323,9 +662,13 @@
     branch_s, gate_s, upper_s, hidden_s = mlp(b_s, gu_all[last], down_all[last])
     y_s = mixed_s + branch_s
     scale_y = inverse_rms(y_s, width)
-    head_in = dense_nt((y_s * scale_y * final_all).astype(LOW), sel).astype(LOW)
-
-    rows_all = lax.all_gather(head_in, BOTH, axis=0, tiled=True)
+    head_in = (y_s * scale_y * final_all).astype(LOW)
+
+    if fast:
+        rows_all = gather_all([head_in], [(0, 16 * k, 16, k % 2) for k in range(4)], 2)[0]
+    else:
+        rows_all = lax.all_gather(head_in, BOTH, axis=0)
+    rows_all = dense_nt(rows_all.reshape(-1, wide), sel).astype(LOW)
     own_rows = rows_all.shape[0] // sections
     table_low = table.astype(LOW)
     logits = dense_nt(rows_all, table_low)
@@ -333,7 +676,11 @@
     top_here = jnp.max(logits, axis=1)
     total_here = jnp.sum(jnp.exp(logits - top_here[:, None]), axis=1)
     target_here = jnp.sum(jnp.where(hit, logits, 0.0), axis=1)
-    stats = lax.all_gather(jnp.stack([top_here, total_here, target_here]), "fsdp", axis=0)
+    stats = jnp.stack([top_here, total_here, target_here])
+    if fast:
+        stats = exchange(stats.reshape(-1, 128), 3, whole=False).reshape(n, 3, -1)
+    else:
+        stats = lax.all_gather(stats, "fsdp", axis=0)
     top = jnp.max(stats[:, 0], axis=0)
     total = jnp.sum(stats[:, 1] * jnp.exp(stats[:, 0] - top), axis=0)
     row_logp = jnp.sum(stats[:, 2], axis=0) - top - jnp.log(total)
@@ -350,11 +697,16 @@
     prob = jnp.exp(logits - top[:, None]) * (1.0 / total)[:, None]
     grad_logits = (grad_row[:, None] * (hit.astype(jnp.float32) - prob)).astype(LOW)
     grad_table = dense_t(grad_logits, rows_all)
-    own_grads = lax.dynamic_slice_in_dim(grad_logits, section_index * own_rows, own_rows)
-    grad_head = lax.psum_scatter(
-        dense(own_grads, table_low).astype(LOW), "fsdp", scatter_dimension=0, tiled=True
-    )
-    grad_y, grad_final = norm_back(y_s, scale_y, final_all, dense(grad_head, sel), width)
+    own_vocab = vshard // sections
+    own_grads = lax.dynamic_slice_in_dim(grad_logits, section_index * own_vocab, own_vocab, 1)
+    own_table = lax.dynamic_slice_in_dim(table_low, section_index * own_vocab, own_vocab)
+    grad_rows = dense(dense(own_grads, own_table).astype(LOW), sel).astype(LOW)
+    if fast:
+        halves = [[grad_rows[k * own_rows : (k + 1) * own_rows]] for k in range(sections)]
+        grad_head = reduce_all(halves, 4, 1)[0]
+    else:
+        grad_head = lax.psum_scatter(grad_rows, BOTH, scatter_dimension=0, tiled=True)
+    grad_y, grad_final = norm_back(y_s, scale_y, final_all, grad_head.astype(jnp.float32), width)
 
     grads = [None] * sections
     g_down, g_gu, grad_b = mlp_back(
@@ -370,7 +722,16 @@
     grad_kv = jnp.concatenate(
         [rotate_back(grad_key, cosine, sine).reshape(-1, KVW), grad_value.reshape(-1, KVW)], axis=1
     ).astype(LOW)
-    g_qkv = jnp.concatenate([dense_t(a_s, grad_q), dense_t(a_last, grad_kv)], axis=1)
+    g_qkv = dense_t(
+        jnp.concatenate([a_s, a_last], axis=0),
+        jnp.concatenate(
+            [
+                jnp.pad(grad_q, ((0, 0), (0, qkv_wide - WIDTH))),
+                jnp.pad(grad_kv, ((0, 0), (WIDTH, qkv_wide - WIDTH - 2 * KVW))),
+            ],
+            axis=0,
+        ),
+    )
     grad_a_s = dense_nt(grad_q, qkv_all[last][:, :WIDTH])
     spread_back = lax.dot_general(
         pick32,
@@ -378,7 +739,7 @@
         (((0,), (0,)), ((), ())),
         precision=HI,
     )
-    grad_a = dense_nt(grad_kv, qkv_all[last][:, WIDTH:]) + spread_back[:, :wide]
+    grad_a = dense_nt(grad_kv, qkv_last) + spread_back[:, :wide]
     grad_in, gain_one = norm_back(x, scale_last, gain_all[last, 0], grad_a, width)
     upstream = grad_in + spread_back[:, wide:]
     grads[last] = (g_qkv, g_out, g_gu, g_down, jnp.stack([gain_one, gain_two]))
@@ -401,6 +762,7 @@
                 rotate_back(grad_query, cosine, sine).reshape(-1, WIDTH),
                 rotate_back(grad_key, cosine, sine).reshape(-1, KVW),
                 grad_value.reshape(-1, KVW),
+                jnp.zeros((TOK_MB, qkv_wide - WIDTH - 2 * KVW), jnp.float32),
             ],
             axis=1,
         ).astype(LOW)
@@ -429,22 +791,29 @@
 
     grad_table = lax.while_loop(lambda state: state[0] < turns, give_more, (jnp.int32(1), grad_table))[1]
 
-    def to_owner(which, rows_each):
-        stacked = jnp.concatenate([grads[layer][which].astype(LOW) for layer in range(sections)], axis=0)
-        return lax.psum_scatter(stacked, BOTH, scatter_dimension=0, tiled=True).astype(jnp.float32)
-
-    s_qkv = to_owner(0, rp)[:r]
-    s_out = to_owner(1, rp)[:r].reshape(r, n, rp)[:, :, :r].reshape(r, width)
-    s_gu = to_owner(2, rp)[:r].reshape(r, 2, n, rdp)[:, :, :, :rd].reshape(r, 2 * n * rd)
-    s_down = to_owner(3, rdp)[:rd].reshape(rd, n, rp)[:, :, :r].reshape(rd, width)
-    small = lax.psum(
-        jnp.concatenate([grads[layer][4] for layer in range(sections)] + [grad_final[None]], axis=0), BOTH
-    )
-    small = lax.dynamic_index_in_dim(
-        small.reshape(2 * sections + 1, n, rp), fsdp_index, 1, keepdims=False
-    )[:, :r]
-    s_gains = lax.dynamic_slice_in_dim(small, 2 * section_index, 2)
-    s_final = small[2 * sections]
+    def gain_rows(layer):
+        rows = jnp.concatenate([grads[layer][4], grad_final[None]], axis=0).reshape(3, n, rp)
+        rows = jnp.pad(jnp.moveaxis(rows, 0, 1), ((0, 0), (0, TILE_R - 3), (0, 128 - rp)))
+        return rows.reshape(n * TILE_R, 128)
+
+    outward = [
+        [g.astype(LOW) for g in grads[layer][:4] + (gain_rows(layer),)] for layer in range(sections)
+    ]
+    if fast:
+        summed = reduce_all(outward, 5, 2)
+    else:
+        summed = [
+            lax.psum_scatter(
+                jnp.concatenate(arrays, axis=0), BOTH, scatter_dimension=0, tiled=True
+            ).astype(jnp.float32)
+            for arrays in zip(*outward)
+        ]
+    s_qkv = summed[0][:r, : w_qkv.shape[2]]
+    s_out = summed[1][:r].reshape(r, n, rp)[:, :, :r].reshape(r, width)
+    s_gu = summed[2][:r].reshape(r, 2, n, rdp)[:, :, :, :rd].reshape(r, 2 * n * rd)
+    s_down = summed[3][:rd].reshape(rd, n, rp)[:, :, :r].reshape(rd, width)
+    s_gains = summed[4][:2, :r]
+    s_final = summed[4][2, :r]
 
     grads_all = (
         grad_table,
@@ -494,7 +863,14 @@
             [jnp.zeros((slot_total - 2,), jnp.float32), common_prompt]
         )
 
-    grad_sq = lax.psum(slot_squares(grads_all), BOTH)
+    def everyones(sums, name):
+        if not fast:
+            return lax.psum(sums, BOTH)
+        flat = sums.reshape(-1)
+        small = jnp.broadcast_to(jnp.pad(flat, (0, 128 - flat.shape[0])), (8, 128))
+        return jnp.sum(exchange(small, name)[:, 0], axis=0)[: flat.shape[0]].reshape(sums.shape)
+
+    grad_sq = everyones(slot_squares(grads_all), 6)
     grad_norm = jnp.sqrt(jnp.sum(grad_sq))
     clip = jnp.minimum(1.0, CLIP / grad_norm)
     decays = (DECAY, DECAY, DECAY, DECAY, DECAY, 0.0, 0.0)
@@ -502,8 +878,8 @@
         lamb_parts(w, clip * g, m, v, d)
         for w, g, m, v, d in zip(weights_all, grads_all, firsts, seconds, decays)
     ]
-    squares = lax.psum(
-        jnp.stack([slot_squares(weights_all), slot_squares(tuple((p[2] for p in parts)))]), BOTH
+    squares = everyones(
+        jnp.stack([slot_squares(weights_all), slot_squares(tuple((p[2] for p in parts)))]), 7
     )
     weight_norms, update_norms = (jnp.sqrt(squares[0]), jnp.sqrt(squares[1]))
     trust_ratio = weight_norms / update_norms

time: 1750 us -> 1160 us (0.66)
  waiting for transfers between devices: 842 us -> 8.89 us
  Pallas kernels: 0 us -> 534 us
  blocking collectives: 303 us -> 0 us
  other arithmetic: 211 us -> 170 us
  local copies, waits for them, and re-layouts: 99.6 us -> 139 us
    pallas_call x0 -> x8, Pallas kernels: none -> 534 us  [the longest x2 268 us: reduce_all(): pl.pallas_call(functools.partial(reduce_kernel, pieces, count, lag), out_...]
    reduce_scatter x4 -> x0, waiting for transfers between devices: 431 us -> none  [the longest x3 373 us: to_owner(): lax.psum_scatter(stacked, BOTH, scatter_dimension=0, tiled=True)]
    all_gather x5 -> x0, waiting for transfers between devices: 229 us -> none  [the longest x4 173 us: everywhere(): lax.all_gather(block, BOTH, axis=0, tiled=True)]
    unnamed x12 -> x1, waiting for transfers between devices: 145 us -> 0.02 us
    all_gather x4 -> x0, blocking collectives: 138 us -> none  [the longest x1 68.6 us: shards(): lax.all_gather(gain_block, BOTH, axis=0).reshape(sections, n, 3, rp)]
    psum x3 -> x0, blocking collectives: 125 us -> none  [the longest x1 45.3 us: shards(): grad_sq = lax.psum(slot_squares(grads_all), BOTH)]
    concatenate x4 -> x2, other arithmetic: 49.6 us -> 1.62 us  [the longest x1 1.02 us: shards(): jnp.concatenate([rotate_back(grad_key, cosine, sine).reshape(-1, KVW), gr...]
    slice x0 -> x6, local copies, waits for them, and re-layouts: none -> 41.9 us  [the longest x2 26.9 us: shards(): branch_s, gate_s, upper_s, hidden_s = mlp(b_s, gu_all[last], down_all[last])]
  transfers between devices with their start and end apart: 12 -> 3, of which waited for: 9 -> 2; matrix products, arithmetic and copies ran while one was open for 11% -> 7% of each run, Pallas kernels for 0% -> 20%
where the time goes in v2:
time: 1160 us; the launch traced here: 1150 us
  Pallas kernels  534 us (46%)
  matrix products  253 us (22%)
  other arithmetic  170 us (15%)
  local copies, waits for them, and re-layouts  139 us (12%)
  between operations  24.6 us (2%)
  starting transfers between devices  19.4 us (2%)
    pallas_call x2, Pallas kernels, reduce_all(): pl.pallas_call(functools.partial(reduce_kernel, pieces, count, lag), out_...  268 us
    pallas_call x2, Pallas kernels, gather_all(): pl.pallas_call(functools.partial(gather_kernel, pieces, len(blocks)), out...  222 us
    dot_general x12, matrix products, dense_nt(): lax.dot_general(left, right, (((1,), (1,)), ((), ())), preferred_element_...  74.9 us
    dot_general x17, matrix products, dense(): return jnp.dot(left, right, preferred_element_type=jnp.float32)  66.9 us
    dot_general x10, matrix products, dense_t(): lax.dot_general(left, right, (((0,), (0,)), ((), ())), preferred_element_...  61.7 us
    pallas_call x4, Pallas kernels, exchange(): pl.pallas_call(functools.partial(exchange_kernel, whole), out_shape=jax.S...  43.8 us
    unnamed x394, local copies, waits for them, and re-layouts  40.8 us
    reduce_sum x2, other arithmetic, slot_squares(): jnp.sum(arrays[0] ** 2)  35.5 us
  transfers between devices with their start and end apart: 3, of which 2 were waited for; matrix products, arithmetic and copies ran while one was open for 7% of the time, Pallas kernels for 20%

profile of v2, /device:TPU:0, one launch (start us, length us, event | category | flops | bytes accessed | tf_op | source)
XLA Modules:
  0.0 1150.1 jit_solution(9957951828914921558)
XLA Ops:
  14.7 12.2 %shard_map.464 = s32[32,8,128]{2,1,0:T(8,128)} custom-call(s32[8,128]{1,0:T(8,128)} %fusion.201.src), custom_call_target="tpu_custom_call" | custom-call | tf_op jit(solution)/shard_map/pallas_call | solution.py:352
  35.7 7.8 convert_element_type.456
  43.6 10.0 copy.233
  65.7 190.9 %shard_map.465 = (bf16[32,64,1664]{2,1,0:T(8,128)(2,1)}, bf16[32,64,1024]{2,1,0:T(8,128)(2,1)}, bf16[32,64,5120]{2,1,0:T(8,128)(2,1)}, bf16[32,160,1024]{2,1,0:T(8,128)(2,1)}, bf16[32,16,128]{2,1,0:T(8,128)(2,1)}) custom-call(bf16[64,1664]{1,0:T(8,128)(2,1)} %pad.49.refs_0_, bf16[64,1024]{1,0:T(8,128)(2,1)} %pad.50.refs_1_, bf16[64,5120]{1,0:T(8,128)(2,1)} %pad.51.refs_2_, ...), custom_call_target="tpu_custom_call" | custom-call | tf_op jit(solution)/shard_map/pallas_call | solution.py:160
  258.2 5.0 fusion.270
  263.2 10.0 fusion.267
  273.8 7.4 gather_fusion.1
  282.7 14.3 %all-to-all-start.2 = ((bf16[16,48,960]{2,1,0:T(8,128)(2,1)}), bf16[16,48,960]{2,1,0:T(8,128)(2,1)S(1)}, u32[]{:S(2)}, u32[]{:S(2)}) async-start(bf16[16,48,960]{2,1,0:T(8,128)(2,1)} %select_convert_fusion.1), calls=%async_computation.2 | async-start | bytes 3145728 | tf_op jit(solution)/shard_map/all_to_all | solution.py:597
  297.7 6.3 fusion.268
  304.0 16.9 %fusion.266 = (bf16[16,64,5120]{2,1,0:T(8,128)(2,1)}, bf16[16,64,5120]{2,1,0:T(8,128)(2,1)}) fusion(bf16[32,64,5120]{2,1,0:T(8,128)(2,1)} %get-tuple-element.359), kind=kLoop, calls=%fused_computation.530 | loop fusion | bytes 41943040 | tf_op jit(solution)/shard_map/slice | solution.py:662
  320.9 8.1 all-to-all-done.2
  335.8 4.7 fusion.251
  346.9 9.5 fusion.276
  356.4 7.2 fusion.86
  369.0 7.4 fusion.252
  405.4 6.1 fusion.250
  413.6 30.8 %shard_map.466 = bf16[32,64,1024]{2,1,0:T(8,128)(2,1)} custom-call(bf16[64,1024]{1,0:T(8,128)(2,1)} %multiply_convert_fusion.10.refs_0_), custom_call_target="tpu_custom_call" | custom-call | tf_op jit(solution)/shard_map/pallas_call | solution.py:160
  444.5 8.3 fusion.55
  452.8 18.1 %fusion.278 = (f32[2048]{0:T(1024)S(1)}, f32[2048,3072]{1,0:T(8,128)S(1)}) fusion(bf16[2048,960]{0,1:T(8,128)(2,1)} %fusion.55, bf16[3072,960]{0,1:T(8,128)(2,1)} %convert_element_type.456), kind=kOutput, calls=%fused_computation.542 | convolution fusion | flops 12085884928 | bytes 35004416 | tf_op jit(solution)/shard_map/dot_general | solution.py:377
  470.9 7.6 exponential_reduce_fusion
  479.9 13.0 %shard_map.467 = f32[16,48,128]{2,1,0:T(8,128)} custom-call(f32[48,128]{1,0:T(8,128)} %reshape.1066.src), custom_call_target="tpu_custom_call" | custom-call | tf_op jit(solution)/shard_map/pallas_call | solution.py:352
  498.3 18.1 %multiply_convert_fusion = bf16[2048,3072]{1,0:T(8,128)(2,1)} fusion(f32[2048,3072]{1,0:T(8,128)} %copy-done.2, f32[2048]{0:T(1024)S(1)} %get-tuple-element.783, f32[2048]{0:T(1024)S(1)} %get-tuple-element.655, f32[2048]{0:T(1024)S(1)} %mul.1556, s32[2048]{0:T(1024)S(1)} %copy-done.112), kind=kLoop, calls=%fused_computation.44 | loop fusion | flops 44040192 | bytes 37781504 | tf_op jit(solution)/shard_map/convert_element_type | solution.py:698
  516.4 15.4 %fusion.52 = bf16[2048,1024]{1,0:T(8,128)(2,1)} fusion(s32[960]{0:T(1024)S(1)} %copy-done.145, bf16[2048,3072]{1,0:T(8,128)(2,1)} %multiply_convert_fusion, s32[]{:T(128)S(6)} %select_n.459, bf16[3072,960]{0,1:T(8,128)(2,1)} %convert_element_type.456), kind=kOutput, calls=%fused_computation.104 | convolution fusion | flops 10071375872 | bytes 13439744 | tf_op jit(solution)/shard_map/dot_general | solution.py:367
  534.7 40.6 %shard_map.468 = f32[64,1024]{1,0:T(8,128)S(1)} custom-call(bf16[4,2,2,64,1024]{4,3,2,1,0:T(8,128)(2,1)S(1)} %bitcast.367, bf16[4,2,2,64,1024]{4,3,2,1,0:T(8,128)(2,1)S(1)} %bitcast.366), custom_call_target="tpu_custom_call" | custom-call | tf_op jit(solution)/shard_map/pallas_call | solution.py:313
  576.1 4.4 multiply_convert_fusion.8
  602.0 4.2 multiply_reduce_fusion.4
  607.7 9.3 multiply_convert_fusion.2
  617.1 11.0 multiply_reduce_fusion.5
  630.0 5.6 fusion.91
  635.6 8.3 fusion.101
  645.3 6.7 fusion.24
  652.0 7.7 fusion.26
  677.4 5.1 all-to-all-start.3
  697.9 5.6 convolution_convert_fusion.5
  703.5 4.5 convolution_convert_fusion.6
  708.0 5.7 convolution_convert_fusion.1
  714.6 6.5 convolution_convert_fusion.3
  721.1 8.9 convolution_convert_fusion.2
  730.1 227.6 %shard_map.469 = (f32[64,1664]{1,0:T(8,128)}, f32[64,1024]{1,0:T(8,128)}, f32[64,5120]{1,0:T(8,128)}, f32[160,1024]{1,0:T(8,128)}, f32[32,128]{1,0:T(8,128)}) custom-call(bf16[4,2,2,64,1664]{4,3,2,1,0:T(8,128)(2,1)} %bitcast.409, bf16[4,2,2,64,1024]{4,3,2,1,0:T(8,128)(2,1)} %bitcast.415, bf16[4,2,2,64,5120]{4,3,2,1,0:T(8,128)(2,1)} %bitcast.389, ...), custom_call_target="tpu_custom_call" | custom-call | tf_op jit(solution)/shard_map/pallas_call | solution.py:313
  971.0 14.9 %fusion.23 = f32[3072,960]{0,1:T(8,128)} fusion(bf16[1536,960]{1,0:T(8,128)(2,1)} %bitcast.479, s32[1536]{0:T(1024)S(1)} %copy-done.131), kind=kOutput, calls=%fused_computation.49 | convolution fusion | flops 9064415232 | bytes 14751744 | tf_op jit(solution)/shard_map/dot_general | solution.py:367
  986.0 19.6 %convolution_add_fusion = f32[3072,960]{0,1:T(8,128)} fusion(f32[3072,960]{0,1:T(8,128)} %fusion.23, bf16[2048,960]{0,1:T(8,128)(2,1)S(1)} %copy-done.171, bf16[2048,3072]{1,0:T(8,128)(2,1)} %multiply_convert_fusion), kind=kOutput, calls=%fused_computation.75 | convolution fusion | flops 12082544640 | bytes 40108032 | tf_op jit(solution)/shard_map/dot_general | solution.py:371
  1006.4 8.1 multiply_reduce_fusion.2
  1016.6 8.7 shard_map.470
  1039.6 4.8 multiply_reduce_fusion.12
  1053.6 4.0 stack.151
  1057.6 27.4 %multiply_reduce_fusion.1 = (f32[]{:T(128)}, f32[]{:T(128)}, f32[3072,960]{0,1:T(8,128)}, f32[3072,960]{0,1:T(8,128)}) fusion(f32[3072,960]{0,1:T(8,128)} %param.33, f32[3072,960]{0,1:T(8,128)} %get-tuple-element.366, f32[]{:T(128)S(6)} %min.3, f32[3072,960]{0,1:T(8,128)} %param.40, f32[3072,960]{0,1:T(8,128)} %param.47), kind=kLoop, calls=%fused_computation.64 | loop fusion | flops 53084160 | bytes 70778896 | tf_op jit(solution)/shard_map/reduce_sum | solution.py:861
  1088.6 9.9 shard_map.471
  1124.5 17.5 %fusion.257 = (bf16[3072,960]{0,1:T(8,128)(2,1)}, f32[3072,960]{0,1:T(8,128)}) fusion(f32[3072,960]{0,1:T(8,128)} %param.33, f32[3072,960]{0,1:T(8,128)} %get-tuple-element.715, f32[3072,960]{0,1:T(8,128)S(1)} %copy-done.3, f32[]{:T(128)} %bitcast.143), kind=kLoop, calls=%fused_computation.529 | loop fusion | flops 26542080 | bytes 53084164 | tf_op jit(solution)/shard_map/convert_element_type | solution.py:901
  (618 shorter events, 213.6 us)
Async XLA Ops:
  7.2 25.1 %copy-start.4 = (f32[1,60,5120]{2,0,1:T(1,128)S(1)}, f32[1,60,5120]{2,0,1:T(1,128)}, u32[]{:S(2)}) copy-start(f32[1,60,5120]{2,0,1:T(1,128)} %param.36) | copy-start | bytes 3686404
  11.7 317.3 %copy-start.132 = (s32[512]{0:T(512)}, s32[512]{0:T(512)S(1)}, u32[]{:S(2)}) copy-start(s32[512]{0:T(512)S(1)} %get-tuple-element.798) | copy-start | bytes 6148
  43.6 10.1 copy-start.161
  43.6 10.1 copy-start.127
  43.6 10.3 copy-start.152
  43.6 11.0 copy-start.156
  43.6 16.6 %copy-start.40 = (f32[1,60,960]{2,0,1:T(1,128)S(1)}, f32[1,60,960]{2,0,1:T(1,128)}, u32[]{:S(2)}) copy-start(f32[1,60,960]{2,0,1:T(1,128)} %param.35) | copy-start | bytes 691204
  53.9 332.3 %copy-start.125 = (s32[64]{0:T(128)}, s32[64]{0:T(128)S(1)}, u32[]{:S(2)}) copy-start(s32[64]{0:T(128)S(1)} %get-tuple-element.738) | copy-start | bytes 772
  258.2 77.6 %copy-start.141 = (f32[1,1,1024]{2,0,1:T(1,128)}, f32[1,1,1024]{2,0,1:T(1,128)S(1)}, u32[]{:S(2)}) copy-start(f32[1,1,1024]{2,0,1:T(1,128)S(1)} %get-tuple-element.782) | copy-start | bytes 12292
  258.2 110.3 %copy-start.122 = (f32[1,1,1024]{2,0,1:T(1,128)}, f32[1,1,1024]{2,0,1:T(1,128)S(1)}, u32[]{:S(2)}) copy-start(f32[1,1,1024]{2,0,1:T(1,128)S(1)} %get-tuple-element.781) | copy-start | bytes 12292
  258.2 127.8 %copy-start.116 = (f32[1,1,1024]{2,0,1:T(1,128)}, f32[1,1,1024]{2,0,1:T(1,128)S(1)}, u32[]{:S(2)}) copy-start(f32[1,1,1024]{2,0,1:T(1,128)S(1)} %get-tuple-element.780) | copy-start | bytes 12292
  282.7 46.3 %all-to-all-start.2 = ((bf16[16,48,960]{2,1,0:T(8,128)(2,1)}), bf16[16,48,960]{2,1,0:T(8,128)(2,1)S(1)}, u32[]{:S(2)}, u32[]{:S(2)}) async-start(bf16[16,48,960]{2,1,0:T(8,128)(2,1)} %select_convert_fusion.1), calls=%async_computation.2 | async-start | bytes 3145728 | tf_op jit(solution)/shard_map/all_to_all | solution.py:597
  333.4 30.3 %copy-start.144 = (s32[960]{0:T(1024)}, s32[960]{0:T(1024)S(1)}, u32[]{:S(2)}) copy-start(s32[960]{0:T(1024)S(1)} %get-tuple-element.1064) | copy-start | bytes 11524
  346.5 9.9 copy-start.84
  346.5 9.9 copy-start.86
  365.2 15.5 %slice-start.15 = ((s8[5242880]{0:T(1024)(128)(4,1)}), s8[4194304]{0:T(1024)(128)(4,1)S(1)}, s32[]{:S(2)}) async-start(s8[5242880]{0:T(1024)(128)(4,1)} %bitcast.401), calls=%async_computation.21 | async-start | bytes 8388608
  369.0 11.7 %slice-start.16 = ((s8[5242880]{0:T(1024)(128)(4,1)}), s8[1048576]{0:T(1024)(128)(4,1)S(1)}, s32[]{:S(2)}) async-start(s8[5242880]{0:T(1024)(128)(4,1)} %bitcast.401), calls=%async_computation.22 | async-start | bytes 2097152
  401.5 10.1 slice-start.3
  405.3 179.2 %copy-start.118 = (f32[64]{0:T(128)}, f32[64]{0:T(128)S(1)}, u32[]{:S(2)}) copy-start(f32[64]{0:T(128)S(1)} %get-tuple-element.815) | copy-start | bytes 772
  452.8 18.1 %copy-start.112 = (s32[2048]{0:T(1024)S(1)}, s32[2048]{0:T(1024)}, u32[]{:S(2)}) copy-start(s32[2048]{0:T(1024)} %sub.372) | copy-start | bytes 24580
  479.2 18.0 %copy-start.139 = (s32[32]{0:T(128)S(1)}, s32[32]{0:T(128)}, u32[]{:S(2)}) copy-start(s32[32]{0:T(128)} %get-tuple-element.656) | copy-start | bytes 388
  479.2 18.0 %copy-start.140 = (s32[32]{0:T(128)S(1)}, s32[32]{0:T(128)}, u32[]{:S(2)}) copy-start(s32[32]{0:T(128)} %get-tuple-element.657) | copy-start | bytes 388
  531.8 48.8 %slice-start = ((s8[10485760]{0:T(1024)(128)(4,1)}), s8[4194304]{0:T(1024)(128)(4,1)S(1)}, s32[]{:S(2)}) async-start(s8[10485760]{0:T(1024)(128)(4,1)} %bitcast.371), calls=%async_computation.6 | async-start | bytes 8388608
  531.8 48.8 %slice-start.1 = ((s8[10485760]{0:T(1024)(128)(4,1)}), s8[4194304]{0:T(1024)(128)(4,1)S(1)}, s32[]{:S(2)}) async-start(s8[10485760]{0:T(1024)(128)(4,1)} %bitcast.371), calls=%async_computation.7 | async-start | bytes 8388608
  534.7 41.4 %copy-start.16 = (f32[64,5120]{1,0:T(8,128)S(1)}, f32[64,5120]{1,0:T(8,128)}, u32[]{:S(2)}) copy-start(f32[64,5120]{1,0:T(8,128)} %copy-done.15) | copy-start | bytes 3932164
  607.7 20.4 %copy-start.11 = (f32[512,1024]{1,0:T(8,128)}, f32[512,1024]{1,0:T(8,128)S(1)}, u32[]{:S(2)}) copy-start(f32[512,1024]{1,0:T(8,128)S(1)} %slice_add_fusion) | copy-start | bytes 6291460
  617.1 11.1 copy-start.166
  617.1 11.1 copy-start.137
  630.0 14.0 %slice-start.5 = ((s8[15728640]{0:T(1024)(128)(4,1)}), s8[3145728]{0:T(1024)(128)(4,1)S(1)}, s32[]{:S(2)}) async-start(s8[15728640]{0:T(1024)(128)(4,1)} %bitcast.381), calls=%async_computation.11 | async-start | bytes 6291456
  645.3 19.0 %copy-start.163 = (bf16[5,64,512]{2,1,0:T(8,128)(2,1)}, bf16[5,64,512]{2,1,0:T(8,128)(2,1)S(1)}, u32[]{:S(2)}) copy-start(bf16[5,64,512]{2,1,0:T(8,128)(2,1)S(1)} %fusion.101) | copy-start | bytes 983044
  677.3 10.8 copy-start.64
  677.4 37.1 %all-to-all-start.3 = ((bf16[16,48,960]{2,1,0:T(8,128)(2,1)}), bf16[16,48,960]{2,1,0:T(8,128)(2,1)}, u32[]{:S(2)}, u32[]{:S(2)}) async-start(bf16[16,48,960]{2,1,0:T(8,128)(2,1)} %bitcast.112), calls=%async_computation.3 | async-start | bytes 3145728 | tf_op jit(solution)/shard_map/all_to_all | solution.py:780
  682.5 288.5 %all-gather.16.cloned.1.call-start = ((), (), s32[]{:S(2)}) async-start(), calls=%async_computation.4 | async-start | bytes 4718592 | tf_op jit(solution)/shard_map/all_gather | solution.py:781
  958.9 11.5 copy-start.159
  958.9 12.1 %copy-start.131 = (s32[1536]{0:T(1024)S(1)}, s32[1536]{0:T(1024)}, u32[]{:S(2)}) copy-start(s32[1536]{0:T(1024)} %eq.410) | copy-start | bytes 18436
  960.6 25.4 %copy-start.6 = (f32[160,16,64]{2,1,0:T(8,128)}, f32[160,16,64]{2,1,0:T(8,128)S(1)}, u32[]{:S(2)}) copy-start(f32[160,16,64]{2,1,0:T(8,128)S(1)} %reshape.1088) | copy-start | bytes 1966084
  971.0 14.9 %copy-start.171 = (bf16[2048,960]{0,1:T(8,128)(2,1)S(1)}, bf16[2048,960]{0,1:T(8,128)(2,1)}, u32[]{:S(2)}) copy-start(bf16[2048,960]{0,1:T(8,128)(2,1)} %fusion.55) | copy-start | bytes 11796484
  985.9 19.6 %copy-start.92 = (s32[1,512]{1,0:T(1,128)S(1)}, s32[1,512]{1,0:T(1,128)}, u32[]{:S(2)}) copy-start(s32[1,512]{1,0:T(1,128)} %param.29) | copy-start | bytes 6148
  985.9 19.6 %copy-start.101 = (s32[512]{0:T(512)S(1)}, s32[512]{0:T(512)}, u32[]{:S(2)}) copy-start(s32[512]{0:T(512)} %copy-done.100) | copy-start | bytes 6148
  985.9 19.6 %copy-start.103 = (s32[512]{0:T(512)S(1)}, s32[512]{0:T(512)}, u32[]{:S(2)}) copy-start(s32[512]{0:T(512)} %copy-done.102) | copy-start | bytes 6148
  985.9 19.6 %copy-start.105 = (s32[512,1]{0,1:T(1,128)S(1)}, s32[512,1]{0,1:T(1,128)}, u32[]{:S(2)}) copy-start(s32[512,1]{0,1:T(1,128)} %copy-done.104) | copy-start | bytes 6148
  1006.4 21.2 %copy-start.7 = (f32[160,16,64]{2,1,0:T(8,128)S(1)}, f32[160,16,64]{2,1,0:T(8,128)}, u32[]{:S(2)}) copy-start(f32[160,16,64]{2,1,0:T(8,128)} %copy-done.6) | copy-start | bytes 1966084
  1014.5 13.2 %copy-start.22 = (f32[60,16,64]{2,1,0:T(8,128)S(1)}, f32[60,16,64]{2,1,0:T(8,128)}, u32[]{:S(2)}) copy-start(f32[60,16,64]{2,1,0:T(8,128)} %copy-done.21) | copy-start | bytes 737284
  1028.7 10.9 copy-start.5
  1047.6 10.0 copy-start.160
  1098.5 10.4 copy-start.18
  1108.9 14.2 %copy-start.33 = (f32[1,160,960]{2,1,0:T(8,128)S(1)}, f32[1,160,960]{2,1,0:T(8,128)}, u32[]{:S(2)}) copy-start(f32[1,160,960]{2,1,0:T(8,128)} %get-tuple-element.736) | copy-start | bytes 1843204
  1124.5 17.5 %copy-start.1 = (s32[1,32,32]{2,1,0:T(8,128)S(1)}, s32[1,32,32]{2,1,0:T(8,128)}, u32[]{:S(2)}) copy-start(s32[1,32,32]{2,1,0:T(8,128)} %param.31) | copy-start | bytes 12292
  (145 other events, 749.5 us)
Sparse Core Ops, SparseCore 0:
  714.6 69.8 all-gather.15

commit v3 on v2

--- a/solution.py
+++ b/solution.py
@@ -84,19 +84,30 @@
     pltpu.make_async_copy(ref, ref, sem).wait()
 
 
-def gather_kernel(pieces, count, *refs):
-    blocks, outs = (refs[:count], refs[count : 2 * count])
-    send_sem, recv_sem, sib_sem, own_sem = refs[2 * count :]
-    y, z, x, c = coords()
+def gather_kernel(pieces, count, carried, *refs):
+    y, f = (lax.axis_index("section"), lax.axis_index("fsdp"))
+    z, x, c = coords()[1:]
+    in_line = [((z + k) % 4) * 4 + x * 2 + c for k in range(1, 4)]
+    near = [f + 2 - 4 * x, f + 1 - 2 * c]
+    away = [(f + k) % 16 for k in range(1, 16)] if carried else in_line + near
+    greet([device(1 - y, z, x, c)] + [(y, peer) for peer in away])
+    for section in range(2):
+        pl.when(y == section)(functools.partial(gather_section, section, pieces, count, carried, *refs))
+
+
+def gather_section(y, pieces, count, carried, *refs):
+    given = count + carried
+    blocks, outs = (refs[:count], refs[given : given + 2 * count])
+    send_sem, recv_sem, sib_sem, own_sem, carry_sem = refs[given + 2 * count + carried :]
+    z, x, c = coords()[1:]
     to_x, to_y, to_sib = (device(y, z, 1 - x, c), device(1 - y, z, x, c), device(y, z, x, 1 - c))
     zs = [(z + k) % 4 for k in range(4)]
-    greet([to_x, to_y, to_sib] + [device(y, zz, x, c) for zz in zs[1:]])
 
     def part(ref, p):
         return ref.at[pl.ds(pieces[p][1], pieces[p][2])]
 
     def there(p, o):
-        return part(outs[pieces[p][0]].at[o[0] * 16 + o[1] * 4 + o[2] * 2 + c], p)
+        return part(outs[o[0] * count + pieces[p][0]].at[o[1] * 4 + o[2] * 2 + c], p)
 
     def mark(p, o):
         return recv_sem.at[p, o[0] * 8 + o[1] * 2 + o[2]]
@@ -114,6 +125,13 @@
             push(p, me, device(y, zz, x, c), own=True)
         push(p, me, to_sib, own=True, sib=True)
         pltpu.make_async_copy(part(blocks[pieces[p][0]], p), there(p, me), own_sem).start()
+    if carried:
+        rows, got = (refs[count], refs[given + 2 * count])
+        f = lax.axis_index("fsdp")
+        for k in range(1, 16):
+            peer = (f + k) % 16
+            send(rows.at[peer], got.at[f], carry_sem.at[0], carry_sem.at[1], (y, peer))
+        pltpu.make_async_copy(rows.at[f], got.at[f], carry_sem.at[2]).start()
 
     def from_x(p, zz):
         o = (y, zz, 1 - x)
@@ -148,28 +166,36 @@
             settle(there(p, o), mark(p, o))
             push(p, o, to_sib, sib=True)
     for p in every:
-        a, start, rows, unused = pieces[p]
-        own = part(blocks[a], p)
-        settle(own, own_sem)
-        settle(outs[a].at[pl.ds(0, 31), pl.ds(start, rows)], send_sem.at[p])
-        settle(outs[a].at[pl.ds(0, 16), pl.ds(start, rows)], sib_sem.at[p])
-
-
-def gather_all(blocks, pieces, name):
+        a, start, rows_each, unused = pieces[p]
+        settle(part(blocks[a], p), own_sem)
+        for times in (16, 15):
+            settle(outs[a].at[pl.ds(0, times), pl.ds(start, rows_each)], send_sem.at[p])
+        settle(outs[a].at[pl.ds(0, 16), pl.ds(start, rows_each)], sib_sem.at[p])
+    if carried:
+        settle(rows.at[pl.ds(0, 15)], carry_sem.at[0])
+        settle(rows.at[pl.ds(0, 15)], carry_sem.at[1])
+        settle(rows.at[0], carry_sem.at[2])
+
+
+def gather_all(blocks, pieces, name, rows=None):
     many = len(pieces)
+    extra = [] if rows is None else [rows]
+    shapes = [jax.ShapeDtypeStruct((16,) + b.shape, b.dtype) for b in blocks] * 2
+    shapes += [jax.ShapeDtypeStruct(e.shape, e.dtype) for e in extra]
     return pl.pallas_call(
-        functools.partial(gather_kernel, pieces, len(blocks)),
-        out_shape=[jax.ShapeDtypeStruct((32,) + b.shape, b.dtype) for b in blocks],
-        in_specs=[ANYWHERE] * len(blocks),
-        out_specs=[ANYWHERE] * len(blocks),
+        functools.partial(gather_kernel, pieces, len(blocks), len(extra)),
+        out_shape=shapes,
+        in_specs=[ANYWHERE] * (len(blocks) + len(extra)),
+        out_specs=[ANYWHERE] * len(shapes),
         scratch_shapes=[
             pltpu.SemaphoreType.DMA((many,)),
             pltpu.SemaphoreType.DMA((many, 16)),
             pltpu.SemaphoreType.DMA((many,)),
             pltpu.SemaphoreType.DMA,
+            pltpu.SemaphoreType.DMA((3,)),
         ],
         compiler_params=pltpu.CompilerParams(collective_id=name, has_side_effects=True),
-    )(*blocks)
+    )(*blocks, *extra)
 
 
 def reduce_pieces(shapes):
@@ -181,18 +207,21 @@
     return out
 
 
-def reduce_kernel(pieces, count, lag, *refs):
+def reduce_kernel(pieces, count, carried, lag, *refs):
     grads = (refs[:count], refs[count : 2 * count])
-    outs = refs[2 * count : 3 * count]
-    held, from_one, from_two, from_z, mine = refs[3 * count : 3 * count + 5]
-    sib_recv, sib_send, recv_one, send_one, recv_two, send_two, recv_z, send_z, own_sem = refs[
-        3 * count + 5 :
+    outs = refs[2 * count + carried : 3 * count + carried]
+    held, from_one, from_two, from_z, mine = refs[3 * count + 2 * carried : 3 * count + 2 * carried + 5]
+    sib_recv, sib_send, recv_one, send_one, recv_two, send_two, recv_z, send_z, own_sem, carry_sem = refs[
+        3 * count + 2 * carried + 5 :
     ]
     y, z, x, c = coords()
     to_x, to_y, to_sib = (device(y, z, 1 - x, c), device(1 - y, z, x, c), device(y, z, x, 1 - c))
     zs = [(z + k) % 4 for k in range(4)]
-    greet([to_x, to_y, to_sib] + [device(y, zz, x, c) for zz in zs[1:]])
     many = len(pieces)
+    f = lax.axis_index("fsdp")
+    alike = [(y, (f + k) % 16) for k in range(1, 16)]
+    near = [to_x, to_sib] + [device(y, zz, x, c) for zz in zs[1:]]
+    greet([to_y] + (alike if carried else near))
 
     def source(p, yo, xo, core):
         a, row, col, cols = pieces[p]
@@ -221,6 +250,20 @@
                 )
         if p == 0:
             fetch(0)
+    if carried:
+        rows, got = (refs[2 * count], refs[3 * count + carried])
+        for peer in alike:
+            send(rows.at[peer[1]], got.at[y * 16 + f], carry_sem.at[0], carry_sem.at[1], peer)
+        pltpu.make_async_copy(rows.at[f], got.at[y * 16 + f], carry_sem.at[2]).start()
+
+    def pass_on():
+        settle(rows.at[pl.ds(0, 15)], carry_sem.at[1])
+        settle(rows.at[0], carry_sem.at[2])
+        ours = got.at[pl.ds(y * 16, 16)]
+        send(ours, ours, carry_sem.at[3], carry_sem.at[4], to_y)
+
+    def y_first(p):
+        return p % 2 == 0
 
     def add(dst, src, p):
         cols = pl.ds(0, pieces[p][3])
@@ -238,7 +281,7 @@
             return carry
 
         lax.fori_loop(0, 16, each, 0)
-        if p % 2 == 0:
+        if y_first(p):
             send(cut(held.at[p, 1 - y], p), cut(from_one.at[p], p), send_one.at[p], recv_one.at[p], to_y)
         else:
             for yo in range(2):
@@ -254,14 +297,14 @@
         settle(cut(from_one.at[p], p), recv_one.at[p])
 
         def each(i, carry):
-            if p % 2 == 0:
+            if y_first(p):
                 add(held.at[p, y, i // 4, i % 4], from_one.at[p, i // 4, i % 4], p)
             else:
                 add(held.at[p, i // 4, x, i % 4], from_one.at[p, i // 4, i % 4], p)
             return carry
 
         lax.fori_loop(0, 8, each, 0)
-        if p % 2 == 0:
+        if y_first(p):
             src, peer = (held.at[p, y, 1 - x], to_x)
         else:
             src, peer = (held.at[p, 1 - y, x], to_y)
@@ -294,6 +337,8 @@
         outs[a][pl.ds(row, TILE_R), pl.ds(col, cols)] = total
 
     for step in range(many + 3 * lag):
+        if carried and step == many // 2:
+            pass_on()
         for k, stage in enumerate((two_cores, first_axis, second_axis, along_z)):
             if 0 <= step - k * lag < many:
                 stage(step - k * lag)
@@ -302,19 +347,25 @@
         settle(cut(from_one.at[p], p), send_one.at[p])
         settle(cut(from_two.at[p], p), send_two.at[p])
         settle(cut(from_z.at[p], p), send_z.at[p])
-
-
-def reduce_all(grads, name, lag):
+    if carried:
+        settle(rows.at[pl.ds(0, 15)], carry_sem.at[0])
+        settle(rows, carry_sem.at[3])
+        settle(rows, carry_sem.at[4])
+
+
+def reduce_all(grads, name, lag, rows=None):
     count = len(grads[0])
     shapes = [(g.shape[0] // 16, g.shape[1]) for g in grads[0]]
     pieces = reduce_pieces(shapes)
     many = len(pieces)
     views = [g.reshape(4, 2, 2, g.shape[0] // 16, g.shape[1]) for layer in grads for g in layer]
+    extra = [] if rows is None else [rows]
     return pl.pallas_call(
-        functools.partial(reduce_kernel, pieces, count, lag),
-        out_shape=[jax.ShapeDtypeStruct(s, jnp.float32) for s in shapes],
-        in_specs=[ANYWHERE] * len(views),
-        out_specs=[IN_VMEM] * count,
+        functools.partial(reduce_kernel, pieces, count, len(extra), lag),
+        out_shape=[jax.ShapeDtypeStruct(s, jnp.float32) for s in shapes]
+        + [jax.ShapeDtypeStruct((32,) + e.shape[1:], e.dtype) for e in extra],
+        in_specs=[ANYWHERE] * (len(views) + len(extra)),
+        out_specs=[IN_VMEM] * count + [ANYWHERE] * len(extra),
         scratch_shapes=[
             pltpu.VMEM((many, 2, 2, 4, TILE_R, TILE_C), LOW),
             pltpu.VMEM((many, 2, 4, TILE_R, TILE_C), LOW),
@@ -323,13 +374,13 @@
             pltpu.VMEM((2, 2, 2, 4, TILE_R, TILE_C), LOW),
         ]
         + [pltpu.SemaphoreType.DMA((many,)) for unused in range(8)]
-        + [pltpu.SemaphoreType.DMA((2,))],
+        + [pltpu.SemaphoreType.DMA((2,)), pltpu.SemaphoreType.DMA((5,))],
         compiler_params=pltpu.CompilerParams(
             collective_id=name,
             has_side_effects=True,
             vmem_limit_bytes=(12 + 3 * many) * 2**20 if many < 16 else 58 * 2**20,
         ),
-    )(*views)
+    )(*views, *extra)
 
 
 def exchange_kernel(whole, src, out, send_sem, recv_sem, own_sem):
@@ -359,6 +410,350 @@
     )(small)
 
 
+def tall_of(height, sections=2):
+    return 256 if height % (256 * sections) == 0 else 128
+
+
+def whole(shape):
+    return pl.BlockSpec(shape, lambda *unused: (0,) * len(shape), pipeline_mode=pl.Buffered(1))
+
+
+def striped(tall, cols):
+    return pl.BlockSpec((tall, cols), lambda i: (i, 0))
+
+
+def lined(rows, wide):
+    return pl.BlockSpec((rows, wide), lambda i: (0, i))
+
+
+def squares_of(value):
+    return jnp.sum(jnp.sum(value * value, axis=1, keepdims=True), axis=0, keepdims=True)
+
+
+def padded_table_kernel(asked, sel, table, low, rows, total):
+    step = pl.program_id(0)
+
+    @pl.when(step == 0)
+    def start():
+        total[...] = jnp.zeros_like(total)
+
+    width, tall = table.shape
+    low[:, pl.ds(low.shape[1] - 128, 128)] = jnp.zeros((tall, 128), LOW)
+    eye = lax.broadcasted_iota(jnp.int32, (tall, tall), 0) == lax.broadcasted_iota(jnp.int32, (tall, tall), 1)
+    low[:, pl.ds(0, width)] = dense_nt(eye.astype(LOW), table[...].astype(LOW)).astype(LOW)
+    place = lax.broadcasted_iota(jnp.int32, (asked.shape[0], tall), 1) + step * tall
+    total[...] += dense((asked[...] == place).astype(LOW), low[...])
+
+    @pl.when(step == pl.num_programs(0) - 1)
+    def end():
+        rows[...] = dense(total[...].astype(LOW), sel[...]).astype(LOW)
+
+
+def padded_table(asked, sel, table):
+    width, height = table.shape
+    wide = sel.shape[0]
+    count = asked.shape[0]
+    tall = tall_of(height)
+    return pl.pallas_call(
+        padded_table_kernel,
+        grid=(height // tall,),
+        out_shape=[
+            jax.ShapeDtypeStruct((height, wide), LOW),
+            jax.ShapeDtypeStruct((count, sel.shape[1]), LOW),
+        ],
+        in_specs=[whole((count, 1)), whole(sel.shape), lined(width, tall)],
+        out_specs=[striped(tall, wide), whole((count, sel.shape[1]))],
+        scratch_shapes=[pltpu.VMEM((count, wide), jnp.float32)],
+        compiler_params=pltpu.CompilerParams(vmem_limit_bytes=48 * 2**20),
+    )(asked[:, None], sel, table)
+
+
+def logits_kernel(wanted, rows, table, logits, top, total, target):
+    step = pl.program_id(0)
+
+    @pl.when(step == 0)
+    def start():
+        top[...] = jnp.full_like(top, -jnp.inf)
+        total[...] = jnp.zeros_like(total)
+        target[...] = jnp.zeros_like(target)
+
+    here = dense_nt(table[...], rows[...])
+    logits[...] = here
+    higher = jnp.maximum(top[...], jnp.max(here, axis=0, keepdims=True))
+    total[...] = total[...] * jnp.exp(top[...] - higher) + jnp.sum(
+        jnp.exp(here - higher), axis=0, keepdims=True
+    )
+    top[...] = higher
+    place = lax.broadcasted_iota(jnp.int32, here.shape, 0) + step * here.shape[0]
+    target[...] += jnp.sum(jnp.where(place == wanted[...], here, 0.0), axis=0, keepdims=True)
+
+
+def logits_of(wanted, rows, table):
+    height, wide = table.shape
+    count = rows.shape[0]
+    tall = tall_of(height)
+    line = jax.ShapeDtypeStruct((1, count), jnp.float32)
+    return pl.pallas_call(
+        logits_kernel,
+        grid=(height // tall,),
+        out_shape=[jax.ShapeDtypeStruct((height, count), jnp.float32), line, line, line],
+        in_specs=[whole((1, count)), whole(rows.shape), striped(tall, wide)],
+        out_specs=[striped(tall, count)] + [whole((1, count))] * 3,
+        compiler_params=pltpu.CompilerParams(vmem_limit_bytes=48 * 2**20),
+    )(wanted[None], rows, table)
+
+
+def logits_back_kernel(share, section, wanted, top, scale, push, logits, table, grad, rows, total):
+    step = pl.program_id(1)
+    mine = (step >= section[0] * share) & (step < (section[0] + 1) * share)
+
+    @pl.when(step == 0)
+    def start():
+        total[...] = jnp.zeros_like(total)
+
+    here = logits[...]
+    place = lax.broadcasted_iota(jnp.int32, here.shape, 0) + step * here.shape[0]
+    hit = jnp.where(place == wanted[...], push[...], 0.0)
+    low = (hit - jnp.exp(here - top[...]) * scale[...]).astype(LOW)
+    grad[...] = low
+
+    @pl.when(mine)
+    def add():
+        total[...] += dense_t(low, table[...])
+
+    @pl.when(step == pl.num_programs(1) - 1)
+    def end():
+        rows[...] = total[...].astype(LOW)
+
+
+def logits_back(section, wanted, top, scale, push, logits, table, sections):
+    height, wide = table.shape
+    count = logits.shape[1]
+    tall = tall_of(height, sections)
+    block = min(count, 2048)
+    line = pl.BlockSpec((1, block), lambda j, i: (0, j))
+    tile = pl.BlockSpec((tall, block), lambda j, i: (i, j))
+    return pl.pallas_call(
+        functools.partial(logits_back_kernel, height // tall // sections),
+        grid=(count // block, height // tall),
+        out_shape=[
+            jax.ShapeDtypeStruct((height, count), LOW),
+            jax.ShapeDtypeStruct((count, wide), LOW),
+        ],
+        in_specs=[
+            pl.BlockSpec(memory_space=pltpu.SMEM),
+            line,
+            line,
+            line,
+            line,
+            tile,
+            pl.BlockSpec((tall, wide), lambda j, i: (i, 0)),
+        ],
+        out_specs=[tile, pl.BlockSpec((block, wide), lambda j, i: (j, 0))],
+        scratch_shapes=[pltpu.VMEM((block, wide), jnp.float32)],
+        compiler_params=pltpu.CompilerParams(vmem_limit_bytes=56 * 2**20),
+    )(section[None], wanted[None], top[None], scale[None], push[None], logits, table)
+
+
+def table_grad_kernel(leader, asked, got, rows, grad_logits, *refs):
+    *others, grad, squares = refs
+    step = pl.program_id(0)
+
+    @pl.when(step == 0)
+    def start():
+        gains = others[-1][...]
+        total = squares_of(gains[:2]) + leader[0] * squares_of(gains[2:3])
+        for other in others[:-1]:
+            total += squares_of(other[...])
+        squares[...] = jnp.broadcast_to(total, squares.shape)
+
+    width, tall = grad.shape
+    place = lax.broadcasted_iota(jnp.int32, (tall, asked.shape[1]), 0) + step * tall
+    here = dense_nt(rows[...], grad_logits[...]) + dense_nt(got[...], (asked[...] == place).astype(LOW))
+    here = here[:width]
+    grad[...] = here
+    squares[pl.ds(0, 1)] += leader[0] * squares_of(here)
+
+
+def table_grad(leader, asked, got, rows, grad_logits, others, width):
+    height, count = grad_logits.shape
+    tall = tall_of(height)
+    return pl.pallas_call(
+        table_grad_kernel,
+        grid=(height // tall,),
+        out_shape=[
+            jax.ShapeDtypeStruct((width, height), jnp.float32),
+            jax.ShapeDtypeStruct((8, 128), jnp.float32),
+        ],
+        in_specs=[
+            pl.BlockSpec(memory_space=pltpu.SMEM),
+            whole((1, asked.shape[0])),
+            whole(got.shape),
+            whole(rows.shape),
+            striped(tall, count),
+        ]
+        + [whole(o.shape) for o in others],
+        out_specs=[lined(width, tall), whole((8, 128))],
+        compiler_params=pltpu.CompilerParams(vmem_limit_bytes=56 * 2**20),
+    )(leader[None], asked[None], got, rows, grad_logits, *others)
+
+
+def exact_product(left, onehot):
+    high = left.astype(LOW)
+    rest = left - high.astype(jnp.float32)
+    middle = rest.astype(LOW)
+    lowest = (rest - middle.astype(jnp.float32)).astype(LOW)
+    return dense_nt(high, onehot) + (dense_nt(middle, onehot) + dense_nt(lowest, onehot))
+
+
+ROWED = 3
+SPREAD = (1, 3)
+
+
+def moments_kernel(decays, clip, sel, *refs):
+    weights, grads, firsts, seconds = (refs[7 * k : 7 * k + 7] for k in range(4))
+    new_firsts, new_seconds, updates = (refs[28 + 7 * k : 35 + 7 * k] for k in range(3))
+    kept, sums, *scratch = refs[49:49 + ROWED] , refs[49 + ROWED], *refs[50 + ROWED:]
+    staged = [scratch[5 * k : 5 * k + 5] for k in range(ROWED)]
+    in_sem, out_sem = scratch[5 * ROWED :]
+    step, steps = (pl.program_id(0), pl.num_programs(0))
+
+    def copies(k, inward):
+        w, m, v, new_m, new_v = staged[k]
+        if inward:
+            pairs = [(weights[k + 1].at[:, 0], w), (firsts[k + 1].at[:, 0], m), (seconds[k + 1].at[:, 0], v)]
+        else:
+            pairs = [(new_m, new_firsts[k + 1].at[:, 0]), (new_v, new_seconds[k + 1].at[:, 0])]
+        return [
+            pltpu.make_async_copy(src, dst, (in_sem if inward else out_sem).at[k, i])
+            for i, (src, dst) in enumerate(pairs)
+        ]
+
+    @pl.when(step == 0)
+    def start():
+        sums[...] = jnp.zeros_like(sums)
+        for k in range(ROWED):
+            for copy in copies(k, True):
+                copy.start()
+
+    def one(weight, grad, first, second, decay):
+        return (weight,) + lamb_parts(weight, clip[0] * grad, first, second, decay)
+
+    weight, new_firsts[0][...], new_seconds[0][...], update = one(
+        weights[0][...], grads[0][...], firsts[0][...], seconds[0][...], decays[0]
+    )
+    updates[0][...] = update
+    sums[pl.ds(0, 1)] += squares_of(weight)
+    sums[pl.ds(8, 1)] += squares_of(update)
+
+    def tensor(k):
+        rows, cols = updates[k + 1].shape
+        grad = grads[k + 1][pl.ds(0, rows)]
+        grad = exact_product(grad, sel[...]) if k in SPREAD else grad[:, :cols]
+        if k < ROWED:
+            for copy in copies(k, True):
+                copy.wait()
+            w, m, v, new_m, new_v = staged[k]
+        else:
+            w, m, v, new_m, new_v = (t[k + 1] for t in (weights, firsts, seconds, new_firsts, new_seconds))
+        weight, new_m[...], new_v[...], update = one(w[...], grad, m[...], v[...], decays[k + 1])
+        updates[k + 1][...] = update
+        if k < ROWED:
+            kept[k][...] = weight
+            for copy in copies(k, False):
+                copy.start()
+        for row in range(rows if k == 4 else 1):
+            part = slice(row, row + 1) if k == 4 else slice(None)
+            line = k + 1 + row + (k > 4)
+            sums[pl.ds(line, 1)] += squares_of(weight[part])
+            sums[pl.ds(8 + line, 1)] += squares_of(update[part])
+
+    for k in range(6):
+        pl.when(step == min(k + 1, 5) % steps)(functools.partial(tensor, k))
+
+    @pl.when(step == steps - 1)
+    def end():
+        for k in range(ROWED):
+            for copy in copies(k, False):
+                copy.wait()
+
+
+def moments(clip, sel, weights, grads, firsts, seconds, decays):
+    width, height = weights[0].shape
+    tall = tall_of(height)
+    flat = [w.shape if w.ndim == 2 else w.shape[::2] for w in weights]
+
+    def specs(arrays, results=False):
+        out = [lined(width, tall)]
+        for a in arrays[1:]:
+            out.append(ANYWHERE if a.ndim == 3 else whole(a.shape))
+        return out
+
+    line = [jax.ShapeDtypeStruct(w.shape, jnp.float32) for w in weights]
+    plain = [jax.ShapeDtypeStruct(s, jnp.float32) for s in flat]
+    kept = plain[1 : 1 + ROWED]
+    out = pl.pallas_call(
+        functools.partial(moments_kernel, decays),
+        grid=(height // tall,),
+        out_shape=line * 2 + plain + kept + [jax.ShapeDtypeStruct((16, 128), jnp.float32)],
+        in_specs=[pl.BlockSpec(memory_space=pltpu.SMEM), whole(sel.shape)]
+        + specs(weights)
+        + specs(grads)
+        + specs(firsts)
+        + specs(seconds),
+        out_specs=specs(line) * 2 + specs(plain) + [whole(s.shape) for s in kept] + [whole((16, 128))],
+        scratch_shapes=[pltpu.VMEM(s.shape, jnp.float32) for s in kept for unused in range(5)]
+        + [pltpu.SemaphoreType.DMA((ROWED, 3)), pltpu.SemaphoreType.DMA((ROWED, 2))],
+        compiler_params=pltpu.CompilerParams(vmem_limit_bytes=60 * 2**20),
+    )(clip[None], sel, *weights, *grads, *firsts, *seconds)
+    return (out[:7], out[7:14], out[14:21], out[21 : 21 + ROWED], out[21 + ROWED])
+
+
+def apply_kernel(scales, *refs):
+    weights, updates, new, half = (refs[5 * k : 5 * k + 5] for k in range(4))
+    staged, sem = (refs[20 : 20 + ROWED], refs[20 + ROWED])
+    step, steps = (pl.program_id(0), pl.num_programs(0))
+
+    def copy(k):
+        return pltpu.make_async_copy(staged[k - 1], new[k].at[:, 0], sem.at[k - 1])
+
+    def one(k):
+        value = weights[k][...] - RATE * scales[k] * updates[k][...]
+        half[k][...] = value.astype(LOW)
+        if 0 < k <= ROWED:
+            staged[k - 1][...] = value
+            copy(k).start()
+        else:
+            new[k][...] = value
+
+    one(0)
+    for k in range(1, 5):
+        pl.when(step == (k - 1) % steps)(functools.partial(one, k))
+
+    @pl.when(step == steps - 1)
+    def end():
+        for k in range(1, 1 + ROWED):
+            copy(k).wait()
+
+
+def apply_updates(scales, weights, updates, shapes):
+    width, height = weights[0].shape
+    tall = tall_of(height)
+    plain = [lined(width, tall)] + [whole(w.shape) for w in weights[1:]]
+    out = pl.pallas_call(
+        apply_kernel,
+        grid=(height // tall,),
+        out_shape=[jax.ShapeDtypeStruct(s, jnp.float32) for s in shapes]
+        + [jax.ShapeDtypeStruct(w.shape, LOW) for w in weights],
+        in_specs=[pl.BlockSpec(memory_space=pltpu.SMEM)] + plain * 2,
+        out_specs=plain[:1] + [ANYWHERE] * ROWED + plain[1 + ROWED :] + plain,
+        scratch_shapes=[pltpu.VMEM(w.shape, jnp.float32) for w in weights[1 : 1 + ROWED]]
+        + [pltpu.SemaphoreType.DMA((ROWED,))],
+        compiler_params=pltpu.CompilerParams(vmem_limit_bytes=56 * 2**20),
+    )(scales, *weights, *updates)
+    return (out[:5], out[5:])
+
+
 def up16(count):
     return -(-count // 16) * 16
 
@@ -484,12 +879,9 @@
 def lamb_parts(weight, grad, first, second, decay):
     first_new = BETA_ONE * first + (1.0 - BETA_ONE) * grad
     second_new = BETA_TWO * second + (1.0 - BETA_TWO) * grad * grad
-    update = (
-        first_new
-        / (1.0 - BETA_ONE**STEP)
-        / (jnp.sqrt(second_new / (1.0 - BETA_TWO**STEP)) + ADAM_EPS)
-        + decay * weight
-    )
+    root = (1.0 - BETA_TWO**STEP) ** 0.5
+    scale = root / (1.0 - BETA_ONE**STEP)
+    update = first_new * scale / (second_new * lax.rsqrt(second_new) + ADAM_EPS * root) + decay * weight
     return (first_new, second_new, update)
 
 
@@ -555,6 +947,7 @@
     ffp = n * rdp
     slots = up16(768 // n)
     sel = spread_matrix(n, r, rp)
+    sel_wide = jnp.pad(sel, ((0, wide - width), (0, 0)))
     fast = (sections, n) == (2, 16)
     qkv_wide = -(-w_qkv.shape[2] // 128) * 128
 
@@ -591,33 +984,38 @@
         mine = lax.dynamic_slice_in_dim(all_wanted.reshape(sections, n, n, slots), fsdp_index, 1, 2)
         return mine[:, :, 0]
 
-    def fetch(all_asked, choose):
-        here = lax.dynamic_index_in_dim(all_asked, section_index, 0, keepdims=False).reshape(-1)
-        rows = jnp.take(table, jnp.maximum(here, 0), axis=0).astype(LOW)
-        got = lax.all_to_all(rows.reshape(n, slots, width), "fsdp", 0, 0).reshape(n * slots, width)
-        return dense(dense(choose, got).astype(LOW), sel)
-
     asked_first = asked(notes[:, : n * slots])
-    x0 = fetch(asked_first, onehot)
+    asked_here = lax.dynamic_index_in_dim(asked_first, section_index, 0, keepdims=False).reshape(-1)
+    table_low, rows = padded_table(asked_here, sel_wide, table.T)
+    rows = rows.reshape(n, slots, wide)
+
+    blocks = (qkv_block, out_block, gu_block, down_block, gain_block)
+    if fast:
+        gathered = gather_all(blocks, WEIGHT_PIECES, 1, rows)
+        got = gathered[10]
+        gathered = (gathered[:5], gathered[5:10])
+    else:
+        got = lax.all_to_all(rows, "fsdp", 0, 0)
+        gathered = [lax.all_gather(block, BOTH, axis=0) for block in blocks]
+        gathered = [[g[k * n : (k + 1) * n] for g in gathered] for k in range(sections)]
+    qkv_all, out_all, gu_all, down_all, gain_all = [
+        [section[k].reshape(n * blocks[k].shape[0], -1) for section in gathered] for k in range(5)
+    ]
+    gain_all = jnp.stack([g.reshape(n, 16, 128)[:, :3, :rp] for g in gain_all])
+    gain_all = jnp.moveaxis(gain_all, 2, 1).reshape(sections, 3, wide).astype(jnp.float32)
+    final_all = gain_all[0, 2]
+    x0 = dense(onehot, got.reshape(n * slots, wide))
 
     def fetch_more(state):
         turn, total = state
         choose, more = lookup_round(ids, owner, rank, turn, slots, n, vshard)
-        return (turn + 1, total + fetch(asked(lax.all_gather(more, BOTH, axis=0)), choose))
+        here = asked(lax.all_gather(more, BOTH, axis=0))
+        here = lax.dynamic_index_in_dim(here, section_index, 0, keepdims=False).reshape(-1)
+        rows = dense(jnp.take(table, jnp.maximum(here, 0), axis=0).astype(LOW), sel).astype(LOW)
+        got = lax.all_to_all(rows.reshape(n, slots, wide), "fsdp", 0, 0).reshape(n * slots, wide)
+        return (turn + 1, total + dense(choose, got))
 
     x0 = lax.while_loop(lambda state: state[0] < turns, fetch_more, (jnp.int32(1), x0))[1]
-
-    blocks = (qkv_block, out_block, gu_block, down_block, gain_block)
-    if fast:
-        gathered = gather_all(blocks, WEIGHT_PIECES, 1)
-    else:
-        gathered = [lax.all_gather(block, BOTH, axis=0) for block in blocks]
-    qkv_all, out_all, gu_all, down_all = [
-        g.reshape(sections, n * g.shape[1], g.shape[2]) for g in gathered[:4]
-    ]
-    gain_all = gathered[4].reshape(sections, n, 16, 128)[:, :, :3, :rp]
-    gain_all = jnp.moveaxis(gain_all, 2, 1).reshape(sections, 3, wide).astype(jnp.float32)
-    final_all = gain_all[0, 2]
 
     everyone = jnp.arange(TOK_MB)
     cosine, sine = rotary_angles(everyone)
@@ -662,21 +1060,17 @@
     branch_s, gate_s, upper_s, hidden_s = mlp(b_s, gu_all[last], down_all[last])
     y_s = mixed_s + branch_s
     scale_y = inverse_rms(y_s, width)
-    head_in = (y_s * scale_y * final_all).astype(LOW)
+    head_in = dense_nt((y_s * scale_y * final_all).astype(LOW), sel_wide).astype(LOW)
 
     if fast:
-        rows_all = gather_all([head_in], [(0, 16 * k, 16, k % 2) for k in range(4)], 2)[0]
+        rows_all = jnp.concatenate(gather_all([head_in], [(0, 16 * k, 16, k % 2) for k in range(4)], 2))
     else:
         rows_all = lax.all_gather(head_in, BOTH, axis=0)
-    rows_all = dense_nt(rows_all.reshape(-1, wide), sel).astype(LOW)
+    rows_all = rows_all.reshape(-1, wide)
     own_rows = rows_all.shape[0] // sections
-    table_low = table.astype(LOW)
-    logits = dense_nt(rows_all, table_low)
-    hit = jnp.arange(vshard)[None, :] == (wanted_rows - vstart)[:, None]
-    top_here = jnp.max(logits, axis=1)
-    total_here = jnp.sum(jnp.exp(logits - top_here[:, None]), axis=1)
-    target_here = jnp.sum(jnp.where(hit, logits, 0.0), axis=1)
-    stats = jnp.stack([top_here, total_here, target_here])
+    wanted_here = wanted_rows - vstart
+    logits, top_here, total_here, target_here = logits_of(wanted_here, rows_all, table_low)
+    stats = jnp.concatenate([top_here, total_here, target_here])
     if fast:
         stats = exchange(stats.reshape(-1, 128), 3, whole=False).reshape(n, 3, -1)
     else:
@@ -694,19 +1088,17 @@
     push = BETA * jax.nn.sigmoid(-BETA * delta)
     grad_seq = jnp.sum((passed - chosen) * push[:, None], axis=0)
     grad_row = jnp.repeat(grad_seq, SCORED)
-    prob = jnp.exp(logits - top[:, None]) * (1.0 / total)[:, None]
-    grad_logits = (grad_row[:, None] * (hit.astype(jnp.float32) - prob)).astype(LOW)
-    grad_table = dense_t(grad_logits, rows_all)
-    own_vocab = vshard // sections
-    own_grads = lax.dynamic_slice_in_dim(grad_logits, section_index * own_vocab, own_vocab, 1)
-    own_table = lax.dynamic_slice_in_dim(table_low, section_index * own_vocab, own_vocab)
-    grad_rows = dense(dense(own_grads, own_table).astype(LOW), sel).astype(LOW)
+    grad_logits, grad_rows = logits_back(
+        section_index, wanted_here, top, grad_row / total, grad_row, logits, table_low, sections
+    )
     if fast:
         halves = [[grad_rows[k * own_rows : (k + 1) * own_rows]] for k in range(sections)]
         grad_head = reduce_all(halves, 4, 1)[0]
     else:
         grad_head = lax.psum_scatter(grad_rows, BOTH, scatter_dimension=0, tiled=True)
-    grad_y, grad_final = norm_back(y_s, scale_y, final_all, grad_head.astype(jnp.float32), width)
+    grad_y, grad_final = norm_back(
+        y_s, scale_y, final_all, jnp.dot(grad_head.astype(jnp.float32), sel_wide.astype(jnp.float32), precision=HI), width
+    )
 
     grads = [None] * sections
     g_down, g_gu, grad_b = mlp_back(
@@ -773,23 +1165,23 @@
         upstream = grad_in + grad_mixed
         grads[layer] = (g_qkv, g_out, g_gu, g_down, jnp.stack([gain_one, gain_two]))
 
-    grad_x0 = dense_nt(upstream.astype(LOW), sel).astype(LOW)
-
-    def give(grad_rows, all_asked, choose):
+    grad_x0 = dense_nt(upstream.astype(LOW), sel_wide).astype(LOW)
+
+    def give(all_asked, choose):
         rows = dense_t(choose, grad_x0).astype(LOW)
-        got = lax.all_to_all(rows.reshape(n, slots, width), "fsdp", 0, 0)
-        every = lax.all_gather(got, "section", axis=0).reshape(-1, width)
-        place_of = (jnp.arange(vshard)[:, None] == all_asked.reshape(-1)[None, :]).astype(LOW)
-        return grad_rows + dense(place_of, every)
-
-    grad_table = give(grad_table, asked_first, onehot)
+        got = lax.all_to_all(rows.reshape(n, slots, wide), "fsdp", 0, 0)
+        return (all_asked.reshape(-1), lax.all_gather(got, "section", axis=0).reshape(-1, wide))
 
     def give_more(state):
-        turn, grad_rows = state
+        turn, grad, squares = state
         choose, more = lookup_round(ids, owner, rank, turn, slots, n, vshard)
-        return (turn + 1, give(grad_rows, asked(lax.all_gather(more, BOTH, axis=0)), choose))
-
-    grad_table = lax.while_loop(lambda state: state[0] < turns, give_more, (jnp.int32(1), grad_table))[1]
+        places, got = give(asked(lax.all_gather(more, BOTH, axis=0)), choose)
+        place_of = (jnp.arange(vshard)[:, None] == places[None, :]).astype(LOW)
+        new = grad + lax.dot_general(
+            got[:, :width], place_of, (((0,), (1,)), ((), ())), preferred_element_type=jnp.float32
+        )
+        every = squares[1] + jnp.where(leader, jnp.sum(new**2), 0.0)
+        return (turn + 1, new, squares.at[0].set(every))
 
     def gain_rows(layer):
         rows = jnp.concatenate([grads[layer][4], grad_final[None]], axis=0).reshape(3, n, rp)
@@ -800,7 +1192,8 @@
         [g.astype(LOW) for g in grads[layer][:4] + (gain_rows(layer),)] for layer in range(sections)
     ]
     if fast:
-        summed = reduce_all(outward, 5, 2)
+        rows = dense_t(onehot, grad_x0).astype(LOW).reshape(n, slots, wide)
+        *summed, got = reduce_all(outward, 5, 2, rows)
     else:
         summed = [
             lax.psum_scatter(
@@ -808,97 +1201,74 @@
             ).astype(jnp.float32)
             for arrays in zip(*outward)
         ]
-    s_qkv = summed[0][:r, : w_qkv.shape[2]]
-    s_out = summed[1][:r].reshape(r, n, rp)[:, :, :r].reshape(r, width)
-    s_gu = summed[2][:r].reshape(r, 2, n, rdp)[:, :, :, :rd].reshape(r, 2 * n * rd)
-    s_down = summed[3][:rd].reshape(rd, n, rp)[:, :, :r].reshape(rd, width)
-    s_gains = summed[4][:2, :r]
-    s_final = summed[4][2, :r]
-
-    grads_all = (
-        grad_table,
-        s_qkv[None],
-        s_out[None],
-        s_gu[None],
-        s_down[None],
-        s_gains[None],
-        s_final,
-    )
-    weights_all = (table, w_qkv, w_out, w_gu, w_down, gains, final_gain)
-    firsts = (first_table, first_qkv, first_out, first_gu, first_down, first_gains, first_final)
-    seconds = (
-        second_table,
-        second_qkv,
-        second_out,
-        second_gu,
-        second_down,
-        second_gains,
-        second_final,
-    )
-    slot_total = 6 * sections + 2
-    shared_share = jnp.where(leader, 1.0, 0.0)
-
-    def slot_squares(arrays):
-        rows_each_section = jnp.stack(
-            [
-                jnp.sum(arrays[1] ** 2),
-                jnp.sum(arrays[2] ** 2),
-                jnp.sum(arrays[3] ** 2),
-                jnp.sum(arrays[4] ** 2),
-                jnp.sum(arrays[5][0, 0] ** 2),
-                jnp.sum(arrays[5][0, 1] ** 2),
-            ]
-        )
-        slot_entries = 6 * section_index + jnp.arange(6)
-        positioned_rows = jnp.sum(
-            jnp.where(
-                slot_entries[:, None] == jnp.arange(slot_total)[None, :],
-                rows_each_section[:, None],
-                0.0,
-            ),
-            axis=0,
-        )
-        common_prompt = shared_share * jnp.stack([jnp.sum(arrays[0] ** 2), jnp.sum(arrays[6] ** 2)])
-        return positioned_rows + jnp.concatenate(
-            [jnp.zeros((slot_total - 2,), jnp.float32), common_prompt]
-        )
+        got = give(asked_first, onehot)[1]
+    if rdp != rd:
+        summed[2] = summed[2].reshape(rp, 2, n, rdp)[:, :, :, :rd].reshape(rp, 2 * n * rd)
+    grad_table, grad_squares = table_grad(
+        leader.astype(jnp.float32),
+        asked_first.reshape(-1),
+        got.reshape(-1, wide).T,
+        rows_all.T,
+        grad_logits,
+        summed,
+        width,
+    )
+    grad_table, grad_squares = lax.while_loop(
+        lambda state: state[0] < turns, give_more, (jnp.int32(1), grad_table, grad_squares)
+    )[1:]
 
     def everyones(sums, name):
-        if not fast:
-            return lax.psum(sums, BOTH)
-        flat = sums.reshape(-1)
-        small = jnp.broadcast_to(jnp.pad(flat, (0, 128 - flat.shape[0])), (8, 128))
-        return jnp.sum(exchange(small, name)[:, 0], axis=0)[: flat.shape[0]].reshape(sums.shape)
-
-    grad_sq = everyones(slot_squares(grads_all), 6)
-    grad_norm = jnp.sqrt(jnp.sum(grad_sq))
+        if fast:
+            return exchange(sums, name)
+        return lax.all_gather(sums, BOTH, axis=0)
+
+    grad_norm = jnp.sqrt(jnp.sum(everyones(grad_squares, 6)[:, 0, 0]))
     clip = jnp.minimum(1.0, CLIP / grad_norm)
-    decays = (DECAY, DECAY, DECAY, DECAY, DECAY, 0.0, 0.0)
-    parts = [
-        lamb_parts(w, clip * g, m, v, d)
-        for w, g, m, v, d in zip(weights_all, grads_all, firsts, seconds, decays)
+
+    def views(arrays):
+        out = [arrays[0].T] + [a.transpose(1, 0, 2) for a in arrays[1:4]]
+        return out + [arrays[4][0], arrays[5][0], arrays[6][None]]
+
+    weights_all = views((table, w_qkv, w_out, w_gu, w_down, gains, final_gain))
+    grads_all = [grad_table] + summed[:4] + [summed[4][:2, :r], summed[4][2:3, :r]]
+    new_firsts, new_seconds, updates, kept_weights, sums = moments(
+        clip,
+        sel,
+        weights_all,
+        grads_all,
+        views((first_table, first_qkv, first_out, first_gu, first_down, first_gains, first_final)),
+        views((second_table, second_qkv, second_out, second_gu, second_down, second_gains, second_final)),
+        (DECAY,) * 5 + (0.0, 0.0),
+    )
+    sums = everyones(sums, 7)[:, :, 0].reshape(sections, n, 2, 8)
+    sums = jnp.sum(sums, axis=1)
+    layered = jnp.moveaxis(sums[:, :, 1:7], 1, 0).reshape(2, -1)
+    matrix_norms = jnp.sqrt(jnp.concatenate([layered, sums[0, :, 0:1], sums[0, :, 7:8]], axis=1))
+    trust_ratio = matrix_norms[0] / matrix_norms[1]
+    own = lax.dynamic_slice_in_dim(trust_ratio, 6 * section_index, 6)
+    last_two = trust_ratio[6 * sections :]
+    new, half = apply_updates(
+        jnp.concatenate([last_two[:1], own[:4]]),
+        [weights_all[0], *kept_weights, weights_all[4]],
+        updates[:5],
+        [w.shape for w in weights_all[:5]],
+    )
+    new = list(new) + [
+        weights_all[5] - RATE * own[4:6][:, None] * updates[5],
+        weights_all[6] - RATE * last_two[1] * updates[6],
     ]
-    squares = everyones(
-        jnp.stack([slot_squares(weights_all), slot_squares(tuple((p[2] for p in parts)))]), 7
-    )
-    weight_norms, update_norms = (jnp.sqrt(squares[0]), jnp.sqrt(squares[1]))
-    trust_ratio = weight_norms / update_norms
-    own = lax.dynamic_slice_in_dim(trust_ratio, 6 * section_index, 6)
-    scales = (
-        trust_ratio[slot_total - 2],
-        own[0],
-        own[1],
-        own[2],
-        own[3],
-        own[4:6][None, :, None],
-        trust_ratio[slot_total - 1],
-    )
-    new = [w - RATE * s * p[2] for w, s, p in zip(weights_all, scales, parts)]
-    matrix_norms = jnp.stack([weight_norms, update_norms])
+
+    def back(k, array):
+        if k == 0:
+            return array.T
+        if k == 6:
+            return array[0]
+        return array.transpose(1, 0, 2) if array.ndim == 3 else array[None]
+
     outs = [loss, grad_norm, matrix_norms]
     for k in range(7):
-        outs += [new[k], parts[k][0], parts[k][1]]
-    return tuple(outs + [new[k].astype(LOW) for k in range(5)])
+        outs += [back(k, t[k]) for t in (new, new_firsts, new_seconds)]
+    return tuple(outs + [back(k, half[k]) for k in range(5)])
 
 
 def solution(mesh):

time: 1160 us -> 1070 us (0.922)
  Pallas kernels: 534 us -> 725 us
  other arithmetic: 170 us -> 49.1 us
  matrix products: 253 us -> 187 us
  local copies, waits for them, and re-layouts: 139 us -> 76.5 us
  starting transfers between devices: 19.4 us -> 0 us
    pallas_call x4 -> x10, Pallas kernels: 490 us -> 678 us  [the longest x2 277 us: reduce_all(): pl.pallas_call(functools.partial(reduce_kernel, pieces, count, len(extra)...]
    reduce_sum x25 -> x2, other arithmetic: 74.6 us -> 1.63 us  [the longest x1 1.54 us: shards(): grad_norm = jnp.sqrt(jnp.sum(everyones(grad_squares, 6)[:, 0, 0]))]
    convert_element_type x8 -> x1, other arithmetic: 48.9 us -> 0.38 us  [spread_matrix(): return (place[:, None] == jnp.arange(parts * padded)[None, :]).astype(LOW)]
    slice x7 -> x6, local copies, waits for them, and re-layouts: 40.2 us -> 4.14 us  [the longest x1 1.24 us: shards(): summed[4][:2, :r]]
    dot_general x17 -> x15, matrix products: 66.9 us -> 39.5 us  [dense(): return jnp.dot(left, right, preferred_element_type=jnp.float32)]
    dot_general x10 -> x9, matrix products: 61.7 us -> 41.1 us  [dense_t(): lax.dot_general(left, right, (((0,), (0,)), ((), ())), preferred_element_...]
    dot_general x12 -> x11, matrix products: 74.9 us -> 54.6 us  [dense_nt(): lax.dot_general(left, right, (((1,), (1,)), ((), ())), preferred_element_...]
    all_to_all x2 -> x0, starting transfers between devices: 19.4 us -> none  [the longest x1 14.3 us: fetch(): lax.all_to_all(rows.reshape(n, slots, width), 'fsdp', 0, 0)]
  transfers between devices with their start and end apart: 3 -> 0, of which waited for: 2 -> 0; matrix products, arithmetic and copies ran while one was open for 7% -> 0% of each run, Pallas kernels for 20% -> 0%
where the time goes in v3:
time: 1070 us; the launch traced here: 1060 us
  Pallas kernels  725 us (68%)
  matrix products  187 us (17%)
  local copies, waits for them, and re-layouts  76.5 us (7%)
  other arithmetic  49.1 us (5%)
  between operations  21.3 us (2%)
    pallas_call x2, Pallas kernels, reduce_all(): pl.pallas_call(functools.partial(reduce_kernel, pieces, count, len(extra)...  277 us
    pallas_call x2, Pallas kernels, gather_all(): pl.pallas_call(functools.partial(gather_kernel, pieces, len(blocks), len(...  242 us
    dot_general x11, matrix products, dense_nt(): lax.dot_general(left, right, (((1,), (1,)), ((), ())), preferred_element_...  54.6 us
    pallas_call x4, Pallas kernels, exchange(): pl.pallas_call(functools.partial(exchange_kernel, whole), out_shape=jax.S...  46.9 us
    dot_general x9, matrix products, dense_t(): lax.dot_general(left, right, (((0,), (0,)), ((), ())), preferred_element_...  41.1 us
    pallas_call x1, Pallas kernels, moments(): pl.pallas_call(functools.partial(moments_kernel, decays), grid=(height //...  40.1 us
    dot_general x15, matrix products, dense(): return jnp.dot(left, right, preferred_element_type=jnp.float32)  39.5 us
    pallas_call x1, Pallas kernels, table_grad(): pl.pallas_call(table_grad_kernel, grid=(height // tall,), out_shape=[jax....  31.7 us

profile of v3, /device:TPU:0, one launch (start us, length us, event | category | flops | bytes accessed | tf_op | source)
XLA Modules:
  0.0 1060.7 jit_solution(4054851670769595076)
XLA Ops:
  16.3 12.2 %shard_map.464 = s32[32,8,128]{2,1,0:T(8,128)} custom-call(s32[8,128]{1,0:T(8,128)} %fusion.170.src), custom_call_target="tpu_custom_call" | custom-call | tf_op jit(solution)/shard_map/pallas_call | solution.py:403
  39.0 17.9 %shard_map.465 = (bf16[3072,1024]{1,0:T(8,128)(2,1)}, bf16[768,1024]{1,0:T(8,128)(2,1)S(1)}) custom-call(s32[768,1]{1,0:T(8,128)S(1)} %broadcast_in_dim_reshape.3.asked, bf16[1024,1024]{1,0:T(8,128)(2,1)S(1)} %pad.48.sel, f32[960,3072]{1,0:T(8,128)} %bitcast.362), custom_call_target="tpu_custom_call" | custom-call | tf_op jit(solution)/shard_map/pallas_call | solution.py:457
  58.0 210.2 %shard_map.466 = (bf16[16,64,1664]{2,1,0:T(8,128)(2,1)}, bf16[16,64,1024]{2,1,0:T(8,128)(2,1)}, bf16[16,64,5120]{2,1,0:T(8,128)(2,1)}, bf16[16,160,1024]{2,1,0:T...) custom-call(bf16[64,1664]{1,0:T(8,128)(2,1)} %pad.44.refs_0_, ...), custom_call_target="tpu_custom_call" | custom-call | tf_op jit(solution)/shard_map/pallas_call | solution.py:185
  268.2 3.7 fusion.68
  272.6 9.8 copy.219
  287.1 4.1 fusion.213
  295.4 3.2 slice.302
  298.5 3.2 copy.223
  302.1 2.8 subtract_convert_fusion.1
  307.6 9.8 fusion.227
  317.4 7.0 fusion.70
  328.7 8.5 fusion.214
  341.3 4.2 multiply_reduce_fusion.7
  346.3 3.3 fusion.135
  367.6 3.2 fusion.228
  375.1 6.1 fusion.212
  384.0 31.7 %shard_map.467 = (bf16[16,64,1024]{2,1,0:T(8,128)(2,1)}, bf16[16,64,1024]{2,1,0:T(8,128)(2,1)}) custom-call(bf16[64,1024]{1,0:T(8,128)(2,1)} %convolution_convert_fusion.15.refs_0_), custom_call_target="tpu_custom_call" | custom-call | tf_op jit(solution)/shard_map/pallas_call | solution.py:185
  418.4 23.7 %shard_map.468 = (f32[3072,2048]{1,0:T(8,128)}, f32[1,2048]{1,0:T(1,128)S(1)}, f32[1,2048]{1,0:T(1,128)S(1)}, f32[1,2048]{1,0:T(1,128)S(1)}) custom-call(s32[1,2048]{1,0:T(1,128)S(1)} %sub.322.wanted, bf16[2048,1024]{1,0:T(8,128)(2,1)S(1)} %bitcast.357, bf16[3072,1024]{1,0:T(8,128)(2,1)} %get-tuple-element.463.table), custom_call_target="tpu_custom_call" | custom-call | tf_op jit(solution)/shard_map/pallas_call | solution.py:496
  442.8 12.7 %shard_map.469 = f32[16,48,128]{2,1,0:T(8,128)} custom-call(f32[48,128]{1,0:T(8,128)} %reshape.970.src), custom_call_target="tpu_custom_call" | custom-call | tf_op jit(solution)/shard_map/pallas_call | solution.py:403
  461.0 25.8 %shard_map.470 = (bf16[3072,2048]{1,0:T(8,128)(2,1)}, bf16[2048,1024]{1,0:T(8,128)(2,1)}) custom-call(s32[1]{0:T(128)} %bitcast.63.section, s32[1,2048]{1,0:T(1,128)} %copy-done.4, f32[1,2048]{1,0:T(1,128)} %bitcast.459, f32[1,2048]{1,0:T(1,128)} %div.285.scale, f32[1,2048]{1,0:T(1,128)} %copy-done.89, f32[3072,2048]{1,0:T(8,128)} %get-tuple-element.467.logits, ...), custom_call_target="tpu_custom_call" | custom-call | tf_op jit(solution)/shard_map/pallas_call | solution.py:536
  486.8 2.8 fusion.221
  489.7 41.4 %shard_map.471 = f32[64,1024]{1,0:T(8,128)S(1)} custom-call(bf16[4,2,2,64,1024]{4,3,2,1,0:T(8,128)(2,1)S(1)} %bitcast.360, bf16[4,2,2,64,1024]{4,3,2,1,0:T(8,128)(2,1)S(1)} %bitcast.359), custom_call_target="tpu_custom_call" | custom-call | tf_op jit(solution)/shard_map/pallas_call | solution.py:363
  533.1 4.5 multiply_convert_fusion.7
  537.6 3.9 multiply_reduce_fusion.10
  541.7 3.2 fusion.95
  556.9 4.7 multiply_reduce_fusion.2
  562.3 9.3 multiply_convert_fusion.1
  571.6 11.0 %multiply_reduce_fusion.3 = (bf16[1024]{0:T(1024)(128)(2,1)}, f32[512]{0:T(512)S(1)}, f32[512,1024]{1,0:T(8,128)S(1)}) fusion(f32[512,1024]{1,0:T(8,128)S(1)} %copy-done.34, f32[512]{0:T(512)S(1)} %copy-done.127, f32[1024]{0:T(1024)S(1)} %bitcast.472, bf16[1024,5120]{1,0:T(8,128)(2,1)} %bitcast.488, bf16[512,2560]{1,0:T(8,128)(2,1)} %get-tuple-element.674, ...), kind=kOutput, calls=%fused_computation.97 | convolution fusion | flops 5382339072 | bytes 19933184 | tf_op jit(solution)/shard_map/dot_general | solution.py:772
  584.5 5.6 fusion.73
  590.1 8.3 fusion.81
  599.9 6.9 fusion.25
  606.9 7.4 fusion.27
  620.4 4.4 convolution_convert_fusion.6
  624.9 2.6 convolution_convert_fusion.8
  628.8 8.7 convolution_convert_fusion.2
  637.5 5.1 convolution_convert_fusion.3
  645.3 7.2 multiply_reduce_fusion.1
  658.0 6.0 convolution_convert_fusion.5
  666.2 5.9 convolution_convert_fusion.1
  672.2 3.9 convolution_convert_fusion.4
  680.6 235.3 %shard_map.472 = (f32[64,1664]{1,0:T(8,128)}, f32[64,1024]{1,0:T(8,128)}, f32[64,5120]{1,0:T(8,128)}, f32[160,1024]{1,0:T(8,128)}, f32[32,128]{1,0:T(8,128)}, /*index=5*/bf16[32,48,1024]{2,1,0:T(8,128)(2,1)}) custom-call(bf16[4,2,2,64,1664]{4,3,2,1,0:T(8,128)(2,1)} %bitcast.392, bf16[4,2,2,64,1024]{4,3,2,1,0:T(8,128)(2,1)} %bitcast.402, ...), custom_call_target="tpu_custom_call" | custom-call | tf_op jit(solution)/shard_map/pallas_call | solution.py:363
  915.9 4.6 copy.241
  920.5 6.4 copy.242
  927.0 31.7 %shard_map.473 = (f32[960,3072]{1,0:T(8,128)}, f32[8,128]{1,0:T(8,128)S(1)}) custom-call(f32[1]{0:T(128)} %bitcast.57.leader, s32[1,1536]{1,0:T(1,128)} %broadcast_in_dim_reshape_squeeze.3.asked, bf16[1024,1536]{1,0:T(8,128)(2,1)} %bitcast.377, bf16[1024,2048]{1,0:T(8,128)(2,1)} %bitcast.374, bf16[3072,2048]{1,0:T(8,128)(2,1)} %get-tuple-element.470.grad_logits, ...), custom_call_target="tpu_custom_call" | custom-call | tf_op jit(solution)/shard_map/pallas_call | solution.py:581
  959.5 9.9 shard_map.474
  974.2 40.1 %shard_map.475 = (f32[960,3072]{1,0:T(8,128)}, f32[60,1,1600]{2,1,0:T(1,128)}, f32[60,1,960]{2,1,0:T(1,128)}, f32[60,1,5120]{2,1,0:T(1,128)}, f32[160,960]{1,0:T...) custom-call(f32[1]{0:T(128)} %bitcast.112.clip, ...), custom_call_target="tpu_custom_call" | custom-call | tf_op jit(solution)/shard_map/pallas_call | solution.py:695
  1014.3 12.0 %shard_map.476 = f32[32,16,128]{2,1,0:T(8,128)} custom-call(f32[16,128]{1,0:T(8,128)} %get-tuple-element.480.src), custom_call_target="tpu_custom_call" | custom-call | tf_op jit(solution)/shard_map/pallas_call | solution.py:403
  1029.9 20.6 %shard_map.477 = (f32[960,3072]{1,0:T(8,128)}, f32[60,1,1600]{2,1,0:T(1,128)}, f32[60,1,960]{2,1,0:T(1,128)}, f32[60,1,5120]{2,1,0:T(1,128)}, f32[160,960]{1,0:T...) custom-call(f32[5]{0:T(128)} %pad_maximum_fusion.24.scales, ...), custom_call_target="tpu_custom_call" | custom-call | tf_op jit(solution)/shard_map/pallas_call | solution.py:743
  (513 shorter events, 122.9 us)
Async XLA Ops:
  7.2 26.7 %copy-start.19 = (f32[1,60,5120]{2,0,1:T(1,128)S(1)}, f32[1,60,5120]{2,0,1:T(1,128)}, u32[]{:S(2)}) copy-start(f32[1,60,5120]{2,0,1:T(1,128)} %param.38) | copy-start | bytes 3686404
  13.5 254.7 %copy-start.123 = (s32[512]{0:T(512)}, s32[512]{0:T(512)S(1)}, u32[]{:S(2)}) copy-start(s32[512]{0:T(512)S(1)} %get-tuple-element.719) | copy-start | bytes 6148
  29.6 388.8 %copy-start.4 = (s32[1,2048]{1,0:T(1,128)}, s32[1,2048]{1,0:T(1,128)S(1)}, u32[]{:S(2)}) copy-start(s32[1,2048]{1,0:T(1,128)S(1)} %sub.322.wanted) | copy-start | bytes 24580
  38.8 492.3 %copy-start.5 = (bf16[960,1024]{1,0:T(8,128)(2,1)}, bf16[960,1024]{1,0:T(8,128)(2,1)S(1)}, u32[]{:S(2)}) copy-start(bf16[960,1024]{1,0:T(8,128)(2,1)S(1)} %fusion.42.sel) | copy-start | bytes 5898244
  272.6 9.8 copy-start.67
  283.1 8.1 copy-start.81
  284.6 90.5 %copy-start.65 = (f32[1,1,1024]{2,0,1:T(1,128)}, f32[1,1,1024]{2,0,1:T(1,128)S(1)}, u32[]{:S(2)}) copy-start(f32[1,1,1024]{2,0,1:T(1,128)S(1)} %get-tuple-element.700) | copy-start | bytes 12292
  307.6 9.8 copy-start.59
  307.6 9.8 copy-start.61
  307.6 9.8 copy-start.71
  326.6 14.7 %slice-start.12 = ((s8[5242880]{0:T(1024)(128)(4,1)}), s8[4194304]{0:T(1024)(128)(4,1)S(1)}, s32[]{:S(2)}) async-start(s8[5242880]{0:T(1024)(128)(4,1)} %bitcast.491), calls=%async_computation.15 | async-start | bytes 8388608
  328.0 13.3 %copy-start.33 = (f32[512,1024]{1,0:T(8,128)}, f32[512,1024]{1,0:T(8,128)S(1)}, u32[]{:S(2)}) copy-start(f32[512,1024]{1,0:T(8,128)S(1)} %get-tuple-element.735) | copy-start | bytes 6291460
  328.7 8.5 copy-start.126
  328.7 12.6 %slice-start.13 = ((s8[5242880]{0:T(1024)(128)(4,1)}), s8[1048576]{0:T(1024)(128)(4,1)S(1)}, s32[]{:S(2)}) async-start(s8[5242880]{0:T(1024)(128)(4,1)} %bitcast.491), calls=%async_computation.16 | async-start | bytes 2097152
  350.5 12.8 %copy-start.22 = (bf16[512,1024]{1,0:T(8,128)(2,1)}, bf16[512,1024]{1,0:T(8,128)(2,1)S(1)}, u32[]{:S(2)}) copy-start(bf16[512,1024]{1,0:T(8,128)(2,1)S(1)} %multiply_convert_fusion.3) | copy-start | bytes 3145732
  370.8 10.6 %slice-start.10 = ((s8[5242880]{0:T(1024)(128)(4,1)}), s8[4194304]{0:T(1024)(128)(4,1)S(1)}, s32[]{:S(2)}) async-start(s8[5242880]{0:T(1024)(128)(4,1)} %bitcast.387), calls=%async_computation.13 | async-start | bytes 8388608
  418.3 23.8 %copy-start.2 = (bf16[32,64,1024]{2,1,0:T(8,128)(2,1)}, bf16[32,64,1024]{2,1,0:T(8,128)(2,1)S(1)}, u32[]{:S(2)}) copy-start(bf16[32,64,1024]{2,1,0:T(8,128)(2,1)S(1)} %pad_maximum_fusion.1) | copy-start | bytes 12582916
  442.1 15.2 %copy-start.146 = (s32[64]{0:T(128)S(1)}, s32[64]{0:T(128)}, u32[]{:S(2)}) copy-start(s32[64]{0:T(128)} %param.34) | copy-start | bytes 772
  486.8 50.8 %slice-start = ((s8[10485760]{0:T(1024)(128)(4,1)}), s8[4194304]{0:T(1024)(128)(4,1)S(1)}, s32[]{:S(2)}) async-start(s8[10485760]{0:T(1024)(128)(4,1)} %bitcast.366), calls=%async_computation.3 | async-start | bytes 8388608
  486.8 50.8 %slice-start.1 = ((s8[10485760]{0:T(1024)(128)(4,1)}), s8[4194304]{0:T(1024)(128)(4,1)S(1)}, s32[]{:S(2)}) async-start(s8[10485760]{0:T(1024)(128)(4,1)} %bitcast.366), calls=%async_computation.4 | async-start | bytes 8388608
  533.0 8.5 copy-start.30
  541.7 10.8 %copy-start.28 = (f32[64,1024]{1,0:T(8,128)}, f32[64,1024]{1,0:T(8,128)S(1)}, u32[]{:S(2)}) copy-start(f32[64,1024]{1,0:T(8,128)S(1)} %subtract_add_fusion.1) | copy-start | bytes 786436
  562.3 20.4 %copy-start.15 = (f32[512,1024]{1,0:T(8,128)}, f32[512,1024]{1,0:T(8,128)S(1)}, u32[]{:S(2)}) copy-start(f32[512,1024]{1,0:T(8,128)S(1)} %slice_add_fusion.1) | copy-start | bytes 6291460
  562.3 9.4 copy-start.34
  562.3 9.4 copy-start.107
  562.3 9.3 copy-start.127
  571.6 11.0 %copy-start.152 = (bf16[512,2560]{1,0:T(8,128)(2,1)}, bf16[512,2560]{1,0:T(8,128)(2,1)S(1)}, u32[]{:S(2)}) copy-start(bf16[512,2560]{1,0:T(8,128)(2,1)S(1)} %get-tuple-element.673) | copy-start | bytes 7864324
  571.6 11.0 %copy-start.129 = (f32[512]{0:T(512)S(1)}, f32[512]{0:T(512)}, u32[]{:S(2)}) copy-start(f32[512]{0:T(512)} %get-tuple-element.713) | copy-start | bytes 6148
  584.5 14.0 %slice-start.3 = ((s8[15728640]{0:T(1024)(128)(4,1)}), s8[3145728]{0:T(1024)(128)(4,1)S(1)}, s32[]{:S(2)}) async-start(s8[15728640]{0:T(1024)(128)(4,1)} %bitcast.375), calls=%async_computation.6 | async-start | bytes 6291456
  590.1 8.4 slice-start.4
  590.1 8.4 slice-start.5
  590.1 9.5 slice-start.6
  590.1 9.5 copy-start.72
  590.1 9.5 copy-start.93
  590.1 9.8 copy-start.150
  598.5 20.5 %copy-start.151 = (bf16[5,64,512]{2,1,0:T(8,128)(2,1)}, bf16[5,64,512]{2,1,0:T(8,128)(2,1)S(1)}, u32[]{:S(2)}) copy-start(bf16[5,64,512]{2,1,0:T(8,128)(2,1)S(1)} %fusion.81) | copy-start | bytes 983044
  628.8 8.7 copy-start.16
  628.8 8.7 copy-start.27
  645.3 11.9 %copy-start.47 = (bf16[64,960]{1,0:T(8,128)(2,1)S(1)}, bf16[64,960]{1,0:T(8,128)(2,1)}, u32[]{:S(2)}) copy-start(bf16[64,960]{1,0:T(8,128)(2,1)} %copy-done.46) | copy-start | bytes 368644
  645.3 12.7 %copy-start.23 = (bf16[512,1024]{1,0:T(8,128)(2,1)S(1)}, bf16[512,1024]{1,0:T(8,128)(2,1)}, u32[]{:S(2)}) copy-start(bf16[512,1024]{1,0:T(8,128)(2,1)} %copy-done.22) | copy-start | bytes 3145732
  927.0 31.7 %copy-start.69 = (s32[1,512]{1,0:T(1,128)S(1)}, s32[1,512]{1,0:T(1,128)}, u32[]{:S(2)}) copy-start(s32[1,512]{1,0:T(1,128)} %param.31) | copy-start | bytes 6148
  927.0 31.7 %copy-start.82 = (s32[512]{0:T(512)S(1)}, s32[512]{0:T(512)}, u32[]{:S(2)}) copy-start(s32[512]{0:T(512)} %copy-done.81) | copy-start | bytes 6148
  1027.9 22.5 %copy-start.144 = (f32[2,14]{1,0:T(2,128)}, f32[2,14]{1,0:T(2,128)S(1)}, u32[]{:S(2)}) copy-start(f32[2,14]{1,0:T(2,128)S(1)} %maximum_sqrt_fusion) | copy-start | bytes 340
  1029.8 20.7 %copy-start.133 = (f32[1,2,60]{2,1,0:T(2,128)S(1)}, f32[1,2,60]{2,1,0:T(2,128)}, u32[]{:S(2)}) copy-start(f32[1,2,60]{2,1,0:T(2,128)} %param.40) | copy-start | bytes 1444
  1029.8 20.7 %copy-start.143 = (f32[2,60]{1,0:T(2,128)S(1)}, f32[2,60]{1,0:T(2,128)}, u32[]{:S(2)}) copy-start(f32[2,60]{1,0:T(2,128)} %get-tuple-element.504) | copy-start | bytes 1444
  1029.9 22.0 %copy-start.142 = (f32[60]{0:T(128)S(1)}, f32[60]{0:T(128)}, u32[]{:S(2)}) copy-start(f32[60]{0:T(128)} %param.41) | copy-start | bytes 724
  1029.9 22.0 %copy-start.147 = (f32[1,60]{1,0:T(1,128)S(1)}, f32[1,60]{1,0:T(1,128)}, u32[]{:S(2)}) copy-start(f32[1,60]{1,0:T(1,128)} %get-tuple-element.507) | copy-start | bytes 724
  1029.9 22.5 %copy-start.1 = (s32[1,32,32]{2,1,0:T(8,128)S(1)}, s32[1,32,32]{2,1,0:T(8,128)}, u32[]{:S(2)}) copy-start(s32[1,32,32]{2,1,0:T(8,128)} %param.33) | copy-start | bytes 12292
  (119 other events, 418.0 us)

commit v4 on v3

--- a/solution.py
+++ b/solution.py
@@ -198,16 +198,16 @@
     )(*blocks, *extra)
 
 
-def reduce_pieces(shapes):
+def reduce_pieces(shapes, tile):
     out = []
     for a, (rows, cols) in enumerate(shapes):
-        for row in range(0, rows, TILE_R):
+        for row in range(0, rows, tile):
             for col in range(0, cols, TILE_C):
                 out.append((a, row, col, min(TILE_C, cols - col)))
     return out
 
 
-def reduce_kernel(pieces, count, carried, lag, *refs):
+def reduce_kernel(pieces, tile, count, carried, lag, *refs):
     grads = (refs[:count], refs[count : 2 * count])
     outs = refs[2 * count + carried : 3 * count + carried]
     held, from_one, from_two, from_z, mine = refs[3 * count + 2 * carried : 3 * count + 2 * carried + 5]
@@ -225,7 +225,7 @@
 
     def source(p, yo, xo, core):
         a, row, col, cols = pieces[p]
-        return grads[yo][a].at[:, xo, core, pl.ds(row, TILE_R), pl.ds(col, cols)]
+        return grads[yo][a].at[:, xo, core, pl.ds(row, tile), pl.ds(col, cols)]
 
     def cut(ref, p):
         cols = pieces[p][3]
@@ -334,7 +334,7 @@
         total = held[p, y, x, z, :, part].astype(jnp.float32)
         for k in range(3):
             total = total + from_z[p, k, :, part].astype(jnp.float32)
-        outs[a][pl.ds(row, TILE_R), pl.ds(col, cols)] = total
+        outs[a][pl.ds(row, tile), pl.ds(col, cols)] = total
 
     for step in range(many + 3 * lag):
         if carried and step == many // 2:
@@ -353,25 +353,25 @@
         settle(rows, carry_sem.at[4])
 
 
-def reduce_all(grads, name, lag, rows=None):
+def reduce_all(grads, name, lag, rows=None, tile=TILE_R):
     count = len(grads[0])
     shapes = [(g.shape[0] // 16, g.shape[1]) for g in grads[0]]
-    pieces = reduce_pieces(shapes)
+    pieces = reduce_pieces(shapes, tile)
     many = len(pieces)
     views = [g.reshape(4, 2, 2, g.shape[0] // 16, g.shape[1]) for layer in grads for g in layer]
     extra = [] if rows is None else [rows]
     return pl.pallas_call(
-        functools.partial(reduce_kernel, pieces, count, len(extra), lag),
+        functools.partial(reduce_kernel, pieces, tile, count, len(extra), lag),
         out_shape=[jax.ShapeDtypeStruct(s, jnp.float32) for s in shapes]
         + [jax.ShapeDtypeStruct((32,) + e.shape[1:], e.dtype) for e in extra],
         in_specs=[ANYWHERE] * (len(views) + len(extra)),
         out_specs=[IN_VMEM] * count + [ANYWHERE] * len(extra),
         scratch_shapes=[
-            pltpu.VMEM((many, 2, 2, 4, TILE_R, TILE_C), LOW),
-            pltpu.VMEM((many, 2, 4, TILE_R, TILE_C), LOW),
-            pltpu.VMEM((many, 4, TILE_R, TILE_C), LOW),
-            pltpu.VMEM((many, 3, TILE_R, TILE_C), LOW),
-            pltpu.VMEM((2, 2, 2, 4, TILE_R, TILE_C), LOW),
+            pltpu.VMEM((many, 2, 2, 4, tile, TILE_C), LOW),
+            pltpu.VMEM((many, 2, 4, tile, TILE_C), LOW),
+            pltpu.VMEM((many, 4, tile, TILE_C), LOW),
+            pltpu.VMEM((many, 3, tile, TILE_C), LOW),
+            pltpu.VMEM((2, 2, 2, 4, tile, TILE_C), LOW),
         ]
         + [pltpu.SemaphoreType.DMA((many,)) for unused in range(8)]
         + [pltpu.SemaphoreType.DMA((2,)), pltpu.SemaphoreType.DMA((5,))],
@@ -571,7 +571,7 @@
     place = lax.broadcasted_iota(jnp.int32, (tall, asked.shape[1]), 0) + step * tall
     here = dense_nt(rows[...], grad_logits[...]) + dense_nt(got[...], (asked[...] == place).astype(LOW))
     here = here[:width]
-    grad[...] = here
+    grad[...] = here.astype(LOW)
     squares[pl.ds(0, 1)] += leader[0] * squares_of(here)
 
 
@@ -582,7 +582,7 @@
         table_grad_kernel,
         grid=(height // tall,),
         out_shape=[
-            jax.ShapeDtypeStruct((width, height), jnp.float32),
+            jax.ShapeDtypeStruct((width, height), LOW),
             jax.ShapeDtypeStruct((8, 128), jnp.float32),
         ],
         in_specs=[
@@ -637,12 +637,12 @@
                 copy.start()
 
     def one(weight, grad, first, second, decay):
-        return (weight,) + lamb_parts(weight, clip[0] * grad, first, second, decay)
+        return (weight,) + lamb_parts(weight, clip[0] * grad.astype(jnp.float32), first, second, decay)
 
     weight, new_firsts[0][...], new_seconds[0][...], update = one(
         weights[0][...], grads[0][...], firsts[0][...], seconds[0][...], decays[0]
     )
-    updates[0][...] = update
+    updates[0][...] = update.astype(LOW)
     sums[pl.ds(0, 1)] += squares_of(weight)
     sums[pl.ds(8, 1)] += squares_of(update)
 
@@ -669,7 +669,7 @@
             sums[pl.ds(8 + line, 1)] += squares_of(update[part])
 
     for k in range(6):
-        pl.when(step == min(k + 1, 5) % steps)(functools.partial(tensor, k))
+        pl.when(step == (6 + k if k < ROWED else k - 2) % steps)(functools.partial(tensor, k))
 
     @pl.when(step == steps - 1)
     def end():
@@ -690,7 +690,7 @@
         return out
 
     line = [jax.ShapeDtypeStruct(w.shape, jnp.float32) for w in weights]
-    plain = [jax.ShapeDtypeStruct(s, jnp.float32) for s in flat]
+    plain = [jax.ShapeDtypeStruct(s, jnp.float32 if k else LOW) for k, s in enumerate(flat)]
     kept = plain[1 : 1 + ROWED]
     out = pl.pallas_call(
         functools.partial(moments_kernel, decays),
@@ -754,6 +754,181 @@
     return (out[:5], out[5:])
 
 
+EACH = HEADS // KV
+
+
+def turned(x, cosine, sine):
+    half = HD // 2
+    u, w = (x[:half], x[half:])
+    return jnp.concatenate([u * cosine - w * sine, w * cosine + u * sine], axis=0)
+
+
+def query_blocks(scored):
+    if scored:
+        return [(0, scored, ((0, TOK_MB),))]
+    out = [(0, PROMPT, ((0, PROMPT),))]
+    for j in range(NCONT):
+        first = PROMPT + j * CONT
+        out.append((first, CONT, ((0, PROMPT), (first, CONT))))
+    return out
+
+
+def masks(place):
+    out = []
+    for first, count, ranges in query_blocks(0 if place is None else place.shape[1]):
+        keys = sum(r[1] for r in ranges)
+        row = lax.broadcasted_iota(jnp.int32, (keys, count), 0)
+        if place is not None:
+            at = place[pl.ds(0, 1)]
+            seen = (row < PROMPT) | ((row >= place[pl.ds(1, 1)]) & (row <= at))
+        else:
+            seen = row - (keys - count) <= lax.broadcasted_iota(jnp.int32, (keys, count), 1)
+        out.append(jnp.concatenate([jnp.where(seen, 0.0, -1e30)] * EACH, axis=1))
+    return out
+
+
+def rows_of(ranges, array):
+    parts = [array[first : first + count] for first, count in ranges]
+    return parts[0] if len(parts) == 1 else jnp.concatenate(parts, axis=0)
+
+
+def head_rows(start):
+    return pl.ds(pl.multiple_of(start, HD), HD)
+
+
+def side_by_side(ref, group, first, count):
+    return jnp.concatenate(
+        [ref[head_rows((group * EACH + j) * HD), pl.ds(first, count)] for j in range(EACH)], axis=1
+    )
+
+
+def attend_kernel(scored, qkv, cosine, sine, *refs):
+    pick, place = refs[:2] if scored else (None, None)
+    low, out, top, share, *queries = refs[2:] if scored else refs
+    queries = queries[0] if scored else low
+    cos, sin = (cosine[...], sine[...])
+    added = masks(place)
+
+    def group_of(group, carry):
+        key = turned(qkv[head_rows(WIDTH + group * HD)], cos, sin)
+        low[head_rows(WIDTH + group * HD)] = key.astype(LOW)
+        value = qkv[head_rows(WIDTH + KVW + group * HD)].astype(LOW)
+        low[head_rows(WIDTH + KVW + group * HD)] = value
+        for j in range(EACH):
+            place_of = head_rows((group * EACH + j) * HD)
+            query = turned(qkv[place_of], cos, sin).astype(LOW)
+            low[place_of] = query
+            if scored:
+                queries[place_of] = dense_nt(query, pick[...]).astype(LOW)
+        keys = key.T.astype(LOW)
+        for (first, count, ranges), extra in zip(query_blocks(scored), added):
+            query = side_by_side(queries, group, first, count)
+            scores = dense(rows_of(ranges, keys), query) * SCALE + extra
+            high = jnp.max(scores, axis=0, keepdims=True)
+            expo = jnp.exp(scores - high)
+            part = 1.0 / jnp.sum(expo, axis=0, keepdims=True)
+            probs = (expo * part).astype(LOW)
+            got, at = (0.0, 0)
+            for start, length in ranges:
+                got += dense(value[:, start : start + length], probs[at : at + length])
+                at += length
+            for j in range(EACH):
+                column = slice(j * count, (j + 1) * count)
+                out[head_rows((group * EACH + j) * HD), pl.ds(first, count)] = got[:, column].astype(LOW)
+                top[group, j : j + 1, pl.ds(first, count)] = high[:, column]
+                share[group, j : j + 1, pl.ds(first, count)] = part[:, column]
+        return carry
+
+    lax.fori_loop(0, KV, group_of, 0)
+
+
+def attention(qkv, cosine, sine, chosen=()):
+    tokens = qkv.shape[1]
+    scored = chosen[0].shape[0] if chosen else 0
+    count = scored or tokens
+    stat = jax.ShapeDtypeStruct((KV, EACH, count), jnp.float32)
+    heads = jax.ShapeDtypeStruct((WIDTH, count), LOW)
+    results = [jax.ShapeDtypeStruct((WIDTH + 2 * KVW, tokens), LOW), heads, stat, stat]
+    results += [heads] if scored else []
+    return pl.pallas_call(
+        functools.partial(attend_kernel, scored),
+        out_shape=results,
+        in_specs=[IN_VMEM] * (3 + len(chosen)),
+        out_specs=[IN_VMEM] * len(results),
+        compiler_params=pltpu.CompilerParams(vmem_limit_bytes=40 * 2**20),
+    )(qkv, cosine, sine, *chosen)
+
+
+def attend_back_kernel(scored, low, top, share, grad, cosine, sine, *refs):
+    pick, place, queries = refs[:3] if scored else (None, None, low)
+    out, key_sum, value_sum = refs[-3:]
+    cos, sin = (cosine[...], sine[...])
+    added = masks(place)
+    spare = out.shape[0] - WIDTH - 2 * KVW
+    out[pl.ds(WIDTH + 2 * KVW, spare)] = jnp.zeros((spare, out.shape[1]), LOW)
+
+    def group_of(group, carry):
+        key = low[head_rows(WIDTH + group * HD)]
+        value = low[head_rows(WIDTH + KVW + group * HD)]
+        keys = key.astype(jnp.float32).T.astype(LOW)
+        values = value.astype(jnp.float32).T.astype(LOW)
+        for number, ((first, count, ranges), extra) in enumerate(zip(query_blocks(scored), added)):
+            sides = range(EACH)
+            columns = pl.ds(first, count)
+            query = side_by_side(queries, group, first, count)
+            upstream = side_by_side(grad, group, first, count)
+            high = jnp.concatenate([top[group, j : j + 1, columns] for j in sides], axis=1)
+            part = jnp.concatenate([share[group, j : j + 1, columns] for j in sides], axis=1)
+            scores = dense(rows_of(ranges, keys), query) * SCALE + extra
+            probs = jnp.exp(scores - high) * part
+            grad_probs = dense(rows_of(ranges, values), upstream)
+            inner = jnp.sum(grad_probs * probs, axis=0, keepdims=True)
+            grad_scores = (probs * (grad_probs - inner)).astype(LOW)
+            probs = probs.astype(LOW)
+            got, at = (0.0, 0)
+            for start, length in ranges:
+                piece = slice(at, at + length)
+                got += dense(key[:, start : start + length], grad_scores[piece])
+                here = pl.ds(start, length)
+                more_key = dense_nt(query, grad_scores[piece])
+                more_value = dense_nt(upstream, probs[piece])
+                if number == 0 or start > 0:
+                    key_sum[:, here] = more_key
+                    value_sum[:, here] = more_value
+                else:
+                    key_sum[:, here] += more_key
+                    value_sum[:, here] += more_value
+                at += length
+            for j in sides:
+                turn = got[:, j * count : (j + 1) * count] * SCALE
+                where = head_rows((group * EACH + j) * HD)
+                if scored:
+                    high_part = turn.astype(LOW)
+                    rest = (turn - high_part.astype(jnp.float32)).astype(LOW)
+                    turn = dense(high_part, pick[...]) + dense(rest, pick[...])
+                    out[where] = turned(turn, cos, -sin).astype(LOW)
+                else:
+                    past = slice(first, first + count)
+                    out[where, columns] = turned(turn, cos[:, past], -sin[:, past]).astype(LOW)
+        out[head_rows(WIDTH + group * HD)] = turned(key_sum[...] * SCALE, cos, -sin).astype(LOW)
+        out[head_rows(WIDTH + KVW + group * HD)] = value_sum[...].astype(LOW)
+        return carry
+
+    lax.fori_loop(0, KV, group_of, 0)
+
+
+def attention_back(low, top, share, grad, cosine, sine, wide, chosen=()):
+    tokens = low.shape[1]
+    return pl.pallas_call(
+        functools.partial(attend_back_kernel, chosen[0].shape[0] if chosen else 0),
+        out_shape=jax.ShapeDtypeStruct((wide, tokens), LOW),
+        in_specs=[IN_VMEM] * (6 + len(chosen)),
+        out_specs=IN_VMEM,
+        scratch_shapes=[pltpu.VMEM((HD, tokens), jnp.float32)] * 2,
+        compiler_params=pltpu.CompilerParams(vmem_limit_bytes=48 * 2**20),
+    )(low, top, share, grad, cosine, sine, *chosen)
+
+
 def up16(count):
     return -(-count // 16) * 16
 
@@ -791,71 +966,18 @@
     return (scale * inner - x * scale**3 * mean, grad_gain)
 
 
-def rotate(x, cosine, sine):
-    half = x.shape[-1] // 2
-    first, second = (x[..., :half], x[..., half:])
-    return jnp.concatenate(
-        [first * cosine - second * sine, second * cosine + first * sine], axis=-1
-    )
-
-
-def rotate_back(grad, cosine, sine):
-    return rotate(grad, cosine, -sine)
-
-
-def rotary_angles(place):
+def rotary_angles():
+    place = jnp.arange(TOK_MB)
     rotary = jnp.where(place >= PROMPT, PROMPT + (place - PROMPT) % CONT, place).astype(jnp.float32)
     freq = THETA ** (-2.0 * jnp.arange(HD // 2).astype(jnp.float32) / HD)
-    angle = rotary[:, None] * freq[None, :]
-    return (jnp.cos(angle)[:, None, :], jnp.sin(angle)[:, None, :])
-
-
-def may_attend(place):
-    keys = jnp.arange(TOK_MB)
-
-    def segment(p):
-        return jnp.where(p >= PROMPT, 1 + (p - PROMPT) // CONT, 0)
-
-    return (keys[None, :] <= place[:, None]) & (
-        (segment(keys)[None, :] == 0) | (segment(keys)[None, :] == segment(place)[:, None])
-    )
-
-
-def attend(query, key, value, allowed):
-    scores = jnp.einsum("qhgd,khd->hgqk", query, key, preferred_element_type=jnp.float32) * SCALE
-    scores = jnp.where(allowed, scores, -1e30)
-    expo = jnp.exp(scores - jnp.max(scores, axis=-1, keepdims=True))
-    probs = expo / jnp.sum(expo, axis=-1, keepdims=True)
-    out = jnp.einsum("hgqk,khd->qhgd", probs.astype(LOW), value, preferred_element_type=jnp.float32)
-    return (out.reshape(-1, WIDTH).astype(LOW), probs)
-
-
-def attend_back(query, key, value, probs, grad):
-    grad = grad.reshape(-1, KV, HEADS // KV, HD)
-    grad_probs = jnp.einsum("qhgd,khd->hgqk", grad, value, preferred_element_type=jnp.float32)
-    grad_scores = probs * (grad_probs - jnp.sum(grad_probs * probs, axis=-1, keepdims=True))
-    grad_scores = grad_scores.astype(LOW)
-    grad_query = (
-        jnp.einsum("hgqk,khd->qhgd", grad_scores, key, preferred_element_type=jnp.float32) * SCALE
-    )
-    grad_key = (
-        jnp.einsum("hgqk,qhgd->khd", grad_scores, query, preferred_element_type=jnp.float32) * SCALE
-    )
-    grad_value = jnp.einsum(
-        "hgqk,qhgd->khd", probs.astype(LOW), grad, preferred_element_type=jnp.float32
-    )
-    return (grad_query.reshape(-1, HEADS, HD), grad_key, grad_value)
-
-
-def heads_of(q, cosine, sine):
-    return (
-        rotate(q.reshape(-1, HEADS, HD), cosine, sine).astype(LOW).reshape(-1, KV, HEADS // KV, HD)
-    )
-
-
-def keys_values(kv, cosine, sine):
-    key = rotate(kv[:, :KVW].reshape(-1, KV, HD), cosine, sine).astype(LOW)
-    return (key, kv[:, KVW:].reshape(-1, KV, HD).astype(LOW))
+    angle = freq[:, None] * rotary[None, :]
+    return (jnp.cos(angle), jnp.sin(angle))
+
+
+def dense_tt(left, right):
+    return lax.dot_general(
+        left, right, (((0,), (1,)), ((), ())), preferred_element_type=jnp.float32
+    )
 
 
 def mlp(b, w_gu, w_down):
@@ -1011,56 +1133,50 @@
         choose, more = lookup_round(ids, owner, rank, turn, slots, n, vshard)
         here = asked(lax.all_gather(more, BOTH, axis=0))
         here = lax.dynamic_index_in_dim(here, section_index, 0, keepdims=False).reshape(-1)
-        rows = dense(jnp.take(table, jnp.maximum(here, 0), axis=0).astype(LOW), sel).astype(LOW)
+        rows = dense(jnp.take(table_low, jnp.maximum(here, 0), axis=0), sel_wide).astype(LOW)
         got = lax.all_to_all(rows.reshape(n, slots, wide), "fsdp", 0, 0).reshape(n * slots, wide)
         return (turn + 1, total + dense(choose, got))
 
     x0 = lax.while_loop(lambda state: state[0] < turns, fetch_more, (jnp.int32(1), x0))[1]
 
     everyone = jnp.arange(TOK_MB)
-    cosine, sine = rotary_angles(everyone)
-    allowed = may_attend(everyone)
+    cosine, sine = rotary_angles()
     x = x0
     kept = []
     for layer in range(sections - 1):
         scale_a = inverse_rms(x, width)
         a = (x * scale_a * gain_all[layer, 0]).astype(LOW)
-        qkv = dense(a, qkv_all[layer])
-        query = heads_of(qkv[:, :WIDTH], cosine, sine)
-        key, value = keys_values(qkv[:, WIDTH : WIDTH + 2 * KVW], cosine, sine)
-        attended, probs = attend(query, key, value, allowed)
-        attended = dense(attended, sel).astype(LOW)
+        low, attended, top, share = attention(dense_tt(qkv_all[layer], a), cosine, sine)
+        attended = dense_t(attended, sel).astype(LOW)
         mixed = x + dense(attended, out_all[layer])
         scale_b = inverse_rms(mixed, width)
         b = (mixed * scale_b * gain_all[layer, 1]).astype(LOW)
         branch, gate, upper, hidden = mlp(b, gu_all[layer], down_all[layer])
-        kept.append(
-            (x, scale_a, a, query, key, value, probs, attended, mixed, scale_b, b, gate, upper, hidden)
-        )
+        kept.append((x, scale_a, a, low, top, share, attended, mixed, scale_b, b, gate, upper, hidden))
         x = mixed + branch
 
     last = sections - 1
     place = (PROMPT + CONT * jnp.arange(NCONT)[:, None] + scored[0]).reshape(-1)
-    pick = (place[:, None] == everyone[None, :]).astype(LOW)
+    taken = place.shape[0]
+    place = jnp.pad(place, (0, -taken % 128), constant_values=PROMPT)
+    real = jnp.arange(place.shape[0]) < taken
+    pick = ((place[:, None] == everyone[None, :]) & real[:, None]).astype(LOW)
     pick32 = pick.astype(jnp.float32)
-    cosine_s, sine_s = rotary_angles(place)
-    allowed_s = may_attend(place)
+    picking = (pick, jnp.stack([place, PROMPT + (place - PROMPT) // CONT * CONT]))
     scale_last = inverse_rms(x, width)
     a_last = (x * scale_last * gain_all[last, 0]).astype(LOW)
-    qkv_last = qkv_all[last][:, WIDTH : WIDTH + 2 * KVW]
-    key_last, value_last = keys_values(dense(a_last, qkv_last), cosine, sine)
-    a_s = dense(pick, a_last).astype(LOW)
+    low_last, attended_s, top_s, share_s, queries = attention(
+        dense_tt(qkv_all[last], a_last), cosine, sine, picking
+    )
     x_s = jnp.dot(pick32, x, precision=HI)
-    query_s = heads_of(dense(a_s, qkv_all[last][:, :WIDTH]), cosine_s, sine_s)
-    attended_s, probs_s = attend(query_s, key_last, value_last, allowed_s)
-    attended_s = dense(attended_s, sel).astype(LOW)
+    attended_s = dense_t(attended_s, sel).astype(LOW)
     mixed_s = x_s + dense(attended_s, out_all[last])
     scale_s = inverse_rms(mixed_s, width)
     b_s = (mixed_s * scale_s * gain_all[last, 1]).astype(LOW)
     branch_s, gate_s, upper_s, hidden_s = mlp(b_s, gu_all[last], down_all[last])
     y_s = mixed_s + branch_s
     scale_y = inverse_rms(y_s, width)
-    head_in = dense_nt((y_s * scale_y * final_all).astype(LOW), sel_wide).astype(LOW)
+    head_in = dense_nt((y_s * scale_y * final_all).astype(LOW), sel_wide).astype(LOW)[:taken]
 
     if fast:
         rows_all = jnp.concatenate(gather_all([head_in], [(0, 16 * k, 16, k % 2) for k in range(4)], 2))
@@ -1093,12 +1209,12 @@
     )
     if fast:
         halves = [[grad_rows[k * own_rows : (k + 1) * own_rows]] for k in range(sections)]
-        grad_head = reduce_all(halves, 4, 1)[0]
+        grad_head = reduce_all(halves, 4, 1, tile=16)[0]
     else:
         grad_head = lax.psum_scatter(grad_rows, BOTH, scatter_dimension=0, tiled=True)
-    grad_y, grad_final = norm_back(
-        y_s, scale_y, final_all, jnp.dot(grad_head.astype(jnp.float32), sel_wide.astype(jnp.float32), precision=HI), width
-    )
+    grad_head = jnp.pad(grad_head.astype(jnp.float32), ((0, place.shape[0] - taken), (0, 0)))
+    grad_z = jnp.dot(grad_head, sel_wide.astype(jnp.float32), precision=HI)
+    grad_y, grad_final = norm_back(y_s, scale_y, final_all, grad_z, width)
 
     grads = [None] * sections
     g_down, g_gu, grad_b = mlp_back(
@@ -1108,38 +1224,19 @@
     grad_mixed = grad_mid + grad_y
     branch = grad_mixed.astype(LOW)
     g_out = dense_t(attended_s, branch)
-    grad_att = dense_nt(dense_nt(branch, out_all[last]).astype(LOW), sel).astype(LOW)
-    grad_query, grad_key, grad_value = attend_back(query_s, key_last, value_last, probs_s, grad_att)
-    grad_q = rotate_back(grad_query, cosine_s, sine_s).reshape(-1, WIDTH).astype(LOW)
-    grad_kv = jnp.concatenate(
-        [rotate_back(grad_key, cosine, sine).reshape(-1, KVW), grad_value.reshape(-1, KVW)], axis=1
-    ).astype(LOW)
-    g_qkv = dense_t(
-        jnp.concatenate([a_s, a_last], axis=0),
-        jnp.concatenate(
-            [
-                jnp.pad(grad_q, ((0, 0), (0, qkv_wide - WIDTH))),
-                jnp.pad(grad_kv, ((0, 0), (WIDTH, qkv_wide - WIDTH - 2 * KVW))),
-            ],
-            axis=0,
-        ),
-    )
-    grad_a_s = dense_nt(grad_q, qkv_all[last][:, :WIDTH])
-    spread_back = lax.dot_general(
-        pick32,
-        jnp.concatenate([grad_a_s, grad_mixed], axis=1),
-        (((0,), (0,)), ((), ())),
-        precision=HI,
-    )
-    grad_a = dense_nt(grad_kv, qkv_last) + spread_back[:, :wide]
-    grad_in, gain_one = norm_back(x, scale_last, gain_all[last, 0], grad_a, width)
-    upstream = grad_in + spread_back[:, wide:]
+    grad_att = dense_nt(sel, dense_nt(branch, out_all[last]).astype(LOW)).astype(LOW)
+    grad_qkv = attention_back(
+        low_last, top_s, share_s, grad_att, cosine, sine, qkv_wide, picking + (queries,)
+    )
+    g_qkv = dense_tt(a_last, grad_qkv)
+    grad_in, gain_one = norm_back(
+        x, scale_last, gain_all[last, 0], dense_tt(grad_qkv, qkv_all[last]), width
+    )
+    upstream = grad_in + lax.dot_general(pick32, grad_mixed, (((0,), (0,)), ((), ())), precision=HI)
     grads[last] = (g_qkv, g_out, g_gu, g_down, jnp.stack([gain_one, gain_two]))
 
     for layer in range(sections - 2, -1, -1):
-        (x, scale_a, a, query, key, value, probs, attended, mixed, scale_b, b, gate, upper, hidden) = kept[
-            layer
-        ]
+        (x, scale_a, a, low, top, share, attended, mixed, scale_b, b, gate, upper, hidden) = kept[layer]
         g_down, g_gu, grad_b = mlp_back(
             upstream.astype(LOW), b, gate, upper, hidden, gu_all[layer], down_all[layer]
         )
@@ -1147,20 +1244,11 @@
         grad_mixed = grad_mid + upstream
         branch = grad_mixed.astype(LOW)
         g_out = dense_t(attended, branch)
-        grad_att = dense_nt(dense_nt(branch, out_all[layer]).astype(LOW), sel).astype(LOW)
-        grad_query, grad_key, grad_value = attend_back(query, key, value, probs, grad_att)
-        grad_qkv = jnp.concatenate(
-            [
-                rotate_back(grad_query, cosine, sine).reshape(-1, WIDTH),
-                rotate_back(grad_key, cosine, sine).reshape(-1, KVW),
-                grad_value.reshape(-1, KVW),
-                jnp.zeros((TOK_MB, qkv_wide - WIDTH - 2 * KVW), jnp.float32),
-            ],
-            axis=1,
-        ).astype(LOW)
-        g_qkv = dense_t(a, grad_qkv)
+        grad_att = dense_nt(sel, dense_nt(branch, out_all[layer]).astype(LOW)).astype(LOW)
+        grad_qkv = attention_back(low, top, share, grad_att, cosine, sine, qkv_wide)
+        g_qkv = dense_tt(a, grad_qkv)
         grad_in, gain_one = norm_back(
-            x, scale_a, gain_all[layer, 0], dense_nt(grad_qkv, qkv_all[layer]), width
+            x, scale_a, gain_all[layer, 0], dense_tt(grad_qkv, qkv_all[layer]), width
         )
         upstream = grad_in + grad_mixed
         grads[layer] = (g_qkv, g_out, g_gu, g_down, jnp.stack([gain_one, gain_two]))
@@ -1177,11 +1265,11 @@
         choose, more = lookup_round(ids, owner, rank, turn, slots, n, vshard)
         places, got = give(asked(lax.all_gather(more, BOTH, axis=0)), choose)
         place_of = (jnp.arange(vshard)[:, None] == places[None, :]).astype(LOW)
-        new = grad + lax.dot_general(
+        new = grad.astype(jnp.float32) + lax.dot_general(
             got[:, :width], place_of, (((0,), (1,)), ((), ())), preferred_element_type=jnp.float32
         )
         every = squares[1] + jnp.where(leader, jnp.sum(new**2), 0.0)
-        return (turn + 1, new, squares.at[0].set(every))
+        return (turn + 1, new.astype(LOW), squares.at[0].set(every))
 
     def gain_rows(layer):
         rows = jnp.concatenate([grads[layer][4], grad_final[None]], axis=0).reshape(3, n, rp)

time: 1070 us -> 994 us (0.929)
  matrix products: 187 us -> 135 us
  local copies, waits for them, and re-layouts: 76.5 us -> 52.3 us
  other arithmetic: 49.1 us -> 29.2 us
  Pallas kernels: 725 us -> 744 us
    pallas_call x2 -> x6, Pallas kernels: 277 us -> 300 us  [the longest x2 272 us: reduce_all(): pl.pallas_call(functools.partial(reduce_kernel, pieces, tile, count, len(...]
    slice x11 -> x1, local copies, waits for them, and re-layouts: 14.5 us -> 0.67 us  [shards(): dense_nt((y_s * scale_y * final_all).astype(LOW), sel_wide).astype(LOW)]
    dot_general x15 -> x9, matrix products: 39.5 us -> 26.5 us  [dense(): return jnp.dot(left, right, preferred_element_type=jnp.float32)]
    sub x2 -> x0, matrix products: 12.9 us -> none  [attend(): expo = jnp.exp(scores - jnp.max(scores, axis=-1, keepdims=True))]
    dot_general x11 -> x8, matrix products: 54.6 us -> 42.5 us  [dense_nt(): lax.dot_general(left, right, (((1,), (1,)), ((), ())), preferred_element_...]
    unnamed x343 -> x271, local copies, waits for them, and re-layouts: 29.6 us -> 21.6 us
    dot_general x12 -> x8, matrix products: 35.6 us -> 31.1 us  [the longest x6 27.8 us: dense_tt(): lax.dot_general(left, right, (((0,), (1,)), ((), ())), preferred_element_...]
where the time goes in v4:
time: 994 us; the launch traced here: 983 us
  Pallas kernels  744 us (75%)
  matrix products  135 us (14%)
  local copies, waits for them, and re-layouts  52.3 us (5%)
  other arithmetic  29.2 us (3%)
  between operations  20.5 us (2%)
    pallas_call x2, Pallas kernels, reduce_all(): pl.pallas_call(functools.partial(reduce_kernel, pieces, tile, count, len(...  272 us
    pallas_call x2, Pallas kernels, gather_all(): pl.pallas_call(functools.partial(gather_kernel, pieces, len(blocks), len(...  242 us
    pallas_call x4, Pallas kernels, exchange(): pl.pallas_call(functools.partial(exchange_kernel, whole), out_shape=jax.S...  47.2 us
    dot_general x8, matrix products, dense_nt(): lax.dot_general(left, right, (((1,), (1,)), ((), ())), preferred_element_...  42.5 us
    pallas_call x1, Pallas kernels, moments(): pl.pallas_call(functools.partial(moments_kernel, decays), grid=(height //...  36.6 us
    dot_general x9, matrix products, dense_t(): lax.dot_general(left, right, (((0,), (0,)), ((), ())), preferred_element_...  33.9 us
    pallas_call x1, Pallas kernels, table_grad(): pl.pallas_call(table_grad_kernel, grid=(height // tall,), out_shape=[jax....  31.5 us
    dot_general x6, matrix products, dense_tt(): lax.dot_general(left, right, (((0,), (1,)), ((), ())), preferred_element_...  27.8 us

profile of v4, /device:TPU:0, one launch (start us, length us, event | category | flops | bytes accessed | tf_op | source)
XLA Modules:
  0.0 982.8 jit_solution(1267451624792015976)
XLA Ops:
  17.5 12.2 %shard_map.464 = s32[32,8,128]{2,1,0:T(8,128)} custom-call(s32[8,128]{1,0:T(8,128)} %fusion.102.src), custom_call_target="tpu_custom_call" | custom-call | tf_op jit(solution)/shard_map/pallas_call | solution.py:403
  41.8 18.1 %shard_map.465 = (bf16[3072,1024]{1,0:T(8,128)(2,1)}, bf16[768,1024]{1,0:T(8,128)(2,1)S(1)}) custom-call(s32[768,1]{1,0:T(8,128)S(1)} %broadcast_in_dim_reshape.5.asked, bf16[1024,1024]{1,0:T(8,128)(2,1)S(1)} %pad.48.sel, f32[960,3072]{1,0:T(8,128)} %bitcast.228), custom_call_target="tpu_custom_call" | custom-call | tf_op jit(solution)/shard_map/pallas_call | solution.py:457
  61.1 210.1 %shard_map.466 = (bf16[16,64,1664]{2,1,0:T(8,128)(2,1)}, bf16[16,64,1024]{2,1,0:T(8,128)(2,1)}, bf16[16,64,5120]{2,1,0:T(8,128)(2,1)}, bf16[16,160,1024]{2,1,0:T...) custom-call(bf16[64,1664]{1,0:T(8,128)(2,1)} %pad.44.refs_0_, ...), custom_call_target="tpu_custom_call" | custom-call | tf_op jit(solution)/shard_map/pallas_call | solution.py:185
  271.2 3.8 fusion.29
  280.4 4.0 fusion.118.qkv
  284.9 7.7 shard_map.467
  298.5 5.8 fusion.119
  306.0 2.4 copy-done.32
  308.4 6.0 multiply_reduce_fusion.7
  315.0 2.1 fusion.120.qkv
  317.6 4.9 shard_map.468
  326.1 5.7 fusion.117
  336.0 31.5 %shard_map.469 = (bf16[16,64,1024]{2,1,0:T(8,128)(2,1)}, bf16[16,64,1024]{2,1,0:T(8,128)(2,1)}) custom-call(bf16[64,1024]{1,0:T(8,128)(2,1)} %slice.239.refs_0_), custom_call_target="tpu_custom_call" | custom-call | tf_op jit(solution)/shard_map/pallas_call | solution.py:185
  367.5 2.6 pad_maximum_fusion.1
  370.1 24.1 %shard_map.470 = (f32[3072,2048]{1,0:T(8,128)}, f32[1,2048]{1,0:T(1,128)S(1)}, f32[1,2048]{1,0:T(1,128)S(1)}, f32[1,2048]{1,0:T(1,128)S(1)}) custom-call(s32[1,2048]{1,0:T(1,128)S(1)} %copy-done.14, bf16[2048,1024]{1,0:T(8,128)(2,1)S(1)} %bitcast.223, bf16[3072,1024]{1,0:T(8,128)(2,1)} %get-tuple-element.888), custom_call_target="tpu_custom_call" | custom-call | tf_op jit(solution)/shard_map/pallas_call | solution.py:496
  394.9 13.1 %shard_map.471 = f32[16,48,128]{2,1,0:T(8,128)} custom-call(f32[48,128]{1,0:T(8,128)} %reshape.655.src), custom_call_target="tpu_custom_call" | custom-call | tf_op jit(solution)/shard_map/pallas_call | solution.py:403
  408.1 1.9 reshape.656
  410.0 2.1 slice_reduce_fusion
  416.1 25.8 %shard_map.472 = (bf16[3072,2048]{1,0:T(8,128)(2,1)}, bf16[2048,1024]{1,0:T(8,128)(2,1)}) custom-call(s32[1]{0:T(128)} %bitcast.39.section, s32[1,2048]{1,0:T(1,128)} %sub.204.wanted, f32[1,2048]{1,0:T(1,128)} %bitcast.290, f32[1,2048]{1,0:T(1,128)} %div.195.scale, f32[1,2048]{1,0:T(1,128)} %copy-done.72, f32[3072,2048]{1,0:T(8,128)} %get-tuple-element.484.logits, ...), custom_call_target="tpu_custom_call" | custom-call | tf_op jit(solution)/shard_map/pallas_call | solution.py:536
  441.8 2.7 fusion.125
  444.5 36.2 %shard_map.473 = f32[64,1024]{1,0:T(8,128)S(1)} custom-call(bf16[4,2,2,64,1024]{4,3,2,1,0:T(8,128)(2,1)S(1)} %bitcast.226, bf16[4,2,2,64,1024]{4,3,2,1,0:T(8,128)(2,1)S(1)} %bitcast.225), custom_call_target="tpu_custom_call" | custom-call | tf_op jit(solution)/shard_map/pallas_call | solution.py:363
  482.6 4.9 multiply_convert_fusion.7
  487.6 4.2 multiply_reduce_fusion.10
  492.5 4.0 fusion.34.grad
  499.4 5.6 shard_map.474
  505.1 5.7 multiply_reduce_fusion.2
  512.6 10.0 %multiply_convert_fusion.1 = (bf16[512,2560]{1,0:T(8,128)(2,1)}, bf16[512,2560]{1,0:T(8,128)(2,1)}) fusion(f32[512,5120]{1,0:T(8,128)S(1)} %bitcast.244, bf16[2560,1024]{1,0:T(8,128)(2,1)} %bitcast.325, f32[512,1024]{1,0:T(8,128)S(1)} %subtract_add_fusion.1), kind=kOutput, calls=%fused_computation.47 | convolution fusion | flops 2701918208 | bytes 23068672 | tf_op jit(solution)/shard_map/dot_general | solution.py:947
  522.6 11.6 %multiply_reduce_fusion.3 = (bf16[1024]{0:T(1024)(128)(2,1)}, f32[512]{0:T(512)S(1)}, f32[512,1024]{1,0:T(8,128)S(1)}) fusion(f32[512,1024]{1,0:T(8,128)S(1)} %copy-done.61, f32[512]{0:T(512)S(1)} %copy-done.100, f32[1024]{0:T(1024)S(1)} %bitcast.300, bf16[1024,5120]{1,0:T(8,128)(2,1)} %bitcast.319, bf16[512,2560]{1,0:T(8,128)(2,1)} %get-tuple-element.598, ...), kind=kOutput, calls=%fused_computation.65 | convolution fusion | flops 5382339072 | bytes 19933184 | tf_op jit(solution)/shard_map/dot_general | solution.py:947
  536.1 5.5 fusion.31.grad
  545.8 10.1 %shard_map.475 = bf16[1664,512]{1,0:T(8,128)(2,1)S(1)} custom-call(bf16[1600,512]{1,0:T(8,128)(2,1)S(1)} %copy-done.4, f32[5,3,512]{2,1,0:T(4,128)S(1)} %copy-done.16, f32[5,3,512]{2,1,0:T(4,128)S(1)} %copy-done.18, bf16[960,512]{1,0:T(8,128)(2,1)S(1)} %copy-done.10, f32[32,512]{1,0:T(8,128)S(1)} %get-tuple-element.615.cosine, ...), custom_call_target="tpu_custom_call" | custom-call | tf_op jit(solution)/shard_map/pallas_call | solution.py:922
  556.0 4.0 convolution_convert_fusion.7
  560.0 2.7 convolution_convert_fusion.8
  564.0 8.6 convolution_convert_fusion.3
  572.6 5.0 convolution_convert_fusion.5
  578.0 6.2 multiply_reduce_fusion.1
  585.0 5.7 convolution_convert_fusion.6
  590.7 2.1 convolution_convert_fusion.9
  592.9 5.8 convolution_convert_fusion.2
  598.7 4.2 convolution_convert_fusion.4
  605.4 2.3 convolution_convert_fusion.10
  607.7 235.7 %shard_map.476 = (f32[64,1664]{1,0:T(8,128)}, f32[64,1024]{1,0:T(8,128)}, f32[64,5120]{1,0:T(8,128)}, f32[160,1024]{1,0:T(8,128)}, f32[32,128]{1,0:T(8,128)}, /*index=5*/bf16[32,48,1024]{2,1,0:T(8,128)(2,1)}) custom-call(bf16[4,2,2,64,1664]{4,3,2,1,0:T(8,128)(2,1)} %bitcast.253, bf16[4,2,2,64,1024]{4,3,2,1,0:T(8,128)(2,1)} %bitcast.261, ...), custom_call_target="tpu_custom_call" | custom-call | tf_op jit(solution)/shard_map/pallas_call | solution.py:363
  843.5 4.6 copy.122
  848.1 6.4 copy.123
  854.5 31.5 %shard_map.477 = (bf16[960,3072]{1,0:T(8,128)(2,1)}, f32[8,128]{1,0:T(8,128)S(1)}) custom-call(f32[1]{0:T(128)} %bitcast.38.leader, s32[1,1536]{1,0:T(1,128)} %broadcast_in_dim_reshape_squeeze.3.asked, bf16[1024,1536]{1,0:T(8,128)(2,1)} %bitcast.240, bf16[1024,2048]{1,0:T(8,128)(2,1)} %bitcast.239, bf16[3072,2048]{1,0:T(8,128)(2,1)} %get-tuple-element.488.grad_logits, ...), custom_call_target="tpu_custom_call" | custom-call | tf_op jit(solution)/shard_map/pallas_call | solution.py:581
  886.9 9.4 shard_map.478
  901.1 36.6 %shard_map.479 = (f32[960,3072]{1,0:T(8,128)}, f32[60,1,1600]{2,1,0:T(1,128)}, f32[60,1,960]{2,1,0:T(1,128)}, f32[60,1,5120]{2,1,0:T(1,128)}, f32[160,960]{1,0:T...) custom-call(f32[1]{0:T(128)} %bitcast.60.clip, ...), custom_call_target="tpu_custom_call" | custom-call | tf_op jit(solution)/shard_map/pallas_call | solution.py:695
  937.7 12.4 %shard_map.480 = f32[32,16,128]{2,1,0:T(8,128)} custom-call(f32[16,128]{1,0:T(8,128)} %get-tuple-element.498.src), custom_call_target="tpu_custom_call" | custom-call | tf_op jit(solution)/shard_map/pallas_call | solution.py:403
  953.6 19.1 %shard_map.481 = (f32[960,3072]{1,0:T(8,128)}, f32[60,1,1600]{2,1,0:T(1,128)}, f32[60,1,960]{2,1,0:T(1,128)}, f32[60,1,5120]{2,1,0:T(1,128)}, f32[160,960]{1,0:T...) custom-call(f32[5]{0:T(128)} %pad_maximum_fusion.10.scales, ...), custom_call_target="tpu_custom_call" | custom-call | tf_op jit(solution)/shard_map/pallas_call | solution.py:743
  (393 shorter events, 75.2 us)
Async XLA Ops:
  7.2 28.5 %copy-start.46 = (f32[1,60,5120]{2,0,1:T(1,128)S(1)}, f32[1,60,5120]{2,0,1:T(1,128)}, u32[]{:S(2)}) copy-start(f32[1,60,5120]{2,0,1:T(1,128)} %param.38) | copy-start | bytes 3686404
  14.6 256.6 %copy-start.94 = (s32[512]{0:T(512)}, s32[512]{0:T(512)S(1)}, u32[]{:S(2)}) copy-start(s32[512]{0:T(512)S(1)} %get-tuple-element.624) | copy-start | bytes 6148
  33.1 259.5 %copy-start.81 = (s32[960]{0:T(1024)}, s32[960]{0:T(1024)S(1)}, u32[]{:S(2)}) copy-start(s32[960]{0:T(1024)S(1)} %fusion.98) | copy-start | bytes 11524
  41.8 18.1 %copy-start.35 = (bf16[1024,1024]{1,0:T(8,128)(2,1)}, bf16[1024,1024]{1,0:T(8,128)(2,1)S(1)}, u32[]{:S(2)}) copy-start(bf16[1024,1024]{1,0:T(8,128)(2,1)S(1)} %pad.48.sel) | copy-start | bytes 6291460
  278.1 6.4 copy-start.76
  278.1 18.0 %copy-start.79 = (f32[1,1,1024]{2,0,1:T(1,128)}, f32[1,1,1024]{2,0,1:T(1,128)S(1)}, u32[]{:S(2)}) copy-start(f32[1,1,1024]{2,0,1:T(1,128)S(1)} %get-tuple-element.608) | copy-start | bytes 12292
  278.1 36.9 %copy-start.83 = (f32[1,1,1024]{2,0,1:T(1,128)}, f32[1,1,1024]{2,0,1:T(1,128)S(1)}, u32[]{:S(2)}) copy-start(f32[1,1,1024]{2,0,1:T(1,128)S(1)} %get-tuple-element.607) | copy-start | bytes 12292
  284.8 9.2 copy-start.116
  295.5 12.9 %copy-start.60 = (f32[512,1024]{1,0:T(8,128)}, f32[512,1024]{1,0:T(8,128)S(1)}, u32[]{:S(2)}) copy-start(f32[512,1024]{1,0:T(8,128)S(1)} %get-tuple-element.638) | copy-start | bytes 6291460
  296.0 8.3 copy-start.99
  308.4 6.6 copy-start.115
  317.4 7.5 copy-start.97
  317.5 7.5 copy-start.103
  317.6 6.8 copy-start.8
  317.6 6.8 copy-start.23
  317.6 6.8 copy-start.59
  324.4 7.8 slice-start.6
  326.0 165.8 %copy-start.28 = (f32[128,1024]{1,0:T(8,128)}, f32[128,1024]{1,0:T(8,128)S(1)}, u32[]{:S(2)}) copy-start(f32[128,1024]{1,0:T(8,128)S(1)} %get-tuple-element.642) | copy-start | bytes 1572868
  326.1 165.8 %copy-start.74 = (f32[128]{0:T(128)}, f32[128]{0:T(128)S(1)}, u32[]{:S(2)}) copy-start(f32[128]{0:T(128)S(1)} %get-tuple-element.629) | copy-start | bytes 1540
  326.1 6.2 slice-start.7
  370.1 24.1 %copy-start.2 = (bf16[32,64,1024]{2,1,0:T(8,128)(2,1)}, bf16[32,64,1024]{2,1,0:T(8,128)(2,1)S(1)}, u32[]{:S(2)}) copy-start(bf16[32,64,1024]{2,1,0:T(8,128)(2,1)S(1)} %pad_maximum_fusion.1) | copy-start | bytes 12582916
  394.3 18.2 %copy-start.113 = (s32[64]{0:T(128)S(1)}, s32[64]{0:T(128)}, u32[]{:S(2)}) copy-start(s32[64]{0:T(128)} %param.34) | copy-start | bytes 772
  444.5 38.1 %copy-start.31 = (f32[128,5120]{1,0:T(8,128)S(1)}, f32[128,5120]{1,0:T(8,128)}, u32[]{:S(2)}) copy-start(f32[128,5120]{1,0:T(8,128)} %copy-done.30) | copy-start | bytes 7864324
  444.5 43.0 %slice-start = ((s8[10485760]{0:T(1024)(128)(4,1)}), s8[4194304]{0:T(1024)(128)(4,1)S(1)}, s32[]{:S(2)}) async-start(s8[10485760]{0:T(1024)(128)(4,1)} %bitcast.232), calls=%async_computation.3 | async-start | bytes 8388608
  480.8 6.8 slice-start.1
  482.6 9.2 copy-start.47
  499.4 13.1 %slice-start.3 = ((s8[10485760]{0:T(1024)(128)(4,1)}), s8[2097152]{0:T(1024)(128)(4,1)S(1)}, s32[]{:S(2)}) async-start(s8[10485760]{0:T(1024)(128)(4,1)} %bitcast.243), calls=%async_computation.6 | async-start | bytes 4194304
  505.1 7.4 slice-start.4
  505.1 7.4 slice-start.5
  512.5 21.8 %copy-start.39 = (f32[512,1024]{1,0:T(8,128)}, f32[512,1024]{1,0:T(8,128)S(1)}, u32[]{:S(2)}) copy-start(f32[512,1024]{1,0:T(8,128)S(1)} %subtract_add_fusion.1) | copy-start | bytes 6291460
  512.5 10.1 %copy-start.61 = (f32[512,1024]{1,0:T(8,128)S(1)}, f32[512,1024]{1,0:T(8,128)}, u32[]{:S(2)}) copy-start(f32[512,1024]{1,0:T(8,128)} %copy-done.60) | copy-start | bytes 6291460
  512.5 10.1 %copy-start.80 = (f32[1,1,1024]{2,0,1:T(1,128)S(1)}, f32[1,1,1024]{2,0,1:T(1,128)}, u32[]{:S(2)}) copy-start(f32[1,1,1024]{2,0,1:T(1,128)} %copy-done.79) | copy-start | bytes 12292
  512.6 10.1 %copy-start.100 = (f32[512]{0:T(512)S(1)}, f32[512]{0:T(512)}, u32[]{:S(2)}) copy-start(f32[512]{0:T(512)} %copy-done.99) | copy-start | bytes 6148
  522.6 11.7 %copy-start.101 = (f32[512]{0:T(512)S(1)}, f32[512]{0:T(512)}, u32[]{:S(2)}) copy-start(f32[512]{0:T(512)} %get-tuple-element.618) | copy-start | bytes 6148
  545.8 10.1 %copy-start.42 = (f32[512,1024]{1,0:T(8,128)S(1)}, f32[512,1024]{1,0:T(8,128)}, u32[]{:S(2)}) copy-start(f32[512,1024]{1,0:T(8,128)} %get-tuple-element.460) | copy-start | bytes 6291460
  545.8 10.1 %copy-start.77 = (f32[1,1,1024]{2,0,1:T(1,128)S(1)}, f32[1,1,1024]{2,0,1:T(1,128)}, u32[]{:S(2)}) copy-start(f32[1,1,1024]{2,0,1:T(1,128)} %copy-done.76) | copy-start | bytes 12292
  545.8 10.1 %copy-start.88 = (f32[512]{0:T(512)S(1)}, f32[512]{0:T(512)}, u32[]{:S(2)}) copy-start(f32[512]{0:T(512)} %copy-done.87) | copy-start | bytes 6148
  564.0 8.6 copy-start.40
  564.0 8.6 copy-start.57
  578.0 7.0 copy-start.85
  578.0 7.0 copy-start.92
  854.5 31.5 %copy-start.69 = (s32[1,512]{1,0:T(1,128)S(1)}, s32[1,512]{1,0:T(1,128)}, u32[]{:S(2)}) copy-start(s32[1,512]{1,0:T(1,128)} %param.31) | copy-start | bytes 6148
  951.7 21.0 %copy-start.112 = (f32[2,14]{1,0:T(2,128)}, f32[2,14]{1,0:T(2,128)S(1)}, u32[]{:S(2)}) copy-start(f32[2,14]{1,0:T(2,128)S(1)} %maximum_sqrt_fusion) | copy-start | bytes 340
  953.6 19.2 %copy-start.106 = (f32[1,2,60]{2,1,0:T(2,128)S(1)}, f32[1,2,60]{2,1,0:T(2,128)}, u32[]{:S(2)}) copy-start(f32[1,2,60]{2,1,0:T(2,128)} %param.40) | copy-start | bytes 1444
  953.6 19.2 %copy-start.111 = (f32[2,60]{1,0:T(2,128)S(1)}, f32[2,60]{1,0:T(2,128)}, u32[]{:S(2)}) copy-start(f32[2,60]{1,0:T(2,128)} %get-tuple-element.522) | copy-start | bytes 1444
  953.6 20.5 %copy-start.108 = (f32[60]{0:T(128)S(1)}, f32[60]{0:T(128)}, u32[]{:S(2)}) copy-start(f32[60]{0:T(128)} %param.41) | copy-start | bytes 724
  953.6 20.5 %copy-start.114 = (f32[1,60]{1,0:T(1,128)S(1)}, f32[1,60]{1,0:T(1,128)}, u32[]{:S(2)}) copy-start(f32[1,60]{1,0:T(1,128)} %get-tuple-element.525) | copy-start | bytes 724
  953.6 21.0 %copy-start.1 = (s32[1,32,32]{2,1,0:T(8,128)S(1)}, s32[1,32,32]{2,1,0:T(8,128)}, u32[]{:S(2)}) copy-start(s32[1,32,32]{2,1,0:T(8,128)} %param.33) | copy-start | bytes 12292
  (85 other events, 280.3 us)

commit v5 on v4

--- a/solution.py
+++ b/solution.py
@@ -91,14 +91,70 @@
     near = [f + 2 - 4 * x, f + 1 - 2 * c]
     away = [(f + k) % 16 for k in range(1, 16)] if carried else in_line + near
     greet([device(1 - y, z, x, c)] + [(y, peer) for peer in away])
-    for section in range(2):
-        pl.when(y == section)(functools.partial(gather_section, section, pieces, count, carried, *refs))
-
-
-def gather_section(y, pieces, count, carried, *refs):
-    given = count + carried
-    blocks, outs = (refs[:count], refs[given : given + 2 * count])
-    send_sem, recv_sem, sib_sem, own_sem, carry_sem = refs[given + 2 * count + carried :]
+    moved = (refs[:count], refs[count + carried : 3 * count + carried])
+    sems = refs[3 * count + carried + (2 if carried else 0) :][:4]
+
+    def phase(name, p=None):
+        for section in range(2):
+            pl.when(y == section)(functools.partial(gather_section, section, pieces, moved, sems, name, p))
+
+    phase("own")
+    if not carried:
+        for p in range(len(pieces)):
+            phase("line", p)
+        phase("rest")
+        return
+    asked, sel, table = refs[count : count + carried]
+    low, got = refs[3 * count + carried : 3 * count + carried + 2]
+    tiles, lows, total, rows, tile_sem, low_sem, carry_sem = refs[3 * count + carried + 6 :]
+    width, tall = tiles.shape[1:]
+    steps = table.shape[1] // tall
+    columns = [pl.ds(i * tall, tall) for i in range(steps)]
+    eye = lax.broadcasted_iota(jnp.int32, (tall, tall), 0) == lax.broadcasted_iota(jnp.int32, (tall, tall), 1)
+    total[...] = jnp.zeros_like(total)
+    lows[...] = jnp.zeros_like(lows)
+
+    def tile_copy(i):
+        return pltpu.make_async_copy(table.at[:, columns[i]], tiles.at[i % 2], tile_sem.at[i % 2])
+
+    def low_copy(i):
+        return pltpu.make_async_copy(lows.at[i % 2], low.at[columns[i]], low_sem.at[i % 2])
+
+    def tile(i):
+        if i + 1 < steps:
+            tile_copy(i + 1).start()
+        tile_copy(i).wait()
+        if i >= 2:
+            low_copy(i - 2).wait()
+        lows[i % 2, :, pl.ds(0, width)] = dense_nt(eye.astype(LOW), tiles[i % 2].astype(LOW)).astype(LOW)
+        place = lax.broadcasted_iota(jnp.int32, (asked.shape[0], tall), 1) + i * tall
+        total[...] += dense((asked[...] == place).astype(LOW), lows[i % 2])
+        low_copy(i).start()
+
+    tile_copy(0).start()
+    for p in range(len(pieces)):
+        for i in (2 * p, 2 * p + 1):
+            if i < steps:
+                tile(i)
+        if 2 * p + 2 == steps:
+            rows[...] = dense(total[...].astype(LOW), sel[...]).astype(LOW).reshape(rows.shape)
+            for k in range(1, 16):
+                peer = (f + k) % 16
+                send(rows.at[peer], got.at[f], carry_sem.at[0], carry_sem.at[1], (y, peer))
+            pltpu.make_async_copy(rows.at[f], got.at[f], carry_sem.at[2]).start()
+        phase("line", p)
+    phase("rest")
+    low_copy(steps - 2).wait()
+    low_copy(steps - 1).wait()
+    settle(rows.at[pl.ds(0, 15)], carry_sem.at[0])
+    settle(rows.at[pl.ds(0, 15)], carry_sem.at[1])
+    settle(rows.at[0], carry_sem.at[2])
+
+
+def gather_section(y, pieces, moved, sems, name, number):
+    blocks, outs = moved
+    count = len(blocks)
+    send_sem, recv_sem, sib_sem, own_sem = sems
     z, x, c = coords()[1:]
     to_x, to_y, to_sib = (device(y, z, 1 - x, c), device(1 - y, z, x, c), device(y, z, x, 1 - c))
     zs = [(z + k) % 4 for k in range(4)]
@@ -117,7 +173,7 @@
         send(src, there(p, o), send_sem.at[p], sib_sem.at[p] if sib else mark(p, o), peer)
 
     every = range(len(pieces))
-    for p in every:
+    for p in every if name == "own" else ():
         me = (y, z, x)
         push(p, me, to_x, own=True)
         push(p, me, to_y, own=True)
@@ -125,14 +181,6 @@
             push(p, me, device(y, zz, x, c), own=True)
         push(p, me, to_sib, own=True, sib=True)
         pltpu.make_async_copy(part(blocks[pieces[p][0]], p), there(p, me), own_sem).start()
-    if carried:
-        rows, got = (refs[count], refs[given + 2 * count])
-        f = lax.axis_index("fsdp")
-        for k in range(1, 16):
-            peer = (f + k) % 16
-            send(rows.at[peer], got.at[f], carry_sem.at[0], carry_sem.at[1], (y, peer))
-        pltpu.make_async_copy(rows.at[f], got.at[f], carry_sem.at[2]).start()
-
     def from_x(p, zz):
         o = (y, zz, 1 - x)
         settle(there(p, o), mark(p, o))
@@ -147,7 +195,8 @@
             push(p, o, to_x)
         push(p, o, to_sib, sib=True)
 
-    for p in every:
+    if name == "line":
+        p = number
         for zz in zs[1:]:
             o = (y, zz, x)
             settle(there(p, o), mark(p, o))
@@ -156,6 +205,8 @@
             push(p, o, to_sib, sib=True)
         from_x(p, z)
         from_y(p, z)
+    if name != "rest":
+        return
     for p in every:
         for zz in zs[1:]:
             from_x(p, zz)
@@ -171,30 +222,39 @@
         for times in (16, 15):
             settle(outs[a].at[pl.ds(0, times), pl.ds(start, rows_each)], send_sem.at[p])
         settle(outs[a].at[pl.ds(0, 16), pl.ds(start, rows_each)], sib_sem.at[p])
-    if carried:
-        settle(rows.at[pl.ds(0, 15)], carry_sem.at[0])
-        settle(rows.at[pl.ds(0, 15)], carry_sem.at[1])
-        settle(rows.at[0], carry_sem.at[2])
-
-
-def gather_all(blocks, pieces, name, rows=None):
+
+
+def gather_all(blocks, pieces, name, extra=(), slots=0):
     many = len(pieces)
-    extra = [] if rows is None else [rows]
     shapes = [jax.ShapeDtypeStruct((16,) + b.shape, b.dtype) for b in blocks] * 2
-    shapes += [jax.ShapeDtypeStruct(e.shape, e.dtype) for e in extra]
+    scratch = [
+        pltpu.SemaphoreType.DMA((many,)),
+        pltpu.SemaphoreType.DMA((many, 16)),
+        pltpu.SemaphoreType.DMA((many,)),
+        pltpu.SemaphoreType.DMA,
+    ]
+    if extra:
+        (deep, wide), (width, height) = (extra[1].shape, extra[2].shape)
+        shapes += [jax.ShapeDtypeStruct((height, deep), LOW), jax.ShapeDtypeStruct((16, slots, wide), LOW)]
+        tall = tall_of(height)
+        scratch += [
+            pltpu.VMEM((2, width, tall), jnp.float32),
+            pltpu.VMEM((2, tall, deep), LOW),
+            pltpu.VMEM((16 * slots, deep), jnp.float32),
+            pltpu.VMEM((16, slots, wide), LOW),
+            pltpu.SemaphoreType.DMA((2,)),
+            pltpu.SemaphoreType.DMA((2,)),
+            pltpu.SemaphoreType.DMA((3,)),
+        ]
     return pl.pallas_call(
         functools.partial(gather_kernel, pieces, len(blocks), len(extra)),
         out_shape=shapes,
-        in_specs=[ANYWHERE] * (len(blocks) + len(extra)),
+        in_specs=[ANYWHERE] * len(blocks) + [IN_VMEM, IN_VMEM, ANYWHERE][: len(extra)],
         out_specs=[ANYWHERE] * len(shapes),
-        scratch_shapes=[
-            pltpu.SemaphoreType.DMA((many,)),
-            pltpu.SemaphoreType.DMA((many, 16)),
-            pltpu.SemaphoreType.DMA((many,)),
-            pltpu.SemaphoreType.DMA,
-            pltpu.SemaphoreType.DMA((3,)),
-        ],
-        compiler_params=pltpu.CompilerParams(collective_id=name, has_side_effects=True),
+        scratch_shapes=scratch,
+        compiler_params=pltpu.CompilerParams(
+            collective_id=name, has_side_effects=True, vmem_limit_bytes=32 * 2**20
+        ),
     )(*blocks, *extra)
 
 
@@ -207,21 +267,35 @@
     return out
 
 
+RING = 8
+
+
 def reduce_kernel(pieces, tile, count, carried, lag, *refs):
+    many = len(pieces)
+    ring = min(RING, many)
     grads = (refs[:count], refs[count : 2 * count])
-    outs = refs[2 * count + carried : 3 * count + carried]
-    held, from_one, from_two, from_z, mine = refs[3 * count + 2 * carried : 3 * count + 2 * carried + 5]
-    sib_recv, sib_send, recv_one, send_one, recv_two, send_two, recv_z, send_z, own_sem, carry_sem = refs[
-        3 * count + 2 * carried + 5 :
+    at = 2 * count + carried
+    outs = refs[at : at + count]
+    at += count
+    if carried:
+        rows, asked, head_rows_all, grad_logits = refs[2 * count : 2 * count + carried]
+        theirs, got, grad_table, sums = refs[at : at + 4]
+        at += 4
+    held, from_one, from_two, from_z, mine, other = refs[at : at + 6]
+    sib_recv, sib_send, recv_one, send_one, recv_two, send_two, recv_z, send_z, own_sem, other_sem = refs[
+        at + 6 : at + 16
     ]
+    if not carried:
+        theirs = other
     y, z, x, c = coords()
     to_x, to_y, to_sib = (device(y, z, 1 - x, c), device(1 - y, z, x, c), device(y, z, x, 1 - c))
     zs = [(z + k) % 4 for k in range(4)]
-    many = len(pieces)
     f = lax.axis_index("fsdp")
+    me = y * 16 + f
     alike = [(y, (f + k) % 16) for k in range(1, 16)]
-    near = [to_x, to_sib] + [device(y, zz, x, c) for zz in zs[1:]]
-    greet([to_y] + (alike if carried else near))
+    others = [(1 - y, (f + k) % 16) for k in range(16)]
+    near = [to_x, to_y, to_sib] + [device(y, zz, x, c) for zz in zs[1:]]
+    greet(alike + others if carried else near)
 
     def source(p, yo, xo, core):
         a, row, col, cols = pieces[p]
@@ -238,23 +312,158 @@
                     source(p, yo, xo, c), cut(mine.at[p % 2, yo, xo], p), own_sem.at[p % 2]
                 ).start()
 
+    def fetch_other(p):
+        settle(cut(theirs.at[p], p), sib_recv.at[p])
+        if carried:
+            pltpu.make_async_copy(cut(theirs.at[p], p), cut(other.at[p % 2], p), other_sem.at[p % 2]).start()
+
     for p in range(many):
         for yo in range(2):
             for xo in range(2):
                 send(
                     source(p, yo, xo, 1 - c),
-                    cut(held.at[p, yo, xo], p),
+                    cut(theirs.at[p, yo, xo], p),
                     sib_send.at[p],
                     sib_recv.at[p],
                     to_sib,
                 )
         if p == 0:
             fetch(0)
+
+    def store_sum(dst, left, right, p):
+        cols = pl.ds(0, pieces[p][3])
+        dst[:, cols] = (left[:, cols].astype(jnp.float32) + right[:, cols].astype(jnp.float32)).astype(LOW)
+
+    def settle_sends(p):
+        settle(cut(from_one.at[p], p), send_one.at[p])
+        settle(cut(from_two.at[p], p), send_two.at[p])
+        settle(cut(from_z.at[p], p), send_z.at[p])
+
+    def two_cores(p):
+        if p == 0:
+            fetch_other(0)
+        if p + 1 < many:
+            fetch(p + 1)
+            fetch_other(p + 1)
+        if p >= ring:
+            settle_sends(p - ring)
+        settle(cut(mine.at[p % 2], p), own_sem.at[p % 2])
+        if carried:
+            settle(cut(other.at[p % 2], p), other_sem.at[p % 2])
+        right, left, here = (other.at[p % 2] if carried else theirs.at[p], mine.at[p % 2], held.at[p % ring])
+
+        def each(i, carry):
+            where = (i // 8, i // 4 % 2, i % 4)
+            store_sum(here.at[where], left.at[where], right.at[where], p)
+            return carry
+
+        lax.fori_loop(0, 16, each, 0)
+        if p % 2 == 0:
+            send(cut(here.at[1 - y], p), cut(from_one.at[p], p), send_one.at[p], recv_one.at[p], to_y)
+        else:
+            for yo in range(2):
+                send(
+                    cut(here.at[yo, 1 - x], p),
+                    cut(from_one.at[p, yo], p),
+                    send_one.at[p],
+                    recv_one.at[p],
+                    to_x,
+                )
+
+    def first_axis(p):
+        settle(cut(from_one.at[p], p), recv_one.at[p])
+        here = held.at[p % ring]
+
+        def each(i, carry):
+            where = (y, i // 4, i % 4) if p % 2 == 0 else (i // 4, x, i % 4)
+            store_sum(here.at[where], here.at[where], from_one.at[p, i // 4, i % 4], p)
+            return carry
+
+        lax.fori_loop(0, 8, each, 0)
+        src, peer = (here.at[y, 1 - x], to_x) if p % 2 == 0 else (here.at[1 - y, x], to_y)
+        send(cut(src, p), cut(from_two.at[p], p), send_two.at[p], recv_two.at[p], peer)
+
+    def second_axis(p):
+        settle(cut(from_two.at[p], p), recv_two.at[p])
+        here = held.at[p % ring, y, x]
+
+        def each(i, carry):
+            store_sum(here.at[i], here.at[i], from_two.at[p, i], p)
+            return carry
+
+        lax.fori_loop(0, 4, each, 0)
+        for k in range(1, 4):
+            send(
+                cut(here.at[zs[k]], p),
+                cut(from_z.at[p, 3 - k], p),
+                send_z.at[p],
+                recv_z.at[p],
+                device(y, zs[k], x, c),
+            )
+
+    def along_z(p):
+        settle(cut(from_z.at[p], p), recv_z.at[p])
+        a, row, col, cols = pieces[p]
+        part = pl.ds(0, cols)
+        total = held[p % ring, y, x, z, :, part].astype(jnp.float32)
+        for k in range(3):
+            total = total + from_z[p, k, :, part].astype(jnp.float32)
+        outs[a][pl.ds(row, tile), pl.ds(col, cols)] = total
+
+    between = [()] * (many + 3 * lag)
     if carried:
-        rows, got = (refs[2 * count], refs[3 * count + carried])
+        natural, turned_rows, turned_got, tiles, made, squares, carry_sem, tile_sem, made_sem, sum_sem = refs[
+            at + 16 :
+        ]
+        between = carried_work(
+            (me, y, f, to_y, alike, others),
+            (rows, asked, head_rows_all, grad_logits, got, grad_table, sums, outs),
+            (natural, turned_rows, turned_got, tiles, made, squares),
+            (carry_sem, tile_sem, made_sem, sum_sem),
+            many + 3 * lag,
+        )
+    for step in range(many + 3 * lag):
+        for work in between[step]:
+            work()
+        for k, stage in enumerate((two_cores, first_axis, second_axis, along_z)):
+            if 0 <= step - k * lag < many:
+                stage(step - k * lag)
+    for p in range(many):
+        settle(cut(theirs.at[p], p), sib_send.at[p])
+        if p >= many - ring:
+            settle_sends(p)
+    if carried:
+        between[-1]()
+
+
+def carried_work(where, arrays, buffers, sems, steps):
+    me, y, f, to_y, alike, others = where
+    rows, asked, head_rows_all, grad_logits, got, grad_table, sums, outs = arrays
+    natural, turned_rows, turned_got, tiles, made, squares = buffers
+    carry_sem, tile_sem, made_sem, sum_sem = sems
+    height, count = grad_logits.shape
+    width = grad_table.shape[0]
+    slots = rows.shape[1]
+    wide = rows.shape[2]
+    tall = tiles.shape[1]
+    turns = height // tall
+    leader = jnp.where(y == 0, 1.0, 0.0)
+    eye = lax.broadcasted_iota(jnp.int32, (tall, tall), 0) == lax.broadcasted_iota(jnp.int32, (tall, tall), 1)
+
+    def turn(source, target):
+        for k in range(wide // tall):
+            part = pl.ds(k * tall, tall)
+            target[part] = dense_nt(eye.astype(LOW), source[:, part]).astype(LOW)
+
+    def start():
         for peer in alike:
-            send(rows.at[peer[1]], got.at[y * 16 + f], carry_sem.at[0], carry_sem.at[1], peer)
-        pltpu.make_async_copy(rows.at[f], got.at[y * 16 + f], carry_sem.at[2]).start()
+            send(rows.at[peer[1]], got.at[me], carry_sem.at[0], carry_sem.at[1], peer)
+        pltpu.make_async_copy(rows.at[f], got.at[me], carry_sem.at[2]).start()
+        pltpu.make_async_copy(head_rows_all, natural.at[pl.ds(0, count)], carry_sem.at[5]).start()
+
+    def turn_rows():
+        settle(natural.at[pl.ds(0, count)], carry_sem.at[5])
+        turn(natural.at[pl.ds(0, count)], turned_rows)
 
     def pass_on():
         settle(rows.at[pl.ds(0, 15)], carry_sem.at[1])
@@ -262,123 +471,118 @@
         ours = got.at[pl.ds(y * 16, 16)]
         send(ours, ours, carry_sem.at[3], carry_sem.at[4], to_y)
 
-    def y_first(p):
-        return p % 2 == 0
-
-    def add(dst, src, p):
-        cols = pl.ds(0, pieces[p][3])
-        dst[:, cols] = (dst[:, cols].astype(jnp.float32) + src[:, cols].astype(jnp.float32)).astype(LOW)
-
-    def two_cores(p):
-        if p + 1 < many:
-            fetch(p + 1)
-        settle(cut(mine.at[p % 2], p), own_sem.at[p % 2])
-        settle(cut(held.at[p], p), sib_recv.at[p])
-
-        def each(i, carry):
-            yo, xo, zo = (i // 8, i // 4 % 2, i % 4)
-            add(held.at[p, yo, xo, zo], mine.at[p % 2, yo, xo, zo], p)
-            return carry
-
-        lax.fori_loop(0, 16, each, 0)
-        if y_first(p):
-            send(cut(held.at[p, 1 - y], p), cut(from_one.at[p], p), send_one.at[p], recv_one.at[p], to_y)
-        else:
-            for yo in range(2):
-                send(
-                    cut(held.at[p, yo, 1 - x], p),
-                    cut(from_one.at[p, yo], p),
-                    send_one.at[p],
-                    recv_one.at[p],
-                    to_x,
-                )
-
-    def first_axis(p):
-        settle(cut(from_one.at[p], p), recv_one.at[p])
-
-        def each(i, carry):
-            if y_first(p):
-                add(held.at[p, y, i // 4, i % 4], from_one.at[p, i // 4, i % 4], p)
-            else:
-                add(held.at[p, i // 4, x, i % 4], from_one.at[p, i // 4, i % 4], p)
-            return carry
-
-        lax.fori_loop(0, 8, each, 0)
-        if y_first(p):
-            src, peer = (held.at[p, y, 1 - x], to_x)
-        else:
-            src, peer = (held.at[p, 1 - y, x], to_y)
-        send(cut(src, p), cut(from_two.at[p], p), send_two.at[p], recv_two.at[p], peer)
-
-    def second_axis(p):
-        settle(cut(from_two.at[p], p), recv_two.at[p])
-
-        def each(i, carry):
-            add(held.at[p, y, x, i], from_two.at[p, i], p)
-            return carry
-
-        lax.fori_loop(0, 4, each, 0)
-        for k in range(1, 4):
-            send(
-                cut(held.at[p, y, x, zs[k]], p),
-                cut(from_z.at[p, 3 - k], p),
-                send_z.at[p],
-                recv_z.at[p],
-                device(y, zs[k], x, c),
-            )
-
-    def along_z(p):
-        settle(cut(from_z.at[p], p), recv_z.at[p])
-        a, row, col, cols = pieces[p]
-        part = pl.ds(0, cols)
-        total = held[p, y, x, z, :, part].astype(jnp.float32)
-        for k in range(3):
-            total = total + from_z[p, k, :, part].astype(jnp.float32)
-        outs[a][pl.ds(row, tile), pl.ds(col, cols)] = total
-
-    for step in range(many + 3 * lag):
-        if carried and step == many // 2:
-            pass_on()
-        for k, stage in enumerate((two_cores, first_axis, second_axis, along_z)):
-            if 0 <= step - k * lag < many:
-                stage(step - k * lag)
-    for p in range(many):
-        settle(cut(held.at[p], p), sib_send.at[p])
-        settle(cut(from_one.at[p], p), send_one.at[p])
-        settle(cut(from_two.at[p], p), send_two.at[p])
-        settle(cut(from_z.at[p], p), send_z.at[p])
-    if carried:
+    def load_got():
+        settle(rows, carry_sem.at[4])
+        for k in range(32):
+            pltpu.make_async_copy(got.at[k], natural.at[pl.ds(k * slots, slots)], carry_sem.at[5]).start()
+        tile_copy(0).start()
+
+    def turn_got():
+        settle(natural.at[pl.ds(0, 32 * slots)], carry_sem.at[5])
+        turn(natural.at[pl.ds(0, 32 * slots)], turned_got)
+        squares[...] = jnp.zeros_like(squares)
+
+    def tile_copy(i):
+        return pltpu.make_async_copy(grad_logits.at[pl.ds(i * tall, tall)], tiles.at[i % 2], tile_sem.at[i % 2])
+
+    def made_copy(i):
+        return pltpu.make_async_copy(made.at[i % 2], grad_table.at[:, pl.ds(i * tall, tall)], made_sem.at[i % 2])
+
+    def table_tile(i):
+        if i + 1 < turns:
+            tile_copy(i + 1).start()
+        tile_copy(i).wait()
+        if i >= 2:
+            made_copy(i - 2).wait()
+        place = lax.broadcasted_iota(jnp.int32, (tall, asked.shape[1]), 0) + i * tall
+        here = dense_nt(turned_rows[...], tiles[i % 2]) + dense_nt(
+            turned_got[...], (asked[...] == place).astype(LOW)
+        )
+        here = here[:width]
+        made[i % 2] = here.astype(LOW)
+        squares[pl.ds(0, 1)] += leader * squares_of(here)
+        made_copy(i).start()
+
+    def end():
+        gains = outs[-1][...]
+        layers = squares_of(gains[:2]) + leader * squares_of(gains[2:3])
+        for out in outs[:-1]:
+            layers += squares_of(out[...])
+        squares[pl.ds(0, 1)] += layers
+        squares[pl.ds(1, 1)] += layers
+        for peer in alike + others:
+            send(squares, sums.at[me], sum_sem.at[0], sum_sem.at[1], peer)
+        sums[me] = squares[...]
+        made_copy(turns - 2).wait()
+        made_copy(turns - 1).wait()
         settle(rows.at[pl.ds(0, 15)], carry_sem.at[0])
         settle(rows, carry_sem.at[3])
-        settle(rows, carry_sem.at[4])
-
-
-def reduce_all(grads, name, lag, rows=None, tile=TILE_R):
+        settle(sums.at[pl.ds(0, 31)], sum_sem.at[0])
+        settle(sums.at[pl.ds(0, 31)], sum_sem.at[1])
+
+    plan = [[] for unused in range(steps)]
+    plan[0].append(start)
+    plan[3].append(turn_rows)
+    plan[9].append(pass_on)
+    plan[13].append(load_got)
+    plan[14].append(turn_got)
+    for i in range(turns):
+        plan[15 + i * (steps - 16) // turns].append(functools.partial(table_tile, i))
+    return plan + [end]
+
+
+def reduce_all(grads, name, lag, tile=TILE_R, extra=(), width=0):
     count = len(grads[0])
     shapes = [(g.shape[0] // 16, g.shape[1]) for g in grads[0]]
     pieces = reduce_pieces(shapes, tile)
     many = len(pieces)
     views = [g.reshape(4, 2, 2, g.shape[0] // 16, g.shape[1]) for layer in grads for g in layer]
-    extra = [] if rows is None else [rows]
+    results = [jax.ShapeDtypeStruct(s, jnp.float32) for s in shapes]
+    piece = (2, 2, 4, tile, TILE_C)
+    scratch = [
+        pltpu.VMEM((min(RING, many),) + piece, LOW),
+        pltpu.VMEM((many, 2, 4, tile, TILE_C), LOW),
+        pltpu.VMEM((many, 4, tile, TILE_C), LOW),
+        pltpu.VMEM((many, 3, tile, TILE_C), LOW),
+        pltpu.VMEM((2,) + piece, LOW),
+        pltpu.VMEM((2 if extra else many,) + piece, LOW),
+    ]
+    scratch += [pltpu.SemaphoreType.DMA((many,)) for unused in range(8)]
+    scratch += [pltpu.SemaphoreType.DMA((2,)), pltpu.SemaphoreType.DMA((2,))]
+    in_specs, out_specs = ([ANYWHERE] * len(views), [IN_VMEM] * count)
+    if extra:
+        rows, asked, scored_rows, grad_logits = extra
+        slots, wide = rows.shape[1:]
+        height, total = grad_logits.shape
+        tall = tall_of(height)
+        results += [
+            jax.ShapeDtypeStruct((many,) + piece, LOW),
+            jax.ShapeDtypeStruct((32, slots, wide), LOW),
+            jax.ShapeDtypeStruct((width, height), LOW),
+            jax.ShapeDtypeStruct((32, 8, 128), jnp.float32),
+        ]
+        in_specs += [ANYWHERE, IN_VMEM, ANYWHERE, ANYWHERE]
+        out_specs += [ANYWHERE] * 3 + [IN_VMEM]
+        scratch += [
+            pltpu.VMEM((max(total, 32 * slots), wide), LOW),
+            pltpu.VMEM((wide, total), LOW),
+            pltpu.VMEM((wide, 32 * slots), LOW),
+            pltpu.VMEM((2, tall, total), LOW),
+            pltpu.VMEM((2, width, tall), LOW),
+            pltpu.VMEM((8, 128), jnp.float32),
+            pltpu.SemaphoreType.DMA((6,)),
+            pltpu.SemaphoreType.DMA((2,)),
+            pltpu.SemaphoreType.DMA((2,)),
+            pltpu.SemaphoreType.DMA((2,)),
+        ]
     return pl.pallas_call(
         functools.partial(reduce_kernel, pieces, tile, count, len(extra), lag),
-        out_shape=[jax.ShapeDtypeStruct(s, jnp.float32) for s in shapes]
-        + [jax.ShapeDtypeStruct((32,) + e.shape[1:], e.dtype) for e in extra],
-        in_specs=[ANYWHERE] * (len(views) + len(extra)),
-        out_specs=[IN_VMEM] * count + [ANYWHERE] * len(extra),
-        scratch_shapes=[
-            pltpu.VMEM((many, 2, 2, 4, tile, TILE_C), LOW),
-            pltpu.VMEM((many, 2, 4, tile, TILE_C), LOW),
-            pltpu.VMEM((many, 4, tile, TILE_C), LOW),
-            pltpu.VMEM((many, 3, tile, TILE_C), LOW),
-            pltpu.VMEM((2, 2, 2, 4, tile, TILE_C), LOW),
-        ]
-        + [pltpu.SemaphoreType.DMA((many,)) for unused in range(8)]
-        + [pltpu.SemaphoreType.DMA((2,)), pltpu.SemaphoreType.DMA((5,))],
+        out_shape=results,
+        in_specs=in_specs,
+        out_specs=out_specs,
+        scratch_shapes=scratch,
         compiler_params=pltpu.CompilerParams(
-            collective_id=name,
-            has_side_effects=True,
-            vmem_limit_bytes=(12 + 3 * many) * 2**20 if many < 16 else 58 * 2**20,
+            collective_id=name, has_side_effects=True, vmem_limit_bytes=(60 if extra else 32) * 2**20
         ),
     )(*views, *extra)
 
@@ -1108,16 +1312,14 @@
 
     asked_first = asked(notes[:, : n * slots])
     asked_here = lax.dynamic_index_in_dim(asked_first, section_index, 0, keepdims=False).reshape(-1)
-    table_low, rows = padded_table(asked_here, sel_wide, table.T)
-    rows = rows.reshape(n, slots, wide)
-
     blocks = (qkv_block, out_block, gu_block, down_block, gain_block)
     if fast:
-        gathered = gather_all(blocks, WEIGHT_PIECES, 1, rows)
-        got = gathered[10]
-        gathered = (gathered[:5], gathered[5:10])
+        extra = (asked_here[:, None], sel_wide, table.T)
+        *gathered, table_low, got = gather_all(blocks, WEIGHT_PIECES, 1, extra, slots)
+        gathered = (gathered[:5], gathered[5:])
     else:
-        got = lax.all_to_all(rows, "fsdp", 0, 0)
+        table_low, rows = padded_table(asked_here, sel_wide, table.T)
+        got = lax.all_to_all(rows.reshape(n, slots, wide), "fsdp", 0, 0)
         gathered = [lax.all_gather(block, BOTH, axis=0) for block in blocks]
         gathered = [[g[k * n : (k + 1) * n] for g in gathered] for k in range(sections)]
     qkv_all, out_all, gu_all, down_all, gain_all = [
@@ -1268,8 +1470,8 @@
         new = grad.astype(jnp.float32) + lax.dot_general(
             got[:, :width], place_of, (((0,), (1,)), ((), ())), preferred_element_type=jnp.float32
         )
-        every = squares[1] + jnp.where(leader, jnp.sum(new**2), 0.0)
-        return (turn + 1, new.astype(LOW), squares.at[0].set(every))
+        every = lax.psum(jnp.where(leader, jnp.sum(new**2), 0.0), BOTH) + jnp.sum(squares[:, 1, 0])
+        return (turn + 1, new.astype(LOW), squares.at[:, 0].set(every / (sections * n)))
 
     def gain_rows(layer):
         rows = jnp.concatenate([grads[layer][4], grad_final[None]], axis=0).reshape(3, n, rp)
@@ -1281,7 +1483,8 @@
     ]
     if fast:
         rows = dense_t(onehot, grad_x0).astype(LOW).reshape(n, slots, wide)
-        *summed, got = reduce_all(outward, 5, 2, rows)
+        extra = (rows, asked_first.reshape(1, -1), rows_all, grad_logits)
+        *summed, unused, got, grad_table, grad_squares = reduce_all(outward, 5, 2, extra=extra, width=width)
     else:
         summed = [
             lax.psum_scatter(
@@ -1290,17 +1493,18 @@
             for arrays in zip(*outward)
         ]
         got = give(asked_first, onehot)[1]
+        grad_table, grad_squares = table_grad(
+            leader.astype(jnp.float32),
+            asked_first.reshape(-1),
+            got.T,
+            rows_all.T,
+            grad_logits,
+            summed,
+            width,
+        )
+        grad_squares = lax.all_gather(grad_squares, BOTH, axis=0)
     if rdp != rd:
         summed[2] = summed[2].reshape(rp, 2, n, rdp)[:, :, :, :rd].reshape(rp, 2 * n * rd)
-    grad_table, grad_squares = table_grad(
-        leader.astype(jnp.float32),
-        asked_first.reshape(-1),
-        got.reshape(-1, wide).T,
-        rows_all.T,
-        grad_logits,
-        summed,
-        width,
-    )
     grad_table, grad_squares = lax.while_loop(
         lambda state: state[0] < turns, give_more, (jnp.int32(1), grad_table, grad_squares)
     )[1:]
@@ -1310,7 +1514,7 @@
             return exchange(sums, name)
         return lax.all_gather(sums, BOTH, axis=0)
 
-    grad_norm = jnp.sqrt(jnp.sum(everyones(grad_squares, 6)[:, 0, 0]))
+    grad_norm = jnp.sqrt(jnp.sum(grad_squares[:, 0, 0]))
     clip = jnp.minimum(1.0, CLIP / grad_norm)
 
     def views(arrays):

time: 994 us -> 916 us (0.922)
  Pallas kernels: 744 us -> 695 us
  local copies, waits for them, and re-layouts: 52.3 us -> 35.2 us
    pallas_call x2 -> x0, Pallas kernels: 49.6 us -> none  [the longest x1 31.5 us: table_grad(): pl.pallas_call(table_grad_kernel, grid=(height // tall,), out_shape=[jax....]
    pallas_call x4 -> x3, Pallas kernels: 47.2 us -> 35.8 us  [exchange(): pl.pallas_call(functools.partial(exchange_kernel, whole), out_shape=jax.S...]
    reshape x2 -> x0, local copies, waits for them, and re-layouts: 11.1 us -> none  [the longest x1 6.42 us: shards(): rows_all = rows_all.reshape(-1, wide)]
    pallas_call x2, Pallas kernels: 272 us -> 282 us  [reduce_all(): pl.pallas_call(functools.partial(reduce_kernel, pieces, tile, count, len(...]
    unnamed x271 -> x177, local copies, waits for them, and re-layouts: 21.6 us -> 19.9 us
where the time goes in v5:
time: 916 us; the launch traced here: 906 us
  Pallas kernels  695 us (76%)
  matrix products  127 us (14%)
  local copies, waits for them, and re-layouts  35.2 us (4%)
  other arithmetic  26.3 us (3%)
  between operations  20.4 us (2%)
    pallas_call x2, Pallas kernels, reduce_all(): pl.pallas_call(functools.partial(reduce_kernel, pieces, tile, count, len(...  282 us
    pallas_call x2, Pallas kernels, gather_all(): pl.pallas_call(functools.partial(gather_kernel, pieces, len(blocks), len(...  241 us
    dot_general x8, matrix products, dense_nt(): lax.dot_general(left, right, (((1,), (1,)), ((), ())), preferred_element_...  40.7 us
    pallas_call x1, Pallas kernels, moments(): pl.pallas_call(functools.partial(moments_kernel, decays), grid=(height //...  37.2 us
    pallas_call x3, Pallas kernels, exchange(): pl.pallas_call(functools.partial(exchange_kernel, whole), out_shape=jax.S...  35.8 us
    dot_general x9, matrix products, dense_t(): lax.dot_general(left, right, (((0,), (0,)), ((), ())), preferred_element_...  34.5 us
    pallas_call x1, Pallas kernels, logits_back(): pl.pallas_call(functools.partial(logits_back_kernel, height // tall // se...  25.8 us
    pallas_call x1, Pallas kernels, logits_of(): pl.pallas_call(logits_kernel, grid=(height // tall,), out_shape=[jax.Shap...  24.1 us

profile of v5, /device:TPU:0, one launch (start us, length us, event | category | flops | bytes accessed | tf_op | source)
XLA Modules:
  0.0 906.1 jit_solution(11568045876775798272)
XLA Ops:
  17.9 12.2 %shard_map.464 = s32[32,8,128]{2,1,0:T(8,128)} custom-call(s32[8,128]{1,0:T(8,128)} %fusion.102.src), custom_call_target="tpu_custom_call" | custom-call | tf_op jit(solution)/shard_map/pallas_call | solution.py:607
  38.6 203.2 %shard_map.465 = (bf16[16,64,1664]{2,1,0:T(8,128)(2,1)S(1)}, bf16[16,64,1024]{2,1,0:T(8,128)(2,1)S(1)}, bf16[16,64,5120]{2,1,0:T(8,128)(2,1)}, bf16[16,160,1024]...) custom-call(bf16[64,1664]{1,0:T(8,128)(2,1)S(1)} %pad.44.refs_0_, ...), custom_call_target="tpu_custom_call" | custom-call | tf_op jit(solution)/shard_map/pallas_call | solution.py:249
  241.8 2.3 copy-done.8
  244.1 1.8 copy-done.9
  245.9 1.7 copy-done.11
  250.3 3.8 fusion.29
  255.2 2.0 multiply_reduce_fusion.9
  257.4 4.1 fusion.118.qkv
  261.6 8.6 shard_map.466
  273.8 9.4 %fusion.119 = f32[512,5120]{1,0:T(8,128)S(1)} fusion(bf16[1024,5120]{1,0:T(8,128)(2,1)} %bitcast.322, f32[512,1024]{1,0:T(8,128)S(1)} %get-tuple-element.633, f32[1024]{0:T(1024)S(1)} %bitcast.298, f32[512]{0:T(512)S(1)} %get-tuple-element.614), kind=kOutput, calls=%fused_computation.287 | convolution fusion | flops 5370281984 | bytes 23074816 | tf_op jit(solution)/shard_map/dot_general | solution.py:1141
  283.2 1.6 multiply_convert_fusion.2
  284.9 2.4 copy-done.25
  287.3 3.1 multiply_reduce_fusion.7
  290.5 2.1 fusion.120.qkv
  292.6 5.2 shard_map.467
  305.6 38.1 %shard_map.468 = (bf16[16,64,1024]{2,1,0:T(8,128)(2,1)S(1)}, bf16[16,64,1024]{2,1,0:T(8,128)(2,1)S(1)}) custom-call(bf16[64,1024]{1,0:T(8,128)(2,1)S(1)} %slice.244.refs_0_), custom_call_target="tpu_custom_call" | custom-call | tf_op jit(solution)/shard_map/pallas_call | solution.py:249
  344.1 24.1 %shard_map.469 = (f32[3072,2048]{1,0:T(8,128)}, f32[1,2048]{1,0:T(1,128)S(1)}, f32[1,2048]{1,0:T(1,128)S(1)}, f32[1,2048]{1,0:T(1,128)S(1)}) custom-call(s32[1,2048]{1,0:T(1,128)S(1)} %sub.204.wanted, bf16[2048,1024]{1,0:T(8,128)(2,1)S(1)} %bitcast.218, bf16[3072,1024]{1,0:T(8,128)(2,1)} %get-tuple-element.886), custom_call_target="tpu_custom_call" | custom-call | tf_op jit(solution)/shard_map/pallas_call | solution.py:700
  368.9 12.3 %shard_map.470 = f32[16,48,128]{2,1,0:T(8,128)} custom-call(f32[48,128]{1,0:T(8,128)} %reshape.651.src), custom_call_target="tpu_custom_call" | custom-call | tf_op jit(solution)/shard_map/pallas_call | solution.py:607
  381.2 1.9 reshape.652
  383.1 2.1 slice_reduce_fusion.1
  387.3 25.8 %shard_map.471 = (bf16[3072,2048]{1,0:T(8,128)(2,1)}, bf16[2048,1024]{1,0:T(8,128)(2,1)}) custom-call(s32[1]{0:T(128)} %bitcast.37.section, s32[1,2048]{1,0:T(1,128)} %copy-done.7, f32[1,2048]{1,0:T(1,128)} %bitcast.293, f32[1,2048]{1,0:T(1,128)} %div.198.scale, f32[1,2048]{1,0:T(1,128)} %copy-done.65, f32[3072,2048]{1,0:T(8,128)} %get-tuple-element.480.logits, ...), custom_call_target="tpu_custom_call" | custom-call | tf_op jit(solution)/shard_map/pallas_call | solution.py:740
  413.1 2.7 fusion.125
  415.8 36.8 %shard_map.472 = f32[64,1024]{1,0:T(8,128)S(1)} custom-call(bf16[4,2,2,64,1024]{4,3,2,1,0:T(8,128)(2,1)S(1)} %bitcast.221, bf16[4,2,2,64,1024]{4,3,2,1,0:T(8,128)(2,1)S(1)} %bitcast.220), custom_call_target="tpu_custom_call" | custom-call | tf_op jit(solution)/shard_map/pallas_call | solution.py:578
  454.1 4.9 multiply_convert_fusion.7
  459.0 3.7 multiply_reduce_fusion.10
  463.8 2.6 fusion.34.grad
  467.8 5.7 shard_map.473
  473.5 5.3 multiply_reduce_fusion.2
  478.8 3.7 subtract_add_fusion.1
  482.5 10.9 %multiply_convert_fusion.1 = (bf16[512,2560]{1,0:T(8,128)(2,1)S(1)}, bf16[512,2560]{1,0:T(8,128)(2,1)}) fusion(f32[512,5120]{1,0:T(8,128)} %copy-done.25, bf16[2560,1024]{1,0:T(8,128)(2,1)} %bitcast.224, f32[512,1024]{1,0:T(8,128)S(1)} %subtract_add_fusion.1), kind=kOutput, calls=%fused_computation.47 | convolution fusion | flops 2701918208 | bytes 23068672 | tf_op jit(solution)/shard_map/dot_general | solution.py:1151
  493.4 4.0 convolution_convert_fusion.6
  497.5 11.7 %multiply_reduce_fusion.3 = (bf16[1024]{0:T(1024)(128)(2,1)S(1)}, f32[512]{0:T(512)S(1)}, f32[512,1024]{1,0:T(8,128)}) fusion(f32[512,1024]{1,0:T(8,128)S(1)} %copy-done.51, f32[512]{0:T(512)S(1)} %get-tuple-element.614, f32[1024]{0:T(1024)S(1)} %bitcast.299, bf16[1024,5120]{1,0:T(8,128)(2,1)} %bitcast.323, bf16[512,2560]{1,0:T(8,128)(2,1)} %get-tuple-element.593, ...), kind=kOutput, calls=%fused_computation.65 | convolution fusion | flops 5382339072 | bytes 19933184 | tf_op jit(solution)/shard_map/dot_general | solution.py:1151
  509.2 4.1 subtract_add_fusion
  513.3 4.6 fusion.31.grad
  518.0 10.4 %shard_map.474 = bf16[1664,512]{1,0:T(8,128)(2,1)S(1)} custom-call(bf16[1600,512]{1,0:T(8,128)(2,1)S(1)} %copy-done.4, f32[5,3,512]{2,1,0:T(4,128)S(1)} %get-tuple-element.475.top, f32[5,3,512]{2,1,0:T(4,128)S(1)} %get-tuple-element.476.share, bf16[960,512]{1,0:T(8,128)(2,1)S(1)} %fusion.31.grad, f32[32,512]{1,0:T(8,128)S(1)} %get-tuple-element.610.cosine, ...), custom_call_target="tpu_custom_call" | custom-call | tf_op jit(solution)/shard_map/pallas_call | solution.py:1126
  528.4 4.2 multiply_reduce_fusion.1
  534.2 2.7 convolution_convert_fusion.8
  536.8 4.1 convolution_convert_fusion.7
  542.6 6.5 convolution_convert_fusion.5
  549.1 2.1 convolution_convert_fusion.9
  551.2 2.3 convolution_convert_fusion.10
  554.9 8.9 convolution_convert_fusion.3
  563.8 3.9 convolution_convert_fusion.4
  567.7 5.8 convolution_convert_fusion.2
  573.5 245.3 %shard_map.475 = (f32[64,1664]{1,0:T(8,128)}, f32[64,1024]{1,0:T(8,128)}, f32[64,5120]{1,0:T(8,128)}, f32[160,1024]{1,0:T(8,128)}, f32[32,128]{1,0:T(8,128)}, /*...) custom-call(bf16[4,2,2,64,1664]{4,3,2,1,0:T(8,128)(2,1)} %bitcast.25, ...), custom_call_target="tpu_custom_call" | custom-call | tf_op jit(solution)/shard_map/pallas_call | solution.py:578
  823.5 37.2 %shard_map.476 = (f32[960,3072]{1,0:T(8,128)}, f32[60,1,1600]{2,1,0:T(1,128)}, f32[60,1,960]{2,1,0:T(1,128)}, f32[60,1,5120]{2,1,0:T(1,128)}, f32[160,960]{1,0:T...) custom-call(f32[1]{0:T(128)} %bitcast.55.clip, ...), custom_call_target="tpu_custom_call" | custom-call | tf_op jit(solution)/shard_map/pallas_call | solution.py:899
  860.7 11.2 %shard_map.477 = f32[32,16,128]{2,1,0:T(8,128)} custom-call(f32[16,128]{1,0:T(8,128)} %get-tuple-element.493.src), custom_call_target="tpu_custom_call" | custom-call | tf_op jit(solution)/shard_map/pallas_call | solution.py:607
  878.7 19.0 %shard_map.478 = (f32[960,3072]{1,0:T(8,128)}, f32[60,1,1600]{2,1,0:T(1,128)}, f32[60,1,960]{2,1,0:T(1,128)}, f32[60,1,5120]{2,1,0:T(1,128)}, f32[160,960]{1,0:T...) custom-call(f32[5]{0:T(128)} %pad_maximum_fusion.10.scales, ...), custom_call_target="tpu_custom_call" | custom-call | tf_op jit(solution)/shard_map/pallas_call | solution.py:947
  (294 shorter events, 53.7 us)
Async XLA Ops:
  7.2 27.1 %copy-start.55 = (f32[1,60,960]{2,0,1:T(1,128)S(1)}, f32[1,60,960]{2,0,1:T(1,128)}, u32[]{:S(2)}) copy-start(f32[1,60,960]{2,0,1:T(1,128)} %param.37) | copy-start | bytes 691204
  14.1 236.3 %copy-start.66 = (s32[512]{0:T(512)}, s32[512]{0:T(512)S(1)}, u32[]{:S(2)}) copy-start(s32[512]{0:T(512)S(1)} %get-tuple-element.619) | copy-start | bytes 6148
  31.9 312.3 %copy-start.7 = (s32[1,2048]{1,0:T(1,128)}, s32[1,2048]{1,0:T(1,128)S(1)}, u32[]{:S(2)}) copy-start(s32[1,2048]{1,0:T(1,128)S(1)} %sub.204.wanted) | copy-start | bytes 24580
  38.6 203.2 %copy-start.28 = (bf16[1024,1024]{1,0:T(8,128)(2,1)}, bf16[1024,1024]{1,0:T(8,128)(2,1)S(1)}, u32[]{:S(2)}) copy-start(bf16[1024,1024]{1,0:T(8,128)(2,1)S(1)} %pad.48.refs_6_) | copy-start | bytes 6291460
  255.2 6.4 copy-start.58
  255.2 6.4 copy-start.60
  255.2 6.4 copy-start.62
  272.4 14.9 %slice-start = ((s8[5242880]{0:T(1024)(128)(4,1)}), s8[4194304]{0:T(1024)(128)(4,1)S(1)}, s32[]{:S(2)}) async-start(s8[5242880]{0:T(1024)(128)(4,1)} %bitcast.225), calls=%async_computation.3 | async-start | bytes 8388608
  273.7 11.1 %copy-start.50 = (f32[512,1024]{1,0:T(8,128)}, f32[512,1024]{1,0:T(8,128)S(1)}, u32[]{:S(2)}) copy-start(f32[512,1024]{1,0:T(8,128)S(1)} %get-tuple-element.633) | copy-start | bytes 6291460
  273.8 13.5 %slice-start.1 = ((s8[5242880]{0:T(1024)(128)(4,1)}), s8[1048576]{0:T(1024)(128)(4,1)S(1)}, s32[]{:S(2)}) async-start(s8[5242880]{0:T(1024)(128)(4,1)} %bitcast.225), calls=%async_computation.4 | async-start | bytes 2097152
  283.2 4.1 copy-start.25
  290.4 8.9 copy-start.29
  290.4 9.9 %slice-start.2 = ((s8[10485760]{0:T(1024)(128)(4,1)}), s8[4194304]{0:T(1024)(128)(4,1)S(1)}, s32[]{:S(2)}) async-start(s8[10485760]{0:T(1024)(128)(4,1)} %bitcast.238), calls=%async_computation.5 | async-start | bytes 8388608
  290.5 9.9 %slice-start.3 = ((s8[10485760]{0:T(1024)(128)(4,1)}), s8[4194304]{0:T(1024)(128)(4,1)S(1)}, s32[]{:S(2)}) async-start(s8[10485760]{0:T(1024)(128)(4,1)} %bitcast.238), calls=%async_computation.6 | async-start | bytes 8388608
  292.6 7.8 slice-start.4
  300.3 162.4 %copy-start.21 = (f32[128,1024]{1,0:T(8,128)}, f32[128,1024]{1,0:T(8,128)S(1)}, u32[]{:S(2)}) copy-start(f32[128,1024]{1,0:T(8,128)S(1)} %get-tuple-element.637) | copy-start | bytes 1572868
  303.7 40.4 %copy-start.37 = (f32[128,1024]{1,0:T(8,128)}, f32[128,1024]{1,0:T(8,128)S(1)}, u32[]{:S(2)}) copy-start(f32[128,1024]{1,0:T(8,128)S(1)} %get-tuple-element.639) | copy-start | bytes 1572868
  344.1 24.1 %copy-start.2 = (bf16[32,64,1024]{2,1,0:T(8,128)(2,1)}, bf16[32,64,1024]{2,1,0:T(8,128)(2,1)S(1)}, u32[]{:S(2)}) copy-start(bf16[32,64,1024]{2,1,0:T(8,128)(2,1)S(1)} %pad_maximum_fusion.1) | copy-start | bytes 12582916
  413.1 39.6 %copy-start.38 = (f32[128,1024]{1,0:T(8,128)S(1)}, f32[128,1024]{1,0:T(8,128)}, u32[]{:S(2)}) copy-start(f32[128,1024]{1,0:T(8,128)} %copy-done.37) | copy-start | bytes 1572868
  415.8 36.9 %copy-start.19 = (bf16[960,1024]{1,0:T(8,128)(2,1)S(1)}, bf16[960,1024]{1,0:T(8,128)(2,1)}, u32[]{:S(2)}) copy-start(bf16[960,1024]{1,0:T(8,128)(2,1)} %copy-done.17) | copy-start | bytes 5898244
  415.8 38.2 %copy-start.24 = (f32[128,5120]{1,0:T(8,128)S(1)}, f32[128,5120]{1,0:T(8,128)}, u32[]{:S(2)}) copy-start(f32[128,5120]{1,0:T(8,128)} %copy-done.23) | copy-start | bytes 7864324
  415.8 43.2 %slice-start.5 = ((s8[10485760]{0:T(1024)(128)(4,1)}), s8[4194304]{0:T(1024)(128)(4,1)S(1)}, s32[]{:S(2)}) async-start(s8[10485760]{0:T(1024)(128)(4,1)} %bitcast.241), calls=%async_computation.8 | async-start | bytes 8388608
  452.7 6.3 slice-start.6
  454.1 8.7 copy-start.40
  454.1 4.9 slice-start.7
  467.8 5.7 copy-start.13
  473.5 5.3 copy-start.42
  482.5 10.9 %copy-start.31 = (f32[512,1024]{1,0:T(8,128)}, f32[512,1024]{1,0:T(8,128)S(1)}, u32[]{:S(2)}) copy-start(f32[512,1024]{1,0:T(8,128)S(1)} %subtract_add_fusion.1) | copy-start | bytes 6291460
  482.5 10.9 %copy-start.30 = (f32[512,1024]{1,0:T(8,128)S(1)}, f32[512,1024]{1,0:T(8,128)}, u32[]{:S(2)}) copy-start(f32[512,1024]{1,0:T(8,128)} %copy-done.29) | copy-start | bytes 6291460
  497.5 11.8 %copy-start.32 = (f32[512,1024]{1,0:T(8,128)S(1)}, f32[512,1024]{1,0:T(8,128)}, u32[]{:S(2)}) copy-start(f32[512,1024]{1,0:T(8,128)} %copy-done.31) | copy-start | bytes 6291460
  513.3 4.7 copy-start.4
  518.0 10.4 %copy-start.10 = (bf16[16,64,1664]{2,1,0:T(8,128)(2,1)S(1)}, bf16[16,64,1664]{2,1,0:T(8,128)(2,1)}, u32[]{:S(2)}) copy-start(bf16[16,64,1664]{2,1,0:T(8,128)(2,1)} %copy-done.9) | copy-start | bytes 10223620
  528.4 4.2 copy-start.20
  528.4 4.2 copy-start.35
  528.4 4.2 copy-start.36
  536.8 5.8 copy-start.33
  542.6 6.5 copy-start.43
  542.6 6.5 copy-start.54
  554.9 8.9 copy-start.27
  554.9 8.9 copy-start.41
  573.5 245.3 %copy-start.57 = (s32[1,512]{1,0:T(1,128)S(1)}, s32[1,512]{1,0:T(1,128)}, u32[]{:S(2)}) copy-start(s32[1,512]{1,0:T(1,128)} %param.31) | copy-start | bytes 6148
  573.5 245.3 %copy-start.59 = (s32[512]{0:T(512)S(1)}, s32[512]{0:T(512)}, u32[]{:S(2)}) copy-start(s32[512]{0:T(512)} %copy-done.58) | copy-start | bytes 6148
  573.5 245.3 %copy-start.61 = (s32[512]{0:T(512)S(1)}, s32[512]{0:T(512)}, u32[]{:S(2)}) copy-start(s32[512]{0:T(512)} %copy-done.60) | copy-start | bytes 6148
  573.5 245.3 %copy-start.63 = (s32[512,1]{0,1:T(1,128)S(1)}, s32[512,1]{0,1:T(1,128)}, u32[]{:S(2)}) copy-start(s32[512,1]{0,1:T(1,128)} %copy-done.62) | copy-start | bytes 6148
  823.5 50.2 %copy-start.68 = (f32[1,2,60]{2,1,0:T(2,128)S(1)}, f32[1,2,60]{2,1,0:T(2,128)}, u32[]{:S(2)}) copy-start(f32[1,2,60]{2,1,0:T(2,128)} %param.40) | copy-start | bytes 1444
  823.5 52.8 %copy-start.69 = (f32[60]{0:T(128)S(1)}, f32[60]{0:T(128)}, u32[]{:S(2)}) copy-start(f32[60]{0:T(128)} %param.41) | copy-start | bytes 724
  873.6 24.2 %copy-start.70 = (f32[2,14]{1,0:T(2,128)}, f32[2,14]{1,0:T(2,128)S(1)}, u32[]{:S(2)}) copy-start(f32[2,14]{1,0:T(2,128)S(1)} %maximum_sqrt_fusion) | copy-start | bytes 340
  878.7 19.1 %copy-start.1 = (s32[1,32,32]{2,1,0:T(8,128)S(1)}, s32[1,32,32]{2,1,0:T(8,128)}, u32[]{:S(2)}) copy-start(s32[1,32,32]{2,1,0:T(8,128)} %param.33) | copy-start | bytes 12292
  (38 other events, 91.3 us)

commit v6 on v5

--- a/solution.py
+++ b/solution.py
@@ -91,19 +91,24 @@
     near = [f + 2 - 4 * x, f + 1 - 2 * c]
     away = [(f + k) % 16 for k in range(1, 16)] if carried else in_line + near
     greet([device(1 - y, z, x, c)] + [(y, peer) for peer in away])
+    if not carried:
+        outs = [ref.at[pl.ds(section * 16, 16)] for section in range(2) for ref in refs[count : 2 * count]]
+
+        def everything(section):
+            for name, p in [("own", None)] + [("line", p) for p in range(len(pieces))] + [("rest", None)]:
+                gather_section(section, pieces, (refs[:count], outs), refs[2 * count :], name, p)
+
+        for section in range(2):
+            pl.when(y == section)(functools.partial(everything, section))
+        return
     moved = (refs[:count], refs[count + carried : 3 * count + carried])
-    sems = refs[3 * count + carried + (2 if carried else 0) :][:4]
+    sems = refs[3 * count + carried + 2 :][:4]
 
     def phase(name, p=None):
         for section in range(2):
             pl.when(y == section)(functools.partial(gather_section, section, pieces, moved, sems, name, p))
 
     phase("own")
-    if not carried:
-        for p in range(len(pieces)):
-            phase("line", p)
-        phase("rest")
-        return
     asked, sel, table = refs[count : count + carried]
     low, got = refs[3 * count + carried : 3 * count + carried + 2]
     tiles, lows, total, rows, tile_sem, low_sem, carry_sem = refs[3 * count + carried + 6 :]
@@ -226,7 +231,8 @@
 
 def gather_all(blocks, pieces, name, extra=(), slots=0):
     many = len(pieces)
-    shapes = [jax.ShapeDtypeStruct((16,) + b.shape, b.dtype) for b in blocks] * 2
+    shapes = [jax.ShapeDtypeStruct((16 if extra else 32,) + b.shape, b.dtype) for b in blocks]
+    shapes = shapes * 2 if extra else shapes
     scratch = [
         pltpu.SemaphoreType.DMA((many,)),
         pltpu.SemaphoreType.DMA((many, 16)),
@@ -253,7 +259,7 @@
         out_specs=[ANYWHERE] * len(shapes),
         scratch_shapes=scratch,
         compiler_params=pltpu.CompilerParams(
-            collective_id=name, has_side_effects=True, vmem_limit_bytes=32 * 2**20
+            collective_id=name, has_side_effects=True, vmem_limit_bytes=32 * 2**20 if extra else None
         ),
     )(*blocks, *extra)
 
@@ -273,8 +279,11 @@
 def reduce_kernel(pieces, tile, count, carried, lag, *refs):
     many = len(pieces)
     ring = min(RING, many)
-    grads = (refs[:count], refs[count : 2 * count])
-    at = 2 * count + carried
+    if carried:
+        grads = (refs[:count], refs[count : 2 * count])
+    else:
+        grads = [[ref.at[section] for ref in refs[:count]] for section in range(2)]
+    at = 2 * count + carried if carried else count
     outs = refs[at : at + count]
     at += count
     if carried:
@@ -532,11 +541,15 @@
 
 
 def reduce_all(grads, name, lag, tile=TILE_R, extra=(), width=0):
-    count = len(grads[0])
-    shapes = [(g.shape[0] // 16, g.shape[1]) for g in grads[0]]
+    first = grads[0] if extra else grads
+    count = len(first)
+    shapes = [(g.shape[0] // (16 if extra else 32), g.shape[1]) for g in first]
     pieces = reduce_pieces(shapes, tile)
     many = len(pieces)
-    views = [g.reshape(4, 2, 2, g.shape[0] // 16, g.shape[1]) for layer in grads for g in layer]
+    if extra:
+        views = [g.reshape(4, 2, 2, g.shape[0] // 16, g.shape[1]) for layer in grads for g in layer]
+    else:
+        views = [g.reshape(2, 4, 2, 2, *s) for g, s in zip(grads, shapes)]
     results = [jax.ShapeDtypeStruct(s, jnp.float32) for s in shapes]
     piece = (2, 2, 4, tile, TILE_C)
     scratch = [
@@ -614,8 +627,10 @@
     )(small)
 
 
-def tall_of(height, sections=2):
-    return 256 if height % (256 * sections) == 0 else 128
+def tall_of(height, sections=2, most=256):
+    while height % (most * sections):
+        most //= 2
+    return most
 
 
 def whole(shape):
@@ -695,7 +710,7 @@
 def logits_of(wanted, rows, table):
     height, wide = table.shape
     count = rows.shape[0]
-    tall = tall_of(height)
+    tall = tall_of(height, most=512 if count <= 2048 else 256)
     line = jax.ShapeDtypeStruct((1, count), jnp.float32)
     return pl.pallas_call(
         logits_kernel,
@@ -733,7 +748,7 @@
 def logits_back(section, wanted, top, scale, push, logits, table, sections):
     height, wide = table.shape
     count = logits.shape[1]
-    tall = tall_of(height, sections)
+    tall = tall_of(height, sections, 512)
     block = min(count, 2048)
     line = pl.BlockSpec((1, block), lambda j, i: (0, j))
     tile = pl.BlockSpec((tall, block), lambda j, i: (i, j))
@@ -811,6 +826,7 @@
 
 
 ROWED = 3
+BAND = 160
 SPREAD = (1, 3)
 
 
@@ -873,7 +889,7 @@
             sums[pl.ds(8 + line, 1)] += squares_of(update[part])
 
     for k in range(6):
-        pl.when(step == (6 + k if k < ROWED else k - 2) % steps)(functools.partial(tensor, k))
+        pl.when(step == (steps // 2 + k if k < ROWED else k - 2) % steps)(functools.partial(tensor, k))
 
     @pl.when(step == steps - 1)
     def end():
@@ -884,11 +900,11 @@
 
 def moments(clip, sel, weights, grads, firsts, seconds, decays):
     width, height = weights[0].shape
-    tall = tall_of(height)
+    band = pl.BlockSpec((BAND, height), lambda i: (i, 0))
     flat = [w.shape if w.ndim == 2 else w.shape[::2] for w in weights]
 
     def specs(arrays, results=False):
-        out = [lined(width, tall)]
+        out = [band]
         for a in arrays[1:]:
             out.append(ANYWHERE if a.ndim == 3 else whole(a.shape))
         return out
@@ -898,7 +914,7 @@
     kept = plain[1 : 1 + ROWED]
     out = pl.pallas_call(
         functools.partial(moments_kernel, decays),
-        grid=(height // tall,),
+        grid=(width // BAND,),
         out_shape=line * 2 + plain + kept + [jax.ShapeDtypeStruct((16, 128), jnp.float32)],
         in_specs=[pl.BlockSpec(memory_space=pltpu.SMEM), whole(sel.shape)]
         + specs(weights)
@@ -942,11 +958,10 @@
 
 def apply_updates(scales, weights, updates, shapes):
     width, height = weights[0].shape
-    tall = tall_of(height)
-    plain = [lined(width, tall)] + [whole(w.shape) for w in weights[1:]]
+    plain = [pl.BlockSpec((BAND, height), lambda i: (i, 0))] + [whole(w.shape) for w in weights[1:]]
     out = pl.pallas_call(
         apply_kernel,
-        grid=(height // tall,),
+        grid=(width // BAND,),
         out_shape=[jax.ShapeDtypeStruct(s, jnp.float32) for s in shapes]
         + [jax.ShapeDtypeStruct(w.shape, LOW) for w in weights],
         in_specs=[pl.BlockSpec(memory_space=pltpu.SMEM)] + plain * 2,
@@ -1381,21 +1396,21 @@
     head_in = dense_nt((y_s * scale_y * final_all).astype(LOW), sel_wide).astype(LOW)[:taken]
 
     if fast:
-        rows_all = jnp.concatenate(gather_all([head_in], [(0, 16 * k, 16, k % 2) for k in range(4)], 2))
+        rows_all = gather_all([head_in], [(0, 16 * k, 16, k % 2) for k in range(4)], 2)[0]
     else:
         rows_all = lax.all_gather(head_in, BOTH, axis=0)
     rows_all = rows_all.reshape(-1, wide)
     own_rows = rows_all.shape[0] // sections
     wanted_here = wanted_rows - vstart
     logits, top_here, total_here, target_here = logits_of(wanted_here, rows_all, table_low)
-    stats = jnp.concatenate([top_here, total_here, target_here])
+    stats = jnp.concatenate([top_here + jnp.log(total_here), target_here])
     if fast:
-        stats = exchange(stats.reshape(-1, 128), 3, whole=False).reshape(n, 3, -1)
+        stats = exchange(stats.reshape(-1, 128), 3, whole=False).reshape(n, 2, -1)
     else:
         stats = lax.all_gather(stats, "fsdp", axis=0)
     top = jnp.max(stats[:, 0], axis=0)
-    total = jnp.sum(stats[:, 1] * jnp.exp(stats[:, 0] - top), axis=0)
-    row_logp = jnp.sum(stats[:, 2], axis=0) - top - jnp.log(total)
+    total = jnp.sum(jnp.exp(stats[:, 0] - top), axis=0)
+    row_logp = jnp.sum(stats[:, 1], axis=0) - top - jnp.log(total)
     seq = jnp.sum(row_logp.reshape(-1, SCORED), axis=1)
     pair = pairs.reshape(-1, 2)
     conts = jnp.arange(seq.shape[0])
@@ -1410,8 +1425,7 @@
         section_index, wanted_here, top, grad_row / total, grad_row, logits, table_low, sections
     )
     if fast:
-        halves = [[grad_rows[k * own_rows : (k + 1) * own_rows]] for k in range(sections)]
-        grad_head = reduce_all(halves, 4, 1, tile=16)[0]
+        grad_head = reduce_all([grad_rows], 4, 1, tile=16)[0]
     else:
         grad_head = lax.psum_scatter(grad_rows, BOTH, scatter_dimension=0, tiled=True)
     grad_head = jnp.pad(grad_head.astype(jnp.float32), ((0, place.shape[0] - taken), (0, 0)))

time: 916 us -> 902 us (0.985)
  Pallas kernels: 695 us -> 683 us
    unnamed x177 -> x181, local copies, waits for them, and re-layouts: 19.9 us -> 23.5 us
where the time goes in v6:
time: 902 us; the launch traced here: 892 us
  Pallas kernels  683 us (76%)
  matrix products  127 us (14%)
  local copies, waits for them, and re-layouts  35.9 us (4%)
  other arithmetic  24.1 us (3%)
  between operations  20.4 us (2%)
    pallas_call x2, Pallas kernels, reduce_all(): pl.pallas_call(functools.partial(reduce_kernel, pieces, tile, count, len(...  281 us
    pallas_call x2, Pallas kernels, gather_all(): pl.pallas_call(functools.partial(gather_kernel, pieces, len(blocks), len(...  243 us
    dot_general x8, matrix products, dense_nt(): lax.dot_general(left, right, (((1,), (1,)), ((), ())), preferred_element_...  40.6 us
    pallas_call x1, Pallas kernels, moments(): pl.pallas_call(functools.partial(moments_kernel, decays), grid=(width //...  35.1 us
    dot_general x9, matrix products, dense_t(): lax.dot_general(left, right, (((0,), (0,)), ((), ())), preferred_element_...  34.4 us
    pallas_call x3, Pallas kernels, exchange(): pl.pallas_call(functools.partial(exchange_kernel, whole), out_shape=jax.S...  33.8 us
    dot_general x6, matrix products, dense_tt(): lax.dot_general(left, right, (((0,), (1,)), ((), ())), preferred_element_...  23.7 us
    unnamed x181, local copies, waits for them, and re-layouts  23.5 us

profile of v6, /device:TPU:0, one launch (start us, length us, event | category | flops | bytes accessed | tf_op | source)
XLA Modules:
  0.0 892.5 jit_solution(12589639076933576664)
XLA Ops:
  17.9 12.2 %shard_map.464 = s32[32,8,128]{2,1,0:T(8,128)} custom-call(s32[8,128]{1,0:T(8,128)} %fusion.100.src), custom_call_target="tpu_custom_call" | custom-call | tf_op jit(solution)/shard_map/pallas_call | solution.py:620
  38.6 203.2 %shard_map.465 = (bf16[16,64,1664]{2,1,0:T(8,128)(2,1)S(1)}, bf16[16,64,1024]{2,1,0:T(8,128)(2,1)S(1)}, bf16[16,64,5120]{2,1,0:T(8,128)(2,1)}, bf16[16,160,1024]...) custom-call(bf16[64,1664]{1,0:T(8,128)(2,1)S(1)} %pad.44.refs_0_, ...), custom_call_target="tpu_custom_call" | custom-call | tf_op jit(solution)/shard_map/pallas_call | solution.py:255
  241.8 1.8 copy-done.10
  243.5 1.7 copy-done.12
  245.3 2.3 copy-done.9
  249.0 3.8 fusion.29
  253.8 2.0 multiply_reduce_fusion.9
  256.0 4.0 fusion.116.qkv
  260.1 8.6 shard_map.466
  272.3 9.4 %fusion.117 = f32[512,5120]{1,0:T(8,128)S(1)} fusion(bf16[1024,5120]{1,0:T(8,128)(2,1)} %bitcast.314, f32[512,1024]{1,0:T(8,128)S(1)} %get-tuple-element.626, f32[1024]{0:T(1024)S(1)} %bitcast.290, f32[512]{0:T(512)S(1)} %get-tuple-element.607), kind=kOutput, calls=%fused_computation.285 | convolution fusion | flops 5370281984 | bytes 23074816 | tf_op jit(solution)/shard_map/dot_general | solution.py:1156
  281.8 1.6 multiply_convert_fusion.2
  283.4 2.4 copy-done.27
  285.9 3.0 multiply_reduce_fusion.7
  288.9 2.1 fusion.118.qkv
  291.0 4.9 shard_map.467
  299.2 1.6 fusion.115
  305.1 39.4 %shard_map.468 = bf16[32,64,1024]{2,1,0:T(8,128)(2,1)} custom-call(bf16[64,1024]{1,0:T(8,128)(2,1)} %slice.231.refs_0_), custom_call_target="tpu_custom_call" | custom-call | tf_op jit(solution)/shard_map/pallas_call | solution.py:255
  344.5 2.2 copy-done.2
  346.7 21.8 %shard_map.469 = (f32[3072,2048]{1,0:T(8,128)}, f32[1,2048]{1,0:T(1,128)S(1)}, f32[1,2048]{1,0:T(1,128)S(1)}, f32[1,2048]{1,0:T(1,128)S(1)}) custom-call(s32[1,2048]{1,0:T(1,128)S(1)} %sub.204.wanted, bf16[2048,1024]{1,0:T(8,128)(2,1)S(1)} %bitcast.212, bf16[3072,1024]{1,0:T(8,128)(2,1)} %get-tuple-element.879), custom_call_target="tpu_custom_call" | custom-call | tf_op jit(solution)/shard_map/pallas_call | solution.py:715
  369.2 9.9 %shard_map.470 = f32[16,32,128]{2,1,0:T(8,128)} custom-call(f32[32,128]{1,0:T(8,128)} %reshape.648.src), custom_call_target="tpu_custom_call" | custom-call | tf_op jit(solution)/shard_map/pallas_call | solution.py:620
  382.5 23.3 %shard_map.471 = (bf16[3072,2048]{1,0:T(8,128)(2,1)}, bf16[2048,1024]{1,0:T(8,128)(2,1)}) custom-call(s32[1]{0:T(128)} %bitcast.36.section, s32[1,2048]{1,0:T(1,128)} %copy-done.8, f32[1,2048]{1,0:T(1,128)} %bitcast.285, f32[1,2048]{1,0:T(1,128)} %div.198.scale, f32[1,2048]{1,0:T(1,128)} %copy-done.67, f32[3072,2048]{1,0:T(8,128)} %get-tuple-element.476.logits, ...), custom_call_target="tpu_custom_call" | custom-call | tf_op jit(solution)/shard_map/pallas_call | solution.py:755
  405.8 2.2 copy-done.3
  408.0 36.3 %shard_map.472 = f32[64,1024]{1,0:T(8,128)S(1)} custom-call(bf16[2,4,2,2,64,1024]{5,4,3,2,1,0:T(8,128)(2,1)S(1)} %bitcast.213), custom_call_target="tpu_custom_call" | custom-call | tf_op jit(solution)/shard_map/pallas_call | solution.py:591
  445.7 4.8 multiply_convert_fusion.7
  450.6 3.7 multiply_reduce_fusion.10
  455.3 2.6 fusion.34.grad
  459.3 5.6 shard_map.473
  465.0 5.3 multiply_reduce_fusion.2
  470.3 3.7 subtract_add_fusion.1
  474.1 10.9 %multiply_convert_fusion.1 = (bf16[512,2560]{1,0:T(8,128)(2,1)S(1)}, bf16[512,2560]{1,0:T(8,128)(2,1)}) fusion(f32[512,5120]{1,0:T(8,128)} %copy-done.27, bf16[2560,1024]{1,0:T(8,128)(2,1)} %bitcast.216, f32[512,1024]{1,0:T(8,128)S(1)} %subtract_add_fusion.1), kind=kOutput, calls=%fused_computation.47 | convolution fusion | flops 2701918208 | bytes 23068672 | tf_op jit(solution)/shard_map/dot_general | solution.py:1166
  485.0 4.0 convolution_convert_fusion.6
  489.1 11.8 %multiply_reduce_fusion.3 = (bf16[1024]{0:T(1024)(128)(2,1)S(1)}, f32[512]{0:T(512)S(1)}, f32[512,1024]{1,0:T(8,128)}) fusion(f32[512,1024]{1,0:T(8,128)S(1)} %copy-done.53, f32[512]{0:T(512)S(1)} %get-tuple-element.607, f32[1024]{0:T(1024)S(1)} %bitcast.291, bf16[1024,5120]{1,0:T(8,128)(2,1)} %bitcast.315, bf16[512,2560]{1,0:T(8,128)(2,1)} %get-tuple-element.589, ...), kind=kOutput, calls=%fused_computation.64 | convolution fusion | flops 5382339072 | bytes 19933184 | tf_op jit(solution)/shard_map/dot_general | solution.py:1166
  501.0 4.0 subtract_add_fusion
  505.0 4.6 fusion.31.grad
  509.7 10.3 %shard_map.474 = bf16[1664,512]{1,0:T(8,128)(2,1)S(1)} custom-call(bf16[1600,512]{1,0:T(8,128)(2,1)S(1)} %copy-done.5, f32[5,3,512]{2,1,0:T(4,128)S(1)} %get-tuple-element.471.top, f32[5,3,512]{2,1,0:T(4,128)S(1)} %get-tuple-element.472.share, bf16[960,512]{1,0:T(8,128)(2,1)S(1)} %fusion.31.grad, f32[32,512]{1,0:T(8,128)S(1)} %get-tuple-element.603.cosine, ...), custom_call_target="tpu_custom_call" | custom-call | tf_op jit(solution)/shard_map/pallas_call | solution.py:1141
  520.0 4.1 multiply_reduce_fusion.1
  525.6 2.6 convolution_convert_fusion.8
  528.2 4.1 convolution_convert_fusion.7
  534.0 6.4 convolution_convert_fusion.5
  540.4 2.1 convolution_convert_fusion.9
  542.5 2.3 convolution_convert_fusion.10
  546.3 8.9 convolution_convert_fusion.3
  555.2 3.9 convolution_convert_fusion.4
  559.1 5.8 convolution_convert_fusion.2
  564.9 244.8 %shard_map.475 = (f32[64,1664]{1,0:T(8,128)}, f32[64,1024]{1,0:T(8,128)}, f32[64,5120]{1,0:T(8,128)}, f32[160,1024]{1,0:T(8,128)}, f32[32,128]{1,0:T(8,128)}, /*...) custom-call(bf16[4,2,2,64,1664]{4,3,2,1,0:T(8,128)(2,1)} %bitcast.25, ...), custom_call_target="tpu_custom_call" | custom-call | tf_op jit(solution)/shard_map/pallas_call | solution.py:591
  814.4 35.1 %shard_map.476 = (f32[960,3072]{1,0:T(8,128)}, f32[60,1,1600]{2,1,0:T(1,128)}, f32[60,1,960]{2,1,0:T(1,128)}, f32[60,1,5120]{2,1,0:T(1,128)}, f32[160,960]{1,0:T...) custom-call(f32[1]{0:T(128)} %bitcast.53.clip, ...), custom_call_target="tpu_custom_call" | custom-call | tf_op jit(solution)/shard_map/pallas_call | solution.py:915
  849.5 11.7 %shard_map.477 = f32[32,16,128]{2,1,0:T(8,128)} custom-call(f32[16,128]{1,0:T(8,128)} %get-tuple-element.489.src), custom_call_target="tpu_custom_call" | custom-call | tf_op jit(solution)/shard_map/pallas_call | solution.py:620
  867.9 16.2 %shard_map.478 = (f32[960,3072]{1,0:T(8,128)}, f32[60,1,1600]{2,1,0:T(1,128)}, f32[60,1,960]{2,1,0:T(1,128)}, f32[60,1,5120]{2,1,0:T(1,128)}, f32[160,960]{1,0:T...) custom-call(f32[5]{0:T(128)} %pad_maximum_fusion.9.scales, ...), custom_call_target="tpu_custom_call" | custom-call | tf_op jit(solution)/shard_map/pallas_call | solution.py:962
  (297 shorter events, 52.9 us)
Async XLA Ops:
  7.2 27.1 %copy-start.57 = (f32[1,60,960]{2,0,1:T(1,128)S(1)}, f32[1,60,960]{2,0,1:T(1,128)}, u32[]{:S(2)}) copy-start(f32[1,60,960]{2,0,1:T(1,128)} %param.37) | copy-start | bytes 691204
  14.1 234.9 %copy-start.68 = (s32[512]{0:T(512)}, s32[512]{0:T(512)S(1)}, u32[]{:S(2)}) copy-start(s32[512]{0:T(512)S(1)} %get-tuple-element.612) | copy-start | bytes 6148
  31.9 312.6 %copy-start.8 = (s32[1,2048]{1,0:T(1,128)}, s32[1,2048]{1,0:T(1,128)S(1)}, u32[]{:S(2)}) copy-start(s32[1,2048]{1,0:T(1,128)S(1)} %sub.204.wanted) | copy-start | bytes 24580
  38.6 203.2 %copy-start.30 = (bf16[1024,1024]{1,0:T(8,128)(2,1)}, bf16[1024,1024]{1,0:T(8,128)(2,1)S(1)}, u32[]{:S(2)}) copy-start(bf16[1024,1024]{1,0:T(8,128)(2,1)S(1)} %pad.48.refs_6_) | copy-start | bytes 6291460
  253.8 6.3 copy-start.60
  253.8 6.3 copy-start.62
  253.8 6.3 copy-start.64
  270.9 14.9 %slice-start = ((s8[5242880]{0:T(1024)(128)(4,1)}), s8[4194304]{0:T(1024)(128)(4,1)S(1)}, s32[]{:S(2)}) async-start(s8[5242880]{0:T(1024)(128)(4,1)} %bitcast.217), calls=%async_computation.3 | async-start | bytes 8388608
  272.3 11.1 %copy-start.52 = (f32[512,1024]{1,0:T(8,128)}, f32[512,1024]{1,0:T(8,128)S(1)}, u32[]{:S(2)}) copy-start(f32[512,1024]{1,0:T(8,128)S(1)} %get-tuple-element.626) | copy-start | bytes 6291460
  272.3 13.5 %slice-start.1 = ((s8[5242880]{0:T(1024)(128)(4,1)}), s8[1048576]{0:T(1024)(128)(4,1)S(1)}, s32[]{:S(2)}) async-start(s8[5242880]{0:T(1024)(128)(4,1)} %bitcast.217), calls=%async_computation.4 | async-start | bytes 2097152
  281.7 4.1 copy-start.27
  288.8 9.2 %copy-start.31 = (f32[512,1024]{1,0:T(8,128)}, f32[512,1024]{1,0:T(8,128)S(1)}, u32[]{:S(2)}) copy-start(f32[512,1024]{1,0:T(8,128)S(1)} %get-tuple-element.628) | copy-start | bytes 6291460
  288.9 10.3 %slice-start.2 = ((s8[10485760]{0:T(1024)(128)(4,1)}), s8[4194304]{0:T(1024)(128)(4,1)S(1)}, s32[]{:S(2)}) async-start(s8[10485760]{0:T(1024)(128)(4,1)} %bitcast.230), calls=%async_computation.5 | async-start | bytes 8388608
  288.9 10.3 %slice-start.3 = ((s8[10485760]{0:T(1024)(128)(4,1)}), s8[4194304]{0:T(1024)(128)(4,1)S(1)}, s32[]{:S(2)}) async-start(s8[10485760]{0:T(1024)(128)(4,1)} %bitcast.230), calls=%async_computation.6 | async-start | bytes 8388608
  291.0 8.1 slice-start.4
  382.5 61.9 %copy-start.40 = (f32[128,1024]{1,0:T(8,128)S(1)}, f32[128,1024]{1,0:T(8,128)}, u32[]{:S(2)}) copy-start(f32[128,1024]{1,0:T(8,128)} %copy-done.39) | copy-start | bytes 1572868
  408.0 36.4 %copy-start.20 = (bf16[960,1024]{1,0:T(8,128)(2,1)S(1)}, bf16[960,1024]{1,0:T(8,128)(2,1)}, u32[]{:S(2)}) copy-start(bf16[960,1024]{1,0:T(8,128)(2,1)} %copy-done.18) | copy-start | bytes 5898244
  408.0 37.7 %copy-start.26 = (f32[128,5120]{1,0:T(8,128)S(1)}, f32[128,5120]{1,0:T(8,128)}, u32[]{:S(2)}) copy-start(f32[128,5120]{1,0:T(8,128)} %copy-done.25) | copy-start | bytes 7864324
  408.0 42.5 %slice-start.5 = ((s8[10485760]{0:T(1024)(128)(4,1)}), s8[4194304]{0:T(1024)(128)(4,1)S(1)}, s32[]{:S(2)}) async-start(s8[10485760]{0:T(1024)(128)(4,1)} %bitcast.233), calls=%async_computation.8 | async-start | bytes 8388608
  444.3 6.2 slice-start.6
  445.7 8.6 copy-start.42
  445.7 4.9 slice-start.7
  445.7 4.9 copy-start.23
  459.3 5.6 copy-start.14
  464.9 5.4 copy-start.44
  474.1 10.9 %copy-start.33 = (f32[512,1024]{1,0:T(8,128)}, f32[512,1024]{1,0:T(8,128)S(1)}, u32[]{:S(2)}) copy-start(f32[512,1024]{1,0:T(8,128)S(1)} %subtract_add_fusion.1) | copy-start | bytes 6291460
  474.1 10.9 %copy-start.32 = (f32[512,1024]{1,0:T(8,128)S(1)}, f32[512,1024]{1,0:T(8,128)}, u32[]{:S(2)}) copy-start(f32[512,1024]{1,0:T(8,128)} %copy-done.31) | copy-start | bytes 6291460
  485.0 4.1 copy-start.73
  485.0 4.1 copy-start.53
  489.1 11.9 %copy-start.34 = (f32[512,1024]{1,0:T(8,128)S(1)}, f32[512,1024]{1,0:T(8,128)}, u32[]{:S(2)}) copy-start(f32[512,1024]{1,0:T(8,128)} %copy-done.33) | copy-start | bytes 6291460
  505.0 4.7 copy-start.5
  509.7 10.3 %copy-start.11 = (bf16[16,64,1664]{2,1,0:T(8,128)(2,1)S(1)}, bf16[16,64,1664]{2,1,0:T(8,128)(2,1)}, u32[]{:S(2)}) copy-start(bf16[16,64,1664]{2,1,0:T(8,128)(2,1)} %copy-done.10) | copy-start | bytes 10223620
  520.0 4.1 copy-start.21
  520.0 4.1 copy-start.37
  520.0 4.1 copy-start.38
  528.2 5.7 copy-start.35
  534.0 6.5 copy-start.45
  534.0 6.5 copy-start.56
  546.3 8.9 copy-start.29
  546.3 8.9 copy-start.43
  564.9 244.8 %copy-start.59 = (s32[1,512]{1,0:T(1,128)S(1)}, s32[1,512]{1,0:T(1,128)}, u32[]{:S(2)}) copy-start(s32[1,512]{1,0:T(1,128)} %param.31) | copy-start | bytes 6148
  564.9 244.8 %copy-start.61 = (s32[512]{0:T(512)S(1)}, s32[512]{0:T(512)}, u32[]{:S(2)}) copy-start(s32[512]{0:T(512)} %copy-done.60) | copy-start | bytes 6148
  564.9 244.8 %copy-start.63 = (s32[512]{0:T(512)S(1)}, s32[512]{0:T(512)}, u32[]{:S(2)}) copy-start(s32[512]{0:T(512)} %copy-done.62) | copy-start | bytes 6148
  564.9 244.8 %copy-start.65 = (s32[512,1]{0,1:T(1,128)S(1)}, s32[512,1]{0,1:T(1,128)}, u32[]{:S(2)}) copy-start(s32[512,1]{0,1:T(1,128)} %copy-done.64) | copy-start | bytes 6148
  814.4 48.5 %copy-start.70 = (f32[1,2,60]{2,1,0:T(2,128)S(1)}, f32[1,2,60]{2,1,0:T(2,128)}, u32[]{:S(2)}) copy-start(f32[1,2,60]{2,1,0:T(2,128)} %param.40) | copy-start | bytes 1444
  814.4 51.1 %copy-start.71 = (f32[60]{0:T(128)S(1)}, f32[60]{0:T(128)}, u32[]{:S(2)}) copy-start(f32[60]{0:T(128)} %param.41) | copy-start | bytes 724
  862.8 21.4 %copy-start.72 = (f32[2,14]{1,0:T(2,128)}, f32[2,14]{1,0:T(2,128)S(1)}, u32[]{:S(2)}) copy-start(f32[2,14]{1,0:T(2,128)S(1)} %maximum_sqrt_fusion) | copy-start | bytes 340
  867.9 16.2 %copy-start.1 = (s32[1,32,32]{2,1,0:T(8,128)S(1)}, s32[1,32,32]{2,1,0:T(8,128)}, u32[]{:S(2)}) copy-start(s32[1,32,32]{2,1,0:T(8,128)} %param.33) | copy-start | bytes 12292
  (40 other events, 95.0 us)

commit v7 on v6

--- a/solution.py
+++ b/solution.py
@@ -532,11 +532,11 @@
     plan = [[] for unused in range(steps)]
     plan[0].append(start)
     plan[3].append(turn_rows)
-    plan[9].append(pass_on)
-    plan[13].append(load_got)
-    plan[14].append(turn_got)
+    plan[6].append(pass_on)
+    plan[10].append(load_got)
+    plan[11].append(turn_got)
     for i in range(turns):
-        plan[15 + i * (steps - 16) // turns].append(functools.partial(table_tile, i))
+        plan[12 + i * (steps - 16) // turns].append(functools.partial(table_tile, i))
     return plan + [end]
 
 
@@ -1425,7 +1425,7 @@
         section_index, wanted_here, top, grad_row / total, grad_row, logits, table_low, sections
     )
     if fast:
-        grad_head = reduce_all([grad_rows], 4, 1, tile=16)[0]
+        grad_head = reduce_all([grad_rows], 4, 2, tile=16)[0]
     else:
         grad_head = lax.psum_scatter(grad_rows, BOTH, scatter_dimension=0, tiled=True)
     grad_head = jnp.pad(grad_head.astype(jnp.float32), ((0, place.shape[0] - taken), (0, 0)))

time: 902 us -> 900 us (level)
  no operation moved by 1% of the time
where the time goes in v7:
time: 900 us; the launch traced here: 890 us
  Pallas kernels  681 us (76%)
  matrix products  127 us (14%)
  local copies, waits for them, and re-layouts  35.9 us (4%)
  other arithmetic  24.1 us (3%)
  between operations  20.2 us (2%)
    pallas_call x2, Pallas kernels, reduce_all(): pl.pallas_call(functools.partial(reduce_kernel, pieces, tile, count, len(...  279 us
    pallas_call x2, Pallas kernels, gather_all(): pl.pallas_call(functools.partial(gather_kernel, pieces, len(blocks), len(...  243 us
    dot_general x8, matrix products, dense_nt(): lax.dot_general(left, right, (((1,), (1,)), ((), ())), preferred_element_...  40.6 us
    pallas_call x1, Pallas kernels, moments(): pl.pallas_call(functools.partial(moments_kernel, decays), grid=(width //...  35.3 us
    dot_general x9, matrix products, dense_t(): lax.dot_general(left, right, (((0,), (0,)), ((), ())), preferred_element_...  34.4 us
    pallas_call x3, Pallas kernels, exchange(): pl.pallas_call(functools.partial(exchange_kernel, whole), out_shape=jax.S...  33.8 us
    dot_general x6, matrix products, dense_tt(): lax.dot_general(left, right, (((0,), (1,)), ((), ())), preferred_element_...  23.7 us
    unnamed x181, local copies, waits for them, and re-layouts  23.5 us

profile of v7, /device:TPU:0, one launch (start us, length us, event | category | flops | bytes accessed | tf_op | source)
XLA Modules:
  0.0 890.1 jit_solution(5005663834155185743)
XLA Ops:
  17.9 12.2 %shard_map.464 = s32[32,8,128]{2,1,0:T(8,128)} custom-call(s32[8,128]{1,0:T(8,128)} %fusion.100.src), custom_call_target="tpu_custom_call" | custom-call | tf_op jit(solution)/shard_map/pallas_call | solution.py:620
  38.6 203.2 %shard_map.465 = (bf16[16,64,1664]{2,1,0:T(8,128)(2,1)S(1)}, bf16[16,64,1024]{2,1,0:T(8,128)(2,1)S(1)}, bf16[16,64,5120]{2,1,0:T(8,128)(2,1)}, bf16[16,160,1024]...) custom-call(bf16[64,1664]{1,0:T(8,128)(2,1)S(1)} %pad.44.refs_0_, ...), custom_call_target="tpu_custom_call" | custom-call | tf_op jit(solution)/shard_map/pallas_call | solution.py:255
  241.8 1.8 copy-done.10
  243.5 1.7 copy-done.12
  245.3 2.3 copy-done.9
  249.0 3.8 fusion.29
  253.8 2.0 multiply_reduce_fusion.9
  256.0 4.0 fusion.116.qkv
  260.1 8.6 shard_map.466
  272.3 9.4 %fusion.117 = f32[512,5120]{1,0:T(8,128)S(1)} fusion(bf16[1024,5120]{1,0:T(8,128)(2,1)} %bitcast.314, f32[512,1024]{1,0:T(8,128)S(1)} %get-tuple-element.626, f32[1024]{0:T(1024)S(1)} %bitcast.290, f32[512]{0:T(512)S(1)} %get-tuple-element.607), kind=kOutput, calls=%fused_computation.285 | convolution fusion | flops 5370281984 | bytes 23074816 | tf_op jit(solution)/shard_map/dot_general | solution.py:1156
  281.8 1.6 multiply_convert_fusion.2
  283.4 2.4 copy-done.27
  285.9 3.0 multiply_reduce_fusion.7
  288.9 2.1 fusion.118.qkv
  291.0 4.9 shard_map.467
  299.2 1.6 fusion.115
  305.1 39.4 %shard_map.468 = bf16[32,64,1024]{2,1,0:T(8,128)(2,1)} custom-call(bf16[64,1024]{1,0:T(8,128)(2,1)} %slice.231.refs_0_), custom_call_target="tpu_custom_call" | custom-call | tf_op jit(solution)/shard_map/pallas_call | solution.py:255
  344.5 2.2 copy-done.2
  346.7 21.8 %shard_map.469 = (f32[3072,2048]{1,0:T(8,128)}, f32[1,2048]{1,0:T(1,128)S(1)}, f32[1,2048]{1,0:T(1,128)S(1)}, f32[1,2048]{1,0:T(1,128)S(1)}) custom-call(s32[1,2048]{1,0:T(1,128)S(1)} %sub.204.wanted, bf16[2048,1024]{1,0:T(8,128)(2,1)S(1)} %bitcast.212, bf16[3072,1024]{1,0:T(8,128)(2,1)} %get-tuple-element.879), custom_call_target="tpu_custom_call" | custom-call | tf_op jit(solution)/shard_map/pallas_call | solution.py:715
  369.2 9.9 %shard_map.470 = f32[16,32,128]{2,1,0:T(8,128)} custom-call(f32[32,128]{1,0:T(8,128)} %reshape.648.src), custom_call_target="tpu_custom_call" | custom-call | tf_op jit(solution)/shard_map/pallas_call | solution.py:620
  382.5 23.3 %shard_map.471 = (bf16[3072,2048]{1,0:T(8,128)(2,1)}, bf16[2048,1024]{1,0:T(8,128)(2,1)}) custom-call(s32[1]{0:T(128)} %bitcast.36.section, s32[1,2048]{1,0:T(1,128)} %copy-done.8, f32[1,2048]{1,0:T(1,128)} %bitcast.285, f32[1,2048]{1,0:T(1,128)} %div.198.scale, f32[1,2048]{1,0:T(1,128)} %copy-done.67, f32[3072,2048]{1,0:T(8,128)} %get-tuple-element.476.logits, ...), custom_call_target="tpu_custom_call" | custom-call | tf_op jit(solution)/shard_map/pallas_call | solution.py:755
  405.8 2.2 copy-done.3
  408.0 35.7 %shard_map.472 = f32[64,1024]{1,0:T(8,128)S(1)} custom-call(bf16[2,4,2,2,64,1024]{5,4,3,2,1,0:T(8,128)(2,1)S(1)} %bitcast.213), custom_call_target="tpu_custom_call" | custom-call | tf_op jit(solution)/shard_map/pallas_call | solution.py:591
  445.0 4.8 multiply_convert_fusion.7
  449.9 3.7 multiply_reduce_fusion.10
  454.6 2.6 fusion.34.grad
  458.6 5.6 shard_map.473
  464.3 5.3 multiply_reduce_fusion.2
  469.7 3.7 subtract_add_fusion.1
  473.4 10.9 %multiply_convert_fusion.1 = (bf16[512,2560]{1,0:T(8,128)(2,1)S(1)}, bf16[512,2560]{1,0:T(8,128)(2,1)}) fusion(f32[512,5120]{1,0:T(8,128)} %copy-done.27, bf16[2560,1024]{1,0:T(8,128)(2,1)} %bitcast.216, f32[512,1024]{1,0:T(8,128)S(1)} %subtract_add_fusion.1), kind=kOutput, calls=%fused_computation.47 | convolution fusion | flops 2701918208 | bytes 23068672 | tf_op jit(solution)/shard_map/dot_general | solution.py:1166
  484.3 4.0 convolution_convert_fusion.6
  488.4 11.8 %multiply_reduce_fusion.3 = (bf16[1024]{0:T(1024)(128)(2,1)S(1)}, f32[512]{0:T(512)S(1)}, f32[512,1024]{1,0:T(8,128)}) fusion(f32[512,1024]{1,0:T(8,128)S(1)} %copy-done.53, f32[512]{0:T(512)S(1)} %get-tuple-element.607, f32[1024]{0:T(1024)S(1)} %bitcast.291, bf16[1024,5120]{1,0:T(8,128)(2,1)} %bitcast.315, bf16[512,2560]{1,0:T(8,128)(2,1)} %get-tuple-element.589, ...), kind=kOutput, calls=%fused_computation.64 | convolution fusion | flops 5382339072 | bytes 19933184 | tf_op jit(solution)/shard_map/dot_general | solution.py:1166
  500.3 4.0 subtract_add_fusion
  504.3 4.6 fusion.31.grad
  509.0 10.3 %shard_map.474 = bf16[1664,512]{1,0:T(8,128)(2,1)S(1)} custom-call(bf16[1600,512]{1,0:T(8,128)(2,1)S(1)} %copy-done.5, f32[5,3,512]{2,1,0:T(4,128)S(1)} %get-tuple-element.471.top, f32[5,3,512]{2,1,0:T(4,128)S(1)} %get-tuple-element.472.share, bf16[960,512]{1,0:T(8,128)(2,1)S(1)} %fusion.31.grad, f32[32,512]{1,0:T(8,128)S(1)} %get-tuple-element.603.cosine, ...), custom_call_target="tpu_custom_call" | custom-call | tf_op jit(solution)/shard_map/pallas_call | solution.py:1141
  519.4 4.1 multiply_reduce_fusion.1
  524.9 2.6 convolution_convert_fusion.8
  527.6 4.1 convolution_convert_fusion.7
  533.3 6.4 convolution_convert_fusion.5
  539.8 2.1 convolution_convert_fusion.9
  541.9 2.3 convolution_convert_fusion.10
  545.6 8.9 convolution_convert_fusion.3
  554.5 3.9 convolution_convert_fusion.4
  558.4 5.8 convolution_convert_fusion.2
  564.2 243.2 %shard_map.475 = (f32[64,1664]{1,0:T(8,128)}, f32[64,1024]{1,0:T(8,128)}, f32[64,5120]{1,0:T(8,128)}, f32[160,1024]{1,0:T(8,128)}, f32[32,128]{1,0:T(8,128)}, /*...) custom-call(bf16[4,2,2,64,1664]{4,3,2,1,0:T(8,128)(2,1)} %bitcast.25, ...), custom_call_target="tpu_custom_call" | custom-call | tf_op jit(solution)/shard_map/pallas_call | solution.py:591
  811.9 35.3 %shard_map.476 = (f32[960,3072]{1,0:T(8,128)}, f32[60,1,1600]{2,1,0:T(1,128)}, f32[60,1,960]{2,1,0:T(1,128)}, f32[60,1,5120]{2,1,0:T(1,128)}, f32[160,960]{1,0:T...) custom-call(f32[1]{0:T(128)} %bitcast.53.clip, ...), custom_call_target="tpu_custom_call" | custom-call | tf_op jit(solution)/shard_map/pallas_call | solution.py:915
  847.2 11.7 %shard_map.477 = f32[32,16,128]{2,1,0:T(8,128)} custom-call(f32[16,128]{1,0:T(8,128)} %get-tuple-element.489.src), custom_call_target="tpu_custom_call" | custom-call | tf_op jit(solution)/shard_map/pallas_call | solution.py:620
  865.6 16.2 %shard_map.478 = (f32[960,3072]{1,0:T(8,128)}, f32[60,1,1600]{2,1,0:T(1,128)}, f32[60,1,960]{2,1,0:T(1,128)}, f32[60,1,5120]{2,1,0:T(1,128)}, f32[160,960]{1,0:T...) custom-call(f32[5]{0:T(128)} %pad_maximum_fusion.9.scales, ...), custom_call_target="tpu_custom_call" | custom-call | tf_op jit(solution)/shard_map/pallas_call | solution.py:962
  (297 shorter events, 52.7 us)
Async XLA Ops:
  7.2 27.1 %copy-start.57 = (f32[1,60,960]{2,0,1:T(1,128)S(1)}, f32[1,60,960]{2,0,1:T(1,128)}, u32[]{:S(2)}) copy-start(f32[1,60,960]{2,0,1:T(1,128)} %param.37) | copy-start | bytes 691204
  14.1 234.9 %copy-start.68 = (s32[512]{0:T(512)}, s32[512]{0:T(512)S(1)}, u32[]{:S(2)}) copy-start(s32[512]{0:T(512)S(1)} %get-tuple-element.612) | copy-start | bytes 6148
  31.9 312.6 %copy-start.8 = (s32[1,2048]{1,0:T(1,128)}, s32[1,2048]{1,0:T(1,128)S(1)}, u32[]{:S(2)}) copy-start(s32[1,2048]{1,0:T(1,128)S(1)} %sub.204.wanted) | copy-start | bytes 24580
  38.6 203.2 %copy-start.30 = (bf16[1024,1024]{1,0:T(8,128)(2,1)}, bf16[1024,1024]{1,0:T(8,128)(2,1)S(1)}, u32[]{:S(2)}) copy-start(bf16[1024,1024]{1,0:T(8,128)(2,1)S(1)} %pad.48.refs_6_) | copy-start | bytes 6291460
  253.8 6.3 copy-start.60
  253.8 6.3 copy-start.62
  253.8 6.3 copy-start.64
  270.9 14.9 %slice-start = ((s8[5242880]{0:T(1024)(128)(4,1)}), s8[4194304]{0:T(1024)(128)(4,1)S(1)}, s32[]{:S(2)}) async-start(s8[5242880]{0:T(1024)(128)(4,1)} %bitcast.217), calls=%async_computation.3 | async-start | bytes 8388608
  272.3 11.1 %copy-start.52 = (f32[512,1024]{1,0:T(8,128)}, f32[512,1024]{1,0:T(8,128)S(1)}, u32[]{:S(2)}) copy-start(f32[512,1024]{1,0:T(8,128)S(1)} %get-tuple-element.626) | copy-start | bytes 6291460
  272.3 13.5 %slice-start.1 = ((s8[5242880]{0:T(1024)(128)(4,1)}), s8[1048576]{0:T(1024)(128)(4,1)S(1)}, s32[]{:S(2)}) async-start(s8[5242880]{0:T(1024)(128)(4,1)} %bitcast.217), calls=%async_computation.4 | async-start | bytes 2097152
  281.7 4.1 copy-start.27
  288.8 9.2 %copy-start.31 = (f32[512,1024]{1,0:T(8,128)}, f32[512,1024]{1,0:T(8,128)S(1)}, u32[]{:S(2)}) copy-start(f32[512,1024]{1,0:T(8,128)S(1)} %get-tuple-element.628) | copy-start | bytes 6291460
  288.9 10.3 %slice-start.2 = ((s8[10485760]{0:T(1024)(128)(4,1)}), s8[4194304]{0:T(1024)(128)(4,1)S(1)}, s32[]{:S(2)}) async-start(s8[10485760]{0:T(1024)(128)(4,1)} %bitcast.230), calls=%async_computation.5 | async-start | bytes 8388608
  288.9 10.3 %slice-start.3 = ((s8[10485760]{0:T(1024)(128)(4,1)}), s8[4194304]{0:T(1024)(128)(4,1)S(1)}, s32[]{:S(2)}) async-start(s8[10485760]{0:T(1024)(128)(4,1)} %bitcast.230), calls=%async_computation.6 | async-start | bytes 8388608
  291.0 8.1 slice-start.4
  382.5 61.2 %copy-start.40 = (f32[128,1024]{1,0:T(8,128)S(1)}, f32[128,1024]{1,0:T(8,128)}, u32[]{:S(2)}) copy-start(f32[128,1024]{1,0:T(8,128)} %copy-done.39) | copy-start | bytes 1572868
  408.0 35.7 %copy-start.20 = (bf16[960,1024]{1,0:T(8,128)(2,1)S(1)}, bf16[960,1024]{1,0:T(8,128)(2,1)}, u32[]{:S(2)}) copy-start(bf16[960,1024]{1,0:T(8,128)(2,1)} %copy-done.18) | copy-start | bytes 5898244
  408.0 37.0 %copy-start.26 = (f32[128,5120]{1,0:T(8,128)S(1)}, f32[128,5120]{1,0:T(8,128)}, u32[]{:S(2)}) copy-start(f32[128,5120]{1,0:T(8,128)} %copy-done.25) | copy-start | bytes 7864324
  408.0 41.9 %slice-start.5 = ((s8[10485760]{0:T(1024)(128)(4,1)}), s8[4194304]{0:T(1024)(128)(4,1)S(1)}, s32[]{:S(2)}) async-start(s8[10485760]{0:T(1024)(128)(4,1)} %bitcast.233), calls=%async_computation.8 | async-start | bytes 8388608
  443.7 6.2 slice-start.6
  445.0 8.6 copy-start.42
  445.0 4.9 slice-start.7
  445.0 4.9 copy-start.23
  458.6 5.6 copy-start.14
  464.3 5.4 copy-start.44
  473.4 10.9 %copy-start.33 = (f32[512,1024]{1,0:T(8,128)}, f32[512,1024]{1,0:T(8,128)S(1)}, u32[]{:S(2)}) copy-start(f32[512,1024]{1,0:T(8,128)S(1)} %subtract_add_fusion.1) | copy-start | bytes 6291460
  473.4 10.9 %copy-start.32 = (f32[512,1024]{1,0:T(8,128)S(1)}, f32[512,1024]{1,0:T(8,128)}, u32[]{:S(2)}) copy-start(f32[512,1024]{1,0:T(8,128)} %copy-done.31) | copy-start | bytes 6291460
  484.3 4.1 copy-start.73
  484.3 4.1 copy-start.53
  488.4 11.9 %copy-start.34 = (f32[512,1024]{1,0:T(8,128)S(1)}, f32[512,1024]{1,0:T(8,128)}, u32[]{:S(2)}) copy-start(f32[512,1024]{1,0:T(8,128)} %copy-done.33) | copy-start | bytes 6291460
  504.3 4.7 copy-start.5
  509.0 10.3 %copy-start.11 = (bf16[16,64,1664]{2,1,0:T(8,128)(2,1)S(1)}, bf16[16,64,1664]{2,1,0:T(8,128)(2,1)}, u32[]{:S(2)}) copy-start(bf16[16,64,1664]{2,1,0:T(8,128)(2,1)} %copy-done.10) | copy-start | bytes 10223620
  519.3 4.1 copy-start.21
  519.4 4.1 copy-start.37
  519.4 4.1 copy-start.38
  527.6 5.7 copy-start.35
  533.3 6.5 copy-start.45
  533.3 6.5 copy-start.56
  545.6 8.9 copy-start.29
  545.6 8.9 copy-start.43
  564.2 243.2 %copy-start.59 = (s32[1,512]{1,0:T(1,128)S(1)}, s32[1,512]{1,0:T(1,128)}, u32[]{:S(2)}) copy-start(s32[1,512]{1,0:T(1,128)} %param.31) | copy-start | bytes 6148
  564.2 243.2 %copy-start.61 = (s32[512]{0:T(512)S(1)}, s32[512]{0:T(512)}, u32[]{:S(2)}) copy-start(s32[512]{0:T(512)} %copy-done.60) | copy-start | bytes 6148
  564.2 243.2 %copy-start.63 = (s32[512]{0:T(512)S(1)}, s32[512]{0:T(512)}, u32[]{:S(2)}) copy-start(s32[512]{0:T(512)} %copy-done.62) | copy-start | bytes 6148
  564.2 243.2 %copy-start.65 = (s32[512,1]{0,1:T(1,128)S(1)}, s32[512,1]{0,1:T(1,128)}, u32[]{:S(2)}) copy-start(s32[512,1]{0,1:T(1,128)} %copy-done.64) | copy-start | bytes 6148
  811.9 48.8 %copy-start.70 = (f32[1,2,60]{2,1,0:T(2,128)S(1)}, f32[1,2,60]{2,1,0:T(2,128)}, u32[]{:S(2)}) copy-start(f32[1,2,60]{2,1,0:T(2,128)} %param.40) | copy-start | bytes 1444
  811.9 51.3 %copy-start.71 = (f32[60]{0:T(128)S(1)}, f32[60]{0:T(128)}, u32[]{:S(2)}) copy-start(f32[60]{0:T(128)} %param.41) | copy-start | bytes 724
  860.5 21.4 %copy-start.72 = (f32[2,14]{1,0:T(2,128)}, f32[2,14]{1,0:T(2,128)S(1)}, u32[]{:S(2)}) copy-start(f32[2,14]{1,0:T(2,128)S(1)} %maximum_sqrt_fusion) | copy-start | bytes 340
  865.6 16.2 %copy-start.1 = (s32[1,32,32]{2,1,0:T(8,128)S(1)}, s32[1,32,32]{2,1,0:T(8,128)}, u32[]{:S(2)}) copy-start(s32[1,32,32]{2,1,0:T(8,128)} %param.33) | copy-start | bytes 12292
  (40 other events, 95.0 us)
